TPU v7x, 32 devices: a whole 2x2x4 slice. The times are simulated.
32 devices in a mesh: dp: 4 (over y, x), key: 8 (over z, core).
Axes of the slice: x: 2, y: 2, z: 4, core: 2. Of those that a mesh axis runs over, the one named last changes fastest.
Arguments:
- inputs: bfloat16 [32, 512, 1024], P(('dp', 'key')), may hold values from -6 to 6
- positions: int32 [32, 512], P(('dp', 'key')), may hold values from 0 to 2045, as said below
- memory_flag: int32 [32], P('dp'), may hold values from 0 to 1, as said below
- partner: int32 [32], P('dp'), may hold values from 0 to 7, as said below
- cache_keys: bfloat16 [32, 512, 1024], P('dp', 'key'), may hold values from -6 to 6
- cache_values: bfloat16 [32, 512, 1024], P('dp', 'key'), may hold values from -6 to 6
- query_proj: bfloat16 [1024, 1024], P('key'), may hold values from -0.1875 to 0.1875
- key_proj: bfloat16 [1024, 1024], P('key'), may hold values from -0.1875 to 0.1875
- value_proj: bfloat16 [1024, 1024], P('key'), may hold values from -0.1875 to 0.1875
- out_proj: bfloat16 [1024, 1024], P('key'), may hold values from -3 to 3
- gate_proj: bfloat16 [1024, 2816], P('key'), may hold values from -0.1875 to 0.1875
- up_proj: bfloat16 [1024, 2816], P('key'), may hold values from -0.1875 to 0.1875
- down_proj: bfloat16 [2816, 1024], P('key'), may hold values from -0.109375 to 0.109375
- attn_gain: bfloat16 [1024], P('key'), may hold values from 0.099609375 to 1.8984375
- ffn_gain: bfloat16 [1024], P('key'), may hold values from 0.099609375 to 1.8984375
- cotangent: bfloat16 [32, 512, 1024], P(('dp', 'key')), may hold values from -6 to 6
Outputs:
- outputs: bfloat16 [32, 512, 1024], P(('dp', 'key'))
- input_grad: float32 [32, 512, 1024], P(('dp', 'key'))
- grad_query: float32 [1024, 1024], P('key')
- grad_key: float32 [1024, 1024], P('key')
- grad_value: float32 [1024, 1024], P('key')
- grad_out: float32 [1024, 1024], P('key')
- grad_gate: float32 [1024, 2816], P('key')
- grad_up: float32 [1024, 2816], P('key')
- grad_down: float32 [2816, 1024], P('key')
- grad_attn_gain: float32 [1024], P('key')
- grad_ffn_gain: float32 [1024], P('key')
- new_keys: bfloat16 [32, 512, 1024], P('dp', 'key')
- new_values: bfloat16 [32, 512, 1024], P('dp', 'key')
Inputs may be any that keep to these rules, and one draw needn't show every extreme that they name: `positions`: within a segment a token's position is one more than the token before it, except at exactly one document start (never the segment's first token) where it is 0. `memory_flag`: exactly half of each group of 8 consecutive segments has 1. Names another segment of the same group of 8 consecutive segments by its index within the group, never the segment itself; each segment of a group is the partner of exactly one segment.
All inputs are finite; a program needn't handle non-finite values.
Results may differ from a plain program's by a relative error of at most 0.017.
Values may be sent and summed in bfloat16 or wider, within the bound.
No kernel may reach another device: no remote copies, remote signals or barrier semaphores. Data moves between devices by JAX's collectives and lax.ppermute only.
A program may use at most 256 MiB of HBM per device.

v0:
```python
import math

import jax
import jax.numpy as jnp
from jax import lax
from jax.sharding import PartitionSpec as P

H = 8
HD = 128


EPSILON = 1e-05
ROPE_BASE = 10000.0
NEG_FILL = -1e30


def matmul(left, right):
    return jnp.dot(left, right, preferred_element_type=jnp.float32)


def contract_rows(left, right):
    return lax.dot_general(
        left, right, (((0,), (0,)), ((), ())), preferred_element_type=jnp.float32
    )


def times_transpose(left, right):
    return lax.dot_general(
        left, right, (((1,), (1,)), ((), ())), preferred_element_type=jnp.float32
    )


def rms_normed(values, gain_values):
    inverse_rms = lax.rsqrt(jnp.mean(values * values, axis=-1, keepdims=True) + EPSILON)
    return values * inverse_rms * gain_values


def rotary_tables(token_positions, head_width):
    half_width = head_width // 2
    frequency = ROPE_BASE ** (-2.0 * jnp.arange(half_width, dtype=jnp.float32) / head_width)
    angles = token_positions.astype(jnp.float32)[:, None] * frequency[None, :]
    return (jnp.cos(angles), jnp.sin(angles))


def rotate(values, cosine, sine_table):
    row_count = values.shape[0]
    split_heads = values.reshape(row_count, H, HD)
    half_width = HD // 2
    first_half = split_heads[:, :, :half_width]
    second = split_heads[:, :, half_width:]
    cos_rows = cosine[:, None, :]
    sin_rows = sine_table[:, None, :]
    turned = jnp.concatenate(
        [first_half * cos_rows - second * sin_rows, second * cos_rows + first_half * sin_rows],
        axis=-1,
    )
    return turned.reshape(row_count, H * HD)


def block_valid(token_pos, row_start, row_count, memory_valid):
    token_count = token_pos.shape[0]
    query_order = row_start + jnp.arange(row_count, dtype=jnp.int32)
    key_order = jnp.arange(token_count, dtype=jnp.int32)
    local_valid = (key_order[None, :] <= query_order[:, None]) & (
        token_pos[:, None] - token_pos[None, :] == query_order[:, None] - key_order[None, :]
    )
    memory_part = jnp.broadcast_to(memory_valid[None, :], (row_count, memory_valid.shape[0]))
    return jnp.concatenate([local_valid, memory_part], axis=-1)


def block_scores(
    query_loc_rows, query_mem_rows, key_heads, memory_key_heads, key_valid, scale_factor
):
    local_part = jnp.einsum(
        "qhd,khd->hqk", query_loc_rows, key_heads, preferred_element_type=jnp.float32
    )
    memory_part = jnp.einsum(
        "qhd,khd->hqk", query_mem_rows, memory_key_heads, preferred_element_type=jnp.float32
    )
    scores = jnp.concatenate([local_part, memory_part], axis=-1) * scale_factor
    return jnp.where(key_valid[None], scores, NEG_FILL)


def per_device(
    inputs,
    positions,
    memory_flag,
    partner,
    cache_keys,
    cache_values,
    query_proj,
    key_proj,
    value_proj,
    out_proj,
    gate_proj,
    up_proj,
    down_proj,
    attn_gain,
    ffn_gain,
    cotangent,
):
    gathered = (
        lax.all_gather(query_proj, "key", axis=0, tiled=True),
        lax.all_gather(key_proj, "key", axis=0, tiled=True),
        lax.all_gather(value_proj, "key", axis=0, tiled=True),
        lax.all_gather(out_proj, "key", axis=0, tiled=True),
        lax.all_gather(gate_proj, "key", axis=0, tiled=True),
        lax.all_gather(up_proj, "key", axis=0, tiled=True),
        lax.all_gather(down_proj, "key", axis=0, tiled=True),
        lax.all_gather(attn_gain, "key", axis=0, tiled=True),
        lax.all_gather(ffn_gain, "key", axis=0, tiled=True),
    )
    (
        query_full,
        key_full,
        value_full,
        out_full,
        gate_full,
        up_full,
        down_full,
        attn_scale,
        ffn_scale,
    ) = gathered
    tokens = inputs[0].astype(jnp.float32)
    token_pos = positions[0]
    token_count = tokens.shape[0]
    model_width = tokens.shape[1]
    seg_group = cache_keys.shape[0]
    slot_count = cache_keys.shape[1]
    self_flag = jnp.take(memory_flag, lax.axis_index("key"))
    partner_keys = jnp.take(cache_keys, partner, axis=0)
    partner_values = jnp.take(cache_values, partner, axis=0)
    outgoing = jnp.concatenate([cache_keys, partner_keys, cache_values, partner_values], axis=1)
    incoming = lax.all_to_all(outgoing, "key", split_axis=0, concat_axis=0, tiled=True)
    memory_keys = jnp.concatenate(
        [
            incoming[:, :slot_count].reshape(-1, model_width),
            incoming[:, slot_count : 2 * slot_count].reshape(-1, model_width),
        ],
        axis=0,
    )
    memory_values = jnp.concatenate(
        [
            incoming[:, 2 * slot_count : 3 * slot_count].reshape(-1, model_width),
            incoming[:, 3 * slot_count :].reshape(-1, model_width),
        ],
        axis=0,
    )
    memory_total = memory_keys.shape[0] // 2
    memory_valid = (jnp.arange(2 * memory_total, dtype=jnp.int32) >= memory_total) | (
        self_flag == 1
    )
    memory_key_heads = memory_keys.reshape(-1, H, HD)
    memory_value_heads = memory_values.reshape(-1, H, HD)
    attn_gain_full = attn_scale.astype(jnp.float32)
    normed_attn = rms_normed(tokens, attn_gain_full).astype(jnp.bfloat16)
    query_raw = matmul(normed_attn, query_full)
    key_raw = matmul(normed_attn, key_full)
    value_raw = matmul(normed_attn, value_full)
    cosine, sine_table = rotary_tables(token_pos, HD)
    query_mem = query_raw.astype(jnp.bfloat16)
    query_loc = rotate(query_raw, cosine, sine_table).astype(jnp.bfloat16)
    key_loc = rotate(key_raw, cosine, sine_table).astype(jnp.bfloat16)
    value_loc = value_raw.astype(jnp.bfloat16)
    fresh_keys = key_raw.astype(jnp.bfloat16)
    fresh_share = token_count // seg_group
    arrived_keys, arrived_values = (
        lax.all_to_all(
            fresh_keys.reshape(seg_group, fresh_share, model_width),
            "key",
            split_axis=0,
            concat_axis=0,
            tiled=True,
        ),
        lax.all_to_all(
            value_loc.reshape(seg_group, fresh_share, model_width),
            "key",
            split_axis=0,
            concat_axis=0,
            tiled=True,
        ),
    )
    new_keys = jnp.concatenate([cache_keys[:, fresh_share:], arrived_keys], axis=1)
    new_values = jnp.concatenate([cache_values[:, fresh_share:], arrived_values], axis=1)
    query_loc_heads = query_loc.reshape(token_count, H, HD)
    query_mem_heads = query_mem.reshape(token_count, H, HD)
    key_heads = key_loc.reshape(token_count, H, HD)
    value_heads = value_loc.reshape(token_count, H, HD)
    scale_factor = 1.0 / math.sqrt(HD)
    block_rows = min(token_count, 512)
    block_index = 0
    row_start = block_index * block_rows
    key_valid = block_valid(token_pos, row_start, block_rows, memory_valid)
    scores = block_scores(
        query_loc_heads, query_mem_heads, key_heads, memory_key_heads, key_valid, scale_factor
    )
    largest = jnp.max(scores, axis=-1, keepdims=True)
    shifted = jnp.exp(scores - largest)
    row_total = jnp.sum(shifted, axis=-1, keepdims=True)
    softmax_probs = shifted / row_total
    log_parts = (largest + jnp.log(row_total))[..., 0]
    probs_low = softmax_probs.astype(jnp.bfloat16)
    local_out = jnp.einsum(
        "hqk,khd->qhd",
        probs_low[..., :token_count],
        value_heads,
        preferred_element_type=jnp.float32,
    )
    memory_out = jnp.einsum(
        "hqk,khd->qhd",
        probs_low[..., token_count:],
        memory_value_heads,
        preferred_element_type=jnp.float32,
    )
    attended_parts = local_out + memory_out
    attended = attended_parts.reshape(token_count, model_width).astype(jnp.bfloat16)
    branch = matmul(attended, out_full)
    mixed_rows = tokens + branch
    ffn_gain_full = ffn_scale.astype(jnp.float32)
    normed_ff = rms_normed(mixed_rows, ffn_gain_full).astype(jnp.bfloat16)
    gate_raw = matmul(normed_ff, gate_full)
    up_raw = matmul(normed_ff, up_full)
    hidden = (jax.nn.silu(gate_raw) * up_raw).astype(jnp.bfloat16)
    outputs = (mixed_rows + matmul(hidden, down_full)).astype(jnp.bfloat16)
    (
        query_full,
        key_full,
        value_full,
        out_full,
        gate_full,
        up_full,
        down_full,
        attn_scale,
        ffn_scale,
    ) = gathered
    attn_gain_full = attn_scale.astype(jnp.float32)
    ffn_gain_full = ffn_scale.astype(jnp.float32)
    cotangent_rows = cotangent[0]
    cotangent_full = cotangent_rows.astype(jnp.float32)
    grad_down = contract_rows(hidden, cotangent_rows)
    hidden_grad = times_transpose(cotangent_rows, down_full)
    unused_product, pull_gate = jax.vjp(
        lambda gate_in, up_in: jax.nn.silu(gate_in) * up_in, gate_raw, up_raw
    )
    gate_grad, up_grad = pull_gate(hidden_grad)
    gate_grad_low = gate_grad.astype(jnp.bfloat16)
    up_grad_low = up_grad.astype(jnp.bfloat16)
    grad_gate = contract_rows(normed_ff, gate_grad_low)
    grad_up = contract_rows(normed_ff, up_grad_low)
    normed_ff_grad = times_transpose(gate_grad_low, gate_full) + times_transpose(
        up_grad_low, up_full
    )
    unused_normed, pull_ffn = jax.vjp(rms_normed, mixed_rows, ffn_gain_full)
    mixed_norm_grad, grad_ffn_gain = pull_ffn(normed_ff_grad)
    mixed_grad = cotangent_full + mixed_norm_grad
    branch_grad = mixed_grad.astype(jnp.bfloat16)
    grad_out = contract_rows(attended, branch_grad)
    attended_grad = times_transpose(branch_grad, out_full).astype(jnp.bfloat16)
    attended_heads_grad = attended_grad.reshape(token_count, H, HD)
    block_index = 0
    row_start = block_index * block_rows
    key_valid = block_valid(token_pos, row_start, block_rows, memory_valid)
    scores = block_scores(
        query_loc_heads, query_mem_heads, key_heads, memory_key_heads, key_valid, scale_factor
    )
    softmax_probs = jnp.exp(scores - log_parts[:, row_start : row_start + block_rows, None])
    prob_grad = jnp.concatenate(
        [
            jnp.einsum(
                "qhd,khd->hqk", attended_heads_grad, value_heads, preferred_element_type=jnp.float32
            ),
            jnp.einsum(
                "qhd,khd->hqk",
                attended_heads_grad,
                memory_value_heads,
                preferred_element_type=jnp.float32,
            ),
        ],
        axis=-1,
    )
    row_delta = jnp.sum(softmax_probs * prob_grad, axis=-1, keepdims=True)
    score_grad = (softmax_probs * (prob_grad - row_delta)).astype(jnp.bfloat16)
    local_grad = score_grad[..., :token_count]
    query_loc_grad_parts = (
        jnp.einsum("hqk,khd->qhd", local_grad, key_heads, preferred_element_type=jnp.float32)
        * scale_factor
    )
    query_mem_grad_parts = (
        jnp.einsum(
            "hqk,khd->qhd",
            score_grad[..., token_count:],
            memory_key_heads,
            preferred_element_type=jnp.float32,
        )
        * scale_factor
    )
    key_loc_grad = (
        jnp.einsum("hqk,qhd->khd", local_grad, query_loc_heads, preferred_element_type=jnp.float32)
        * scale_factor
    )
    probs_low = softmax_probs[..., :token_count].astype(jnp.bfloat16)
    value_loc_grad = jnp.einsum(
        "hqk,qhd->khd", probs_low, attended_heads_grad, preferred_element_type=jnp.float32
    )
    query_loc_grad = query_loc_grad_parts.reshape(token_count, model_width)
    query_mem_grad = query_mem_grad_parts.reshape(token_count, model_width)
    query_grad = (query_mem_grad + rotate(query_loc_grad, cosine, -sine_table)).astype(jnp.bfloat16)
    key_grad = rotate(key_loc_grad.reshape(token_count, model_width), cosine, -sine_table).astype(
        jnp.bfloat16
    )
    value_grad = value_loc_grad.reshape(token_count, model_width).astype(jnp.bfloat16)
    grad_query = contract_rows(normed_attn, query_grad)
    grad_key = contract_rows(normed_attn, key_grad)
    grad_value = contract_rows(normed_attn, value_grad)
    normed_attn_grad = (
        times_transpose(query_grad, query_full)
        + times_transpose(key_grad, key_full)
        + times_transpose(value_grad, value_full)
    )
    unused_attn, pull_attn = jax.vjp(rms_normed, tokens, attn_gain_full)
    tokens_norm_grad, grad_attn_gain = pull_attn(normed_attn_grad)
    input_grad = mixed_grad + tokens_norm_grad
    all_shares = (
        lax.psum_scatter(grad_query, "key", scatter_dimension=0, tiled=True),
        lax.psum_scatter(grad_key, "key", scatter_dimension=0, tiled=True),
        lax.psum_scatter(grad_value, "key", scatter_dimension=0, tiled=True),
        lax.psum_scatter(grad_out, "key", scatter_dimension=0, tiled=True),
        lax.psum_scatter(grad_gate, "key", scatter_dimension=0, tiled=True),
        lax.psum_scatter(grad_up, "key", scatter_dimension=0, tiled=True),
        lax.psum_scatter(grad_down, "key", scatter_dimension=0, tiled=True),
        lax.psum_scatter(grad_attn_gain, "key", scatter_dimension=0, tiled=True),
        lax.psum_scatter(grad_ffn_gain, "key", scatter_dimension=0, tiled=True),
    )
    (
        share_query,
        share_key,
        share_value,
        share_out,
        share_gate,
        share_up,
        share_down,
        share_attn_gain,
        share_ffn_gain,
    ) = all_shares
    summed = (
        lax.psum(share_query.astype(jnp.bfloat16), "dp").astype(jnp.float32),
        lax.psum(share_key.astype(jnp.bfloat16), "dp").astype(jnp.float32),
        lax.psum(share_value.astype(jnp.bfloat16), "dp").astype(jnp.float32),
        lax.psum(share_out.astype(jnp.bfloat16), "dp").astype(jnp.float32),
        lax.psum(share_gate.astype(jnp.bfloat16), "dp").astype(jnp.float32),
        lax.psum(share_up.astype(jnp.bfloat16), "dp").astype(jnp.float32),
        lax.psum(share_down.astype(jnp.bfloat16), "dp").astype(jnp.float32),
        lax.psum(share_attn_gain.astype(jnp.bfloat16), "dp").astype(jnp.float32),
        lax.psum(share_ffn_gain.astype(jnp.bfloat16), "dp").astype(jnp.float32),
    )
    (
        total_query,
        total_key,
        total_value,
        total_out,
        total_gate,
        total_up,
        total_down,
        total_attn_gain,
        total_ffn_gain,
    ) = summed
    return (
        outputs[None],
        input_grad[None],
        total_query,
        total_key,
        total_value,
        total_out,
        total_gate,
        total_up,
        total_down,
        total_attn_gain,
        total_ffn_gain,
        new_keys,
        new_values,
    )


def solution(mesh):
    placed = (
        P(("dp", "key"), None, None),
        P(("dp", "key"), None),
        P("dp"),
        P("dp"),
        P("dp", "key", None),
        P("dp", "key", None),
        P("key", None),
        P("key", None),
        P("key", None),
        P("key", None),
        P("key", None),
        P("key", None),
        P("key", None),
        P("key"),
        P("key"),
        P(("dp", "key"), None, None),
    )
    return jax.shard_map(
        per_device,
        mesh=mesh,
        in_specs=placed,
        out_specs=(
            P(("dp", "key"), None, None),
            P(("dp", "key"), None, None),
            P("key", None),
            P("key", None),
            P("key", None),
            P("key", None),
            P("key", None),
            P("key", None),
            P("key", None),
            P("key"),
            P("key"),
            P("dp", "key", None),
            P("dp", "key", None),
        ),
        check_vma=False,
    )
```

profile of v0, /device:TPU:0, one launch (start us, length us, event | category | flops | bytes accessed | tf_op | source)
XLA Modules:
  0.0 1193.3 jit_solution(11113431275451597658)
XLA Ops:
  11.8 1.8 gather_fusion.1
  14.9 2.2 pad_maximum_fusion.2
  17.1 6.5 all-to-all-start
  24.4 103.8 %all-gather = bf16[8,1,128]{2,1,0:T(2,128)(2,1)S(1)} all-gather(bf16[1,1,128]{2,1,0:T(2,128)(2,1)S(1)} %bitcast.188), channel_id=1, replica_groups=mesh['dp'=4,'key'=8] {'key'}, dimensions={0}, use_global_device_ids=true | all-gather | bytes 2304 | tf_op jit(solution)/shard_map/all_gather | solution.py:110
  128.8 42.1 %all-gather.1 = bf16[8,1,128]{2,1,0:T(2,128)(2,1)S(1)} all-gather(bf16[1,1,128]{2,1,0:T(2,128)(2,1)S(1)} %bitcast.189), channel_id=1, replica_groups=mesh['dp'=4,'key'=8] {'key'}, dimensions={0}, use_global_device_ids=true | all-gather | bytes 2304 | tf_op jit(solution)/shard_map/all_gather | solution.py:111
  172.8 2.1 fusion.68
  176.0 2.9 fusion.86
  180.8 3.9 fusion.92
  190.5 4.6 fusion.67
  195.2 3.9 convolution_convert_fusion.1
  199.0 4.1 fusion.89
  206.7 4.7 fusion.51
  211.5 8.3 fusion.38
  219.8 7.0 fusion.5
  227.7 2.9 copy.120
  232.2 18.6 %subtract_exponential_fusion = (f32[8,512,1536]{2,1,0:T(8,128)}, bf16[8,512,1536]{2,1,0:T(8,128)(2,1)S(1)}) fusion(f32[8,512]{1,0:T(8,128)S(1)} %log_add_fusion, f32[8,512,1024]{2,1,0:T(8,128)} %copy-done, f32[8,512,512]{2,1,0:T(8,128)} %fusion.67, pred[512,1536]{1,0:T(8,128)(4,1)S(1)} %copy-done.8, f32[8,512]{1,0:T(8,128)S(1)} %fusion.5, f32[8,512]{1,0:T(8,128)S(1)} %fusion.38), kind=kLoop, calls=%fused_computation.9 | loop fusion | flops 44040192 | bytes 63750144 | tf_op jit(solution)/shard_map/exp | solution.py:266
  250.9 3.0 fusion.8
  253.9 3.8 add_convert_fusion.1
  257.7 3.3 multiply_reduce_fusion.3
  261.3 8.2 fusion.93
  269.4 47.8 %all-gather.20.cloned.1.call-done = bf16[1024,2816]{1,0:T(8,128)(2,1)} async-done(((bf16[128,2816]{1,0:T(8,128)(2,1)}), bf16[1024,2816]{1,0:T(8,128)(2,1)}) %all-gather.20.cloned.1.call-update) | async-done | bytes 5767184 | tf_op jit(solution)/shard_map/all_gather | solution.py:108
  317.2 7.6 fusion.94
  324.8 53.2 %all-gather.22.cloned.1.call-done = bf16[2816,1024]{1,0:T(8,128)(2,1)} async-done(((bf16[352,1024]{1,0:T(8,128)(2,1)}), bf16[2816,1024]{1,0:T(8,128)(2,1)}) %all-gather.22.cloned.1.call-update) | async-done | bytes 5767184 | tf_op jit(solution)/shard_map/all_gather | solution.py:109
  378.0 11.4 multiply_convert_fusion.1
  389.4 7.3 fusion.95
  396.8 3.5 multiply_reduce_fusion.1
  402.4 2.3 convolution_convert_fusion
  406.1 9.7 fusion.49
  415.8 5.8 fusion.55
  421.6 36.0 %multiply_convert_fusion = bf16[8,512,1536]{2,1,0:T(8,128)(2,1)} fusion(f32[8,512,1536]{2,1,0:T(8,128)} %get-tuple-element.40, f32[8,512,1024]{2,1,0:T(8,128)} %fusion.49, f32[8,512,512]{2,1,0:T(8,128)} %fusion.55), kind=kOutput, calls=%fused_computation.6 | output fusion | flops 37754368 | bytes 62914560 | tf_op jit(solution)/shard_map/sub | solution.py:282
  457.6 4.3 multiply_bitcast_fusion.1
  461.9 3.6 multiply_subtract_fusion.1
  465.6 5.5 fusion.37
  471.1 2.3 copy.95
  473.4 5.0 fusion.82
  478.4 4.6 multiply_bitcast_fusion
  485.4 2.3 copy.98
  487.7 5.0 fusion.80
  493.2 4.3 fusion.47
  498.4 3.5 fusion.78
  503.2 4.8 fusion.64
  509.3 7.8 fusion.98
  517.2 7.8 fusion.99
  526.2 8.0 fusion.57
  535.5 47.1 %all_to_all.15 = bf16[8,64,1024]{2,1,0:T(8,128)(2,1)} all-to-all(bf16[8,64,1024]{2,1,0:T(8,128)(2,1)S(1)} %bitcast.170), channel_id=1, replica_groups=mesh['dp'=4,'key'=8] {'key'}, dimensions={0} | all-to-all | bytes 2097152 | tf_op jit(solution)/shard_map/all_to_all | solution.py:168
  582.6 3.6 all-to-all-start.2
  588.2 12.9 %reduce-scatter.10.cloned.1.call-done = f32[128,1024]{1,0:T(8,128)} async-done(((f32[1024,1024]{1,0:T(8,128)}), f32[128,1024]{1,0:T(8,128)}) %reduce-scatter.10.cloned.1.call-update) | async-done | bytes 524304 | tf_op jit(solution)/shard_map/reduce_scatter | solution.py:325
  602.9 69.4 %reduce-scatter.12.cloned.1.call-done = f32[128,1024]{1,0:T(8,128)} async-done(((f32[1024,1024]{1,0:T(8,128)}), f32[128,1024]{1,0:T(8,128)}) %reduce-scatter.12.cloned.1.call-update) | async-done | bytes 524304 | tf_op jit(solution)/shard_map/reduce_scatter | solution.py:326
  674.1 48.7 %reduce-scatter.14.cloned.1.call-done = f32[128,1024]{1,0:T(8,128)} async-done(((f32[1024,1024]{1,0:T(8,128)}), f32[128,1024]{1,0:T(8,128)}) %reduce-scatter.14.cloned.1.call-update) | async-done | bytes 524304 | tf_op jit(solution)/shard_map/reduce_scatter | solution.py:327
  724.6 117.9 %reduce-scatter.16.cloned.1.call-done = f32[128,2816]{1,0:T(8,128)} async-done(((f32[1024,2816]{1,0:T(8,128)}), f32[128,2816]{1,0:T(8,128)}) %reduce-scatter.16.cloned.1.call-update) | async-done | bytes 1441808 | tf_op jit(solution)/shard_map/reduce_scatter | solution.py:328
  842.4 2.3 convert_element_type.213
  844.8 117.7 %reduce-scatter.18.cloned.1.call-done = f32[128,2816]{1,0:T(8,128)} async-done(((f32[1024,2816]{1,0:T(8,128)}), f32[128,2816]{1,0:T(8,128)}) %reduce-scatter.18.cloned.1.call-update) | async-done | bytes 1441808 | tf_op jit(solution)/shard_map/reduce_scatter | solution.py:329
  962.4 2.3 convert_element_type.215
  964.7 117.5 %reduce-scatter.20.cloned.1.call-done = f32[352,1024]{1,0:T(8,128)} async-done(((f32[2816,1024]{1,0:T(8,128)}), f32[352,1024]{1,0:T(8,128)}) %reduce-scatter.20.cloned.1.call-update) | async-done | bytes 1441808 | tf_op jit(solution)/shard_map/reduce_scatter | solution.py:330
  1082.3 2.3 convert_element_type.217
  1087.5 3.4 fusion.96
  1093.3 3.1 fusion.29
  1096.4 13.9 %all-reduce.2 = (bf16[1024]{0:T(1024)(128)(2,1)S(1)}, bf16[1024]{0:T(1024)(128)(2,1)S(1)}) all-reduce(f32[1024]{0:T(1024)S(1)} %get-tuple-element.27, f32[1024]{0:T(1024)S(1)} %get-tuple-element.25), channel_id=9, replica_groups=mesh['dp'=4,'key'=8] {'key'}, use_global_device_ids=true, to_apply=%region_22.24.clone | all-reduce | flops 2048 | bytes 12288
  1110.4 10.1 all-reduce.3
  1121.6 4.3 fusion.36
  1125.9 6.8 fusion.48
  1132.7 41.9 %all-reduce.7.cloned.1.call-done = (bf16[128,1024]{1,0:T(8,128)(2,1)}, bf16[128,1024]{1,0:T(8,128)(2,1)}, bf16[128,1024]{1,0:T(8,128)(2,1)}, bf16[128,1024]{1,0:...) async-done(((bf16[128,1024]{1,0:T(8,128)(2,1)}, bf16[128,1024]{1,0:T(8,128)(2,1)}, bf16[128,1024]{1,0:T(8,128)(2,1)}, ...) | async-done | bytes 3211280 | tf_op jit(solution)/shard_map/psum | solution.py:346
  1174.6 1.9 convert_element_type.206
  1176.5 1.9 convert_element_type.208
  (208 shorter events, 57.1 us)
Async XLA Ops:
  7.2 4.0 copy-start.50
  7.2 4.0 copy-start.22
  7.2 168.8 %all-gather.12.cloned.1.call-start = ((), (), s32[]{:S(2)}) async-start(), calls=%async_computation.11 | async-start | bytes 2359296 | tf_op jit(solution)/shard_map/all_gather | solution.py:103
  7.9 172.9 %all-gather.14.cloned.1.call-start = ((), (), s32[]{:S(2)}) async-start(), calls=%async_computation.12 | async-start | bytes 2359296 | tf_op jit(solution)/shard_map/all_gather | solution.py:104
  8.7 186.5 %all-gather.10.cloned.1.call-start = ((), (), s32[]{:S(2)}) async-start(), calls=%async_computation.10 | async-start | bytes 2359296 | tf_op jit(solution)/shard_map/all_gather | solution.py:105
  9.4 248.3 %all-gather.16.cloned.1.call-start = ((), (), s32[]{:S(2)}) async-start(), calls=%async_computation.13 | async-start | bytes 2359296 | tf_op jit(solution)/shard_map/all_gather | solution.py:106
  10.0 251.3 %all-gather.18.cloned.1.call-start = ((), (), s32[]{:S(2)}) async-start(), calls=%async_computation.14 | async-start | bytes 6488064 | tf_op jit(solution)/shard_map/all_gather | solution.py:107
  10.6 306.6 %all-gather.20.cloned.1.call-start = ((), (), s32[]{:S(2)}) async-start(), calls=%async_computation.15 | async-start | bytes 6488064 | tf_op jit(solution)/shard_map/all_gather | solution.py:108
  17.1 7.3 copy-start.46
  17.1 111.1 %copy-start.41 = (s32[1,512]{1,0:T(1,128)S(1)}, s32[1,512]{1,0:T(1,128)}, u32[]{:S(2)}) copy-start(s32[1,512]{1,0:T(1,128)} %param.19) | copy-start | bytes 6148
  17.1 111.1 %copy-start.51 = (s32[8]{0:T(128)S(1)}, s32[8]{0:T(128)}, u32[]{:S(2)}) copy-start(s32[8]{0:T(128)} %param.20) | copy-start | bytes 100
  17.1 111.7 %copy-start.47 = (bf16[128]{0:T(256)(128)(2,1)S(1)}, bf16[128]{0:T(256)(128)(2,1)}, u32[]{:S(2)}) copy-start(bf16[128]{0:T(256)(128)(2,1)} %param.32) | copy-start | bytes 772
  17.1 154.5 %copy-start.3 = (bf16[1,512,1024]{2,1,0:T(8,128)(2,1)S(1)}, bf16[1,512,1024]{2,1,0:T(8,128)(2,1)}, u32[]{:S(2)}) copy-start(bf16[1,512,1024]{2,1,0:T(8,128)(2,1)} %param.18) | copy-start | bytes 3145732
  17.1 181.9 %all-to-all-start = ((bf16[8,256,1024]{2,1,0:T(8,128)(2,1)}), bf16[8,256,1024]{2,1,0:T(8,128)(2,1)}, u32[]{:S(2)}, u32[]{:S(2)}) async-start(bf16[8,256,1024]{2,1,0:T(8,128)(2,1)} %pad_maximum_fusion.2), calls=%async_computation | async-start | bytes 8388608 | tf_op jit(solution)/shard_map/all_to_all | solution.py:134
  23.6 354.4 %all-gather.22.cloned.1.call-start = ((), (), s32[]{:S(2)}) async-start(), calls=%async_computation.16 | async-start | bytes 6488064 | tf_op jit(solution)/shard_map/all_gather | solution.py:109
  24.3 562.0 %reduce-scatter.8.cloned.1.call-start = ((), (), s32[]{:S(2)}) async-start(), calls=%async_computation.17 | async-start | bytes 4718592 | tf_op jit(solution)/shard_map/reduce_scatter | solution.py:324
  128.2 67.0 %copy-start.39 = (f32[8,1,128]{2,1,0:T(1,128)}, f32[8,1,128]{2,1,0:T(1,128)S(1)}, u32[]{:S(2)}) copy-start(f32[8,1,128]{2,1,0:T(1,128)S(1)} %convert_element_type.225) | copy-start | bytes 12292
  172.5 22.7 %copy-start.44 = (f32[512]{0:T(512)}, f32[512]{0:T(512)S(1)}, u32[]{:S(2)}) copy-start(f32[512]{0:T(512)S(1)} %fusion.70) | copy-start | bytes 6148
  178.9 1.4 copy-start.11
  185.1 1.6 copy-start.32
  188.4 1.7 copy-start.13
  188.5 2.0 copy-start.14
  204.5 2.1 copy-start.12
  204.8 6.6 slice-start
  206.7 4.8 slice-start.1
  206.7 4.8 copy-start.8
  211.5 8.3 copy-start
  219.7 7.0 copy-start.24
  227.7 23.2 %copy-start.15 = (bf16[512,8,128]{0,2,1:T(8,128)(2,1)}, bf16[512,8,128]{0,2,1:T(8,128)(2,1)S(1)}, u32[]{:S(2)}) copy-start(bf16[512,8,128]{0,2,1:T(8,128)(2,1)S(1)} %copy.85) | copy-start | bytes 3145732
  232.2 18.7 %copy-start.16 = (bf16[512,8,128]{0,2,1:T(8,128)(2,1)}, bf16[512,8,128]{0,2,1:T(8,128)(2,1)S(1)}, u32[]{:S(2)}) copy-start(bf16[512,8,128]{0,2,1:T(8,128)(2,1)S(1)} %copy.84) | copy-start | bytes 3145732
  253.9 3.8 copy-start.4
  261.2 56.0 %copy-start.30 = (bf16[512,1024]{1,0:T(8,128)(2,1)}, bf16[512,1024]{1,0:T(8,128)(2,1)S(1)}, u32[]{:S(2)}) copy-start(bf16[512,1024]{1,0:T(8,128)(2,1)S(1)} %multiply_convert_fusion.3) | copy-start | bytes 3145732
  389.4 7.4 copy-start.54
  389.4 7.4 copy-start.53
  389.4 7.4 copy-start.48
  396.8 3.6 copy-start.33
  400.4 2.0 copy-start.26
  401.0 1.4 copy-start.2
  457.6 7.9 copy-start.1
  471.1 2.3 copy-start.40
  471.1 2.3 copy-start.45
  478.4 122.7 %reduce-scatter.10.cloned.1.call-start = ((), (), s32[]{:S(2)}) async-start(), calls=%async_computation.18 | async-start | bytes 4718592 | tf_op jit(solution)/shard_map/reduce_scatter | solution.py:325
  478.4 4.7 copy-start.25
  492.7 179.6 %reduce-scatter.12.cloned.1.call-start = ((), (), s32[]{:S(2)}) async-start(), calls=%async_computation.19 | async-start | bytes 4718592 | tf_op jit(solution)/shard_map/reduce_scatter | solution.py:326
  493.2 5.3 copy-start.5
  502.0 220.8 %reduce-scatter.14.cloned.1.call-start = ((), (), s32[]{:S(2)}) async-start(), calls=%async_computation.20 | async-start | bytes 4718592 | tf_op jit(solution)/shard_map/reduce_scatter | solution.py:327
  508.0 334.4 %reduce-scatter.16.cloned.1.call-start = ((), (), s32[]{:S(2)}) async-start(), calls=%async_computation.21 | async-start | bytes 12976128 | tf_op jit(solution)/shard_map/reduce_scatter | solution.py:328
  517.1 445.3 %reduce-scatter.18.cloned.1.call-start = ((), (), s32[]{:S(2)}) async-start(), calls=%async_computation.22 | async-start | bytes 12976128 | tf_op jit(solution)/shard_map/reduce_scatter | solution.py:329
  525.0 557.3 %reduce-scatter.20.cloned.1.call-start = ((), (), s32[]{:S(2)}) async-start(), calls=%async_computation.23 | async-start | bytes 12976128 | tf_op jit(solution)/shard_map/reduce_scatter | solution.py:330
  582.6 504.0 %all-to-all-start.2 = ((bf16[8,64,1024]{2,1,0:T(8,128)(2,1)}), bf16[8,64,1024]{2,1,0:T(8,128)(2,1)S(1)}, u32[]{:S(2)}, u32[]{:S(2)}) async-start(bf16[8,64,1024]{2,1,0:T(8,128)(2,1)} %bitcast.24), calls=%async_computation.9 | async-start | bytes 2097152 | tf_op jit(solution)/shard_map/all_to_all | solution.py:175
  586.1 588.5 %all-reduce.7.cloned.1.call-start = ((), (), s32[]{:S(2)}) async-start(), calls=%async_computation.24 | async-start | bytes 6422528 | tf_op jit(solution)/shard_map/psum | solution.py:346
  1087.5 3.4 copy-start.29
  1087.5 3.4 copy-start.49
  1090.9 1.4 copy-start.6
  1090.9 1.7 copy-start.21
  1090.9 2.4 copy-start.27
  1093.3 28.3 %copy-start.43 = (f32[512]{0:T(512)S(1)}, f32[512]{0:T(512)}, u32[]{:S(2)}) copy-start(f32[512]{0:T(512)} %copy-done.42) | copy-start | bytes 6148
  1121.6 4.3 copy-start.55
  1174.6 5.5 copy-start.38
  1174.6 6.4 copy-start.37
  1176.5 5.7 copy-start.36
  1181.0 2.4 copy-start.35
  1182.2 2.5 copy-start.17
  1183.4 2.2 copy-start.19
  (11 other events, 11.7 us)
Sparse Core Ops, SparseCore 0:
  9.6 44.7 all-gather.11
  56.0 75.4 all-gather.13
  133.1 32.5 all-gather.9
  167.1 27.9 all-gather.15
  196.6 59.9 all-gather.17
  258.1 59.0 all-gather.19
  318.9 59.1 all-gather.21
  478.5 48.6 reduce-scatter.7
  529.5 71.5 reduce-scatter.9
  603.2 68.9 reduce-scatter.11
  674.6 48.1 reduce-scatter.13
  724.9 117.4 reduce-scatter.15
  844.7 117.6 reduce-scatter.17
  964.6 117.6 reduce-scatter.19
  1086.6 87.9 all-reduce.6
where the time goes:
time: 1200 us; the launch traced here: 1190 us
  waiting for transfers between devices  631 us (53%)
  blocking collectives  217 us (18%)
  matrix products  161 us (13%)
  other arithmetic  114 us (10%)
  local copies, waits for them, and re-layouts  42.2 us (4%)
  between operations  16.2 us (1%)
    reduce_scatter x1, waiting for transfers between devices, per_device(): lax.psum_scatter(grad_gate, 'key', scatter_dimension=0, tiled=True)  118 us
    reduce_scatter x1, waiting for transfers between devices, per_device(): lax.psum_scatter(grad_up, 'key', scatter_dimension=0, tiled=True)  118 us
    reduce_scatter x1, waiting for transfers between devices, per_device(): lax.psum_scatter(grad_down, 'key', scatter_dimension=0, tiled=True)  118 us
    all_gather x1, blocking collectives, per_device(): lax.all_gather(attn_gain, 'key', axis=0, tiled=True)  104 us
    reduce_scatter x1, waiting for transfers between devices, per_device(): lax.psum_scatter(grad_value, 'key', scatter_dimension=0, tiled=True)  69.4 us
    all_gather x1, waiting for transfers between devices, per_device(): lax.all_gather(down_proj, 'key', axis=0, tiled=True)  53.2 us
    reduce_scatter x1, waiting for transfers between devices, per_device(): lax.psum_scatter(grad_out, 'key', scatter_dimension=0, tiled=True)  48.7 us
    all_gather x1, waiting for transfers between devices, per_device(): lax.all_gather(up_proj, 'key', axis=0, tiled=True)  47.8 us
  transfers between devices with their start and end apart: 17, of which 9 were waited for; matrix products, arithmetic and copies ran while one was open for 16% of the time, Pallas kernels for 0%

commit v1 on v0

v1 whole, which is shorter than its diff:
```python
import functools
import math

import jax
import jax.numpy as jnp
from jax import lax
from jax.experimental import pallas as pl
from jax.experimental.pallas import tpu as pltpu
from jax.sharding import PartitionSpec as P

H = 8
HD = 128
EPSILON = 1e-05
ROPE_BASE = 10000.0
NEG_FILL = -1e30
SCALE = 1.0 / math.sqrt(HD)
BF16 = jnp.bfloat16
F32 = jnp.float32
COLS = 256
GAIN_ROWS = 16
VMEM_LIMIT = 58 * 1024 * 1024


def dot(left, right):
    return jnp.dot(left, right, preferred_element_type=F32)


def dot_nt(left, right):
    return lax.dot_general(left, right, (((1,), (1,)), ((), ())), preferred_element_type=F32)


def dot_tn(left, right):
    return lax.dot_general(left, right, (((0,), (0,)), ((), ())), preferred_element_type=F32)


def inverse_rms(values):
    return lax.rsqrt(jnp.mean(values * values, axis=-1, keepdims=True) + EPSILON)


def turn(values, cosine, sine):
    return values * cosine + pltpu.roll(values, HD // 2, 1) * sine


class Plan:
    def __init__(self, n_dp, n_key):
        self.n_dp, self.n_key = n_dp, n_key
        self.fast = n_dp == 4 and n_key == 8
        self.halves = 2 if self.fast else 1


def swap(values, axis, size, distance):
    return lax.ppermute(values, axis, [(i, i ^ distance) for i in range(size)])


def own_quarter(weight, n_dp):
    width = weight.shape[1] // n_dp
    return lax.dynamic_slice_in_dim(weight, lax.axis_index("dp") * width, width, 1)


def along_z(quarter):
    return jnp.stack([quarter] + [swap(quarter, "key", 8, 2 * r) for r in (1, 2, 3)])


def across(held):
    return [held] + [swap(held, "dp", 4, r) for r in (1, 2, 3)]


def other_core(pieces):
    return [swap(piece, "key", 8, 1) for piece in pieces]


def after(values, token):
    return lax.optimization_barrier((values, token))[0]


def place(plan, pieces, first_row, rows, target, sem):
    copies = []
    q, key = lax.axis_index("dp"), lax.axis_index("key")
    for core in range(2):
        for far in range(4):
            for zr in range(4):
                block = key ^ (2 * zr + core)
                row = pl.multiple_of(block * rows, 16)
                column = pl.multiple_of((q ^ far) * COLS, COLS)
                copies.append(
                    pltpu.make_async_copy(
                        pieces[core * 4 + far].at[zr, pl.ds(first_row, rows)],
                        target.at[pl.ds(row, rows), pl.ds(column, COLS)],
                        sem,
                    )
                )
    return copies


def row_blocks(plan, width):
    if not plan.fast:
        return [(0, None, None, width)]
    rows = width // (plan.n_key * plan.n_dp)
    return [((z * 2 + c) * 4 + q, (z, c, q), None, rows) for z in range(4) for c in range(2) for q in range(4)]


def store_turned(plan, values, target, relative):
    turned = values.T
    if not plan.fast:
        target[0] = turned
        return
    q, key = lax.axis_index("dp"), lax.axis_index("key")
    core, z = lax.rem(key, 2), key // 2
    for natural, (zz, cc, qq), _, rows in row_blocks(plan, turned.shape[0]):
        qi = (q ^ qq) if relative else qq
        zi = (z ^ zz) if relative else zz
        row = pl.multiple_of((qi * 4 + zi) * rows, rows)
        target[core ^ cc, pl.ds(row, rows), :] = turned[natural * rows : (natural + 1) * rows]


def project_kernel(plan, n_pieces, x_ref, cos_ref, sin_ref, *refs):
    pieces, refs = refs[:n_pieces], refs[n_pieces:]
    qmem_ref, qloc_ref, kloc_ref, kraw_ref, v_ref, normed_ref, gains_ref, w_ref, g_ref, sems = refs
    width = x_ref.shape[1]
    if plan.fast:
        rows = width // plan.n_key
        copies = []
        for m in range(3):
            copies += place(plan, pieces, GAIN_ROWS + m * rows, rows, w_ref.at[m], sems.at[0])
        key = lax.axis_index("key")
        for core in range(2):
            for zr in range(4):
                copies.append(
                    pltpu.make_async_copy(
                        pieces[core * 4].at[zr, pl.ds(0, GAIN_ROWS)],
                        g_ref.at[key ^ (2 * zr + core)],
                        sems.at[1],
                    )
                )
        for copy in copies:
            copy.start()
        pltpu.make_async_copy(g_ref, g_ref, sems.at[1]).wait()
        lead = [g_ref[k][0:1, :].astype(F32) for k in range(plan.n_key)]
        attn_gain = jnp.concatenate([row[:, :rows] for row in lead], axis=1)
        ffn_gain = jnp.concatenate([row[:, rows:] for row in lead], axis=1)
    else:
        copy = pltpu.make_async_copy(pieces[0], w_ref, sems.at[0])
        copy.start()
        attn_gain = pieces[1][0:1, :]
        ffn_gain = pieces[1][1:2, :]
    gains_ref[0:1, :] = attn_gain
    gains_ref[1:2, :] = ffn_gain
    x = x_ref[...].astype(F32)
    normed = (x * inverse_rms(x) * attn_gain).astype(BF16)
    normed_ref[...] = normed
    pltpu.make_async_copy(w_ref, w_ref, sems.at[0]).wait()
    cosine, sine = cos_ref[...], sin_ref[...]
    for m in range(3):
        for c in range(width // COLS):
            cols = slice(c * COLS, (c + 1) * COLS)
            raw = dot(normed, w_ref[m, :, cols])
            low = raw.astype(BF16)
            if m == 2:
                v_ref[:, cols] = low
                continue
            (qmem_ref if m == 0 else kraw_ref)[:, cols] = low
            out = qloc_ref if m == 0 else kloc_ref
            for h in range(COLS // HD):
                part = raw[:, h * HD : (h + 1) * HD]
                start = c * COLS + h * HD
                out[:, start : start + HD] = turn(part, cosine, sine).astype(BF16)


def project(plan, x, cosine, sine, pieces):
    tokens, width = x.shape
    whole = pl.BlockSpec(memory_space=pltpu.VMEM)
    anywhere = pl.BlockSpec(memory_space=pl.ANY)
    row = jax.ShapeDtypeStruct((tokens, width), BF16)
    return pl.pallas_call(
        functools.partial(project_kernel, plan, len(pieces)),
        out_shape=[row] * 6 + [jax.ShapeDtypeStruct((2, width), F32)],
        in_specs=[whole] * 3 + ([anywhere] * len(pieces) if plan.fast else [anywhere, whole]),
        out_specs=[whole] * 7,
        scratch_shapes=[
            pltpu.VMEM((3, width, width), BF16),
            pltpu.VMEM((plan.n_key, GAIN_ROWS, COLS), BF16),
            pltpu.SemaphoreType.DMA((2,)),
        ],
        compiler_params=pltpu.CompilerParams(vmem_limit_bytes=VMEM_LIMIT),
        cost_estimate=pl.CostEstimate(
            flops=6 * tokens * width * width, bytes_accessed=16 * 2**20, transcendentals=0
        ),
        name="project",
    )(x, cosine, sine, *pieces)


def memory_of(memory_ref):
    block = memory_ref[...]
    sources, rows, width = block.shape
    half = rows // 2
    keys = block[:, :half].reshape(sources * half, width)
    values = block[:, half:].reshape(sources * half, width)
    return keys, values


def attend_kernel(qmem, qloc, kloc, v, memory, local_bias, memory_bias, out, p_loc, p_mem):
    mem_k, mem_v = memory_of(memory)
    s_loc = dot_nt(qloc[...], kloc[...]) * SCALE + local_bias[...]
    s_mem = dot_nt(qmem[...], mem_k) * SCALE + memory_bias[...]
    largest = jnp.maximum(
        jnp.max(s_loc, axis=-1, keepdims=True), jnp.max(s_mem, axis=-1, keepdims=True)
    )
    e_loc = jnp.exp(s_loc - largest)
    e_mem = jnp.exp(s_mem - largest)
    total = jnp.sum(e_loc, axis=-1, keepdims=True) + jnp.sum(e_mem, axis=-1, keepdims=True)
    inverse = 1.0 / total
    low_loc = (e_loc * inverse).astype(BF16)
    low_mem = (e_mem * inverse).astype(BF16)
    p_loc[0] = low_loc
    p_mem[0] = low_mem
    out[...] = (dot(low_loc, v[...]) + dot(low_mem, mem_v)).astype(BF16)


def attend(qmem, qloc, kloc, v, memory, local_bias, memory_bias):
    tokens, width = qmem.shape
    keys = memory_bias.shape[1]
    head = pl.BlockSpec((tokens, HD), lambda h: (0, h))
    return pl.pallas_call(
        attend_kernel,
        grid=(width // HD,),
        in_specs=[head] * 4
        + [
            pl.BlockSpec(memory.shape[:2] + (HD,), lambda h: (0, 0, h)),
            pl.BlockSpec((tokens, tokens), lambda h: (0, 0)),
            pl.BlockSpec((1, keys), lambda h: (0, 0)),
        ],
        out_specs=[
            head,
            pl.BlockSpec((1, tokens, tokens), lambda h: (h, 0, 0)),
            pl.BlockSpec((1, tokens, keys), lambda h: (h, 0, 0)),
        ],
        out_shape=[
            jax.ShapeDtypeStruct((tokens, width), BF16),
            jax.ShapeDtypeStruct((width // HD, tokens, tokens), BF16),
            jax.ShapeDtypeStruct((width // HD, tokens, keys), BF16),
        ],
        compiler_params=pltpu.CompilerParams(vmem_limit_bytes=VMEM_LIMIT),
        cost_estimate=pl.CostEstimate(
            flops=4 * tokens * (tokens + keys) * width,
            bytes_accessed=24 * 2**20,
            transcendentals=tokens * (tokens + keys) * (width // HD),
        ),
        name="attend",
    )(qmem, qloc, kloc, v, memory, local_bias, memory_bias)


def feed_kernel(plan, n_pieces, x_ref, att_ref, ct_ref, gains_ref, gate_ref, up_ref, *refs):
    pieces, refs = refs[:n_pieces], refs[n_pieces:]
    n_half = plan.halves
    gu_refs, refs = refs[:n_half], refs[n_half:]
    (gd_ref, go_ref, out_ref, dmix_ref, datt_ref, dgain_ref) = refs[:6]
    wo, wd, mixed, normed, turned, acc_out, acc_back, sems = refs[6:]
    step = pl.program_id(0)
    width = x_ref.shape[1]
    gain = gains_ref[1:2, :]

    @pl.when(step == 0)
    def _():
        if plan.fast:
            rows = width // plan.n_key
            for copy in place(plan, pieces, 0, rows, wo, sems.at[0]):
                copy.start()
            for copy in place(plan, pieces, rows, wd.shape[0] // plan.n_key, wd, sems.at[1]):
                copy.start()
        else:
            pltpu.make_async_copy(pieces[0], wo, sems.at[0]).start()
            pltpu.make_async_copy(pieces[1], wd, sems.at[1]).start()
        pltpu.make_async_copy(wo, wo, sems.at[0]).wait()
        mixed[...] = x_ref[...].astype(F32) + dot(att_ref[...], wo[...])
        value = mixed[...]
        low = (value * inverse_rms(value) * gain).astype(BF16)
        normed[...] = low
        store_turned(plan, low, turned, False)
        acc_out[...] = jnp.zeros_like(acc_out)
        acc_back[...] = jnp.zeros_like(acc_back)
        pltpu.make_async_copy(wd, wd, sems.at[1]).wait()

    ct = ct_ref[...]
    down = wd[pl.ds(pl.multiple_of(step * COLS, COLS), COLS), :]
    gate = dot(normed[...], gate_ref[...])
    up = dot(normed[...], up_ref[...])
    back = dot_nt(ct, down)
    sigma = 1.0 / (1.0 + jnp.exp(-gate))
    swish = gate * sigma
    hidden = (swish * up).astype(BF16)
    d_gate = (back * up * (sigma * (1.0 + gate * (1.0 - sigma)))).astype(BF16)
    d_up = (back * swish).astype(BF16)
    acc_out[...] += dot(hidden, down)
    acc_back[...] += dot_nt(d_gate, gate_ref[...]) + dot_nt(d_up, up_ref[...])
    grad_down = dot_tn(hidden, ct).astype(BF16)
    for c in range(width // COLS):
        gd_ref[c] = grad_down[:, c * COLS : (c + 1) * COLS]
    for half in range(n_half):
        lead = gu_refs[half].shape[:2]
        for i, grad in enumerate((d_gate, d_up)):
            value = dot(turned[half], grad).astype(BF16)
            gu_refs[half][:, :, i] = value.reshape(lead + (-1, COLS))

    @pl.when(step == pl.num_programs(0) - 1)
    def _():
        value = mixed[...]
        out_ref[...] = (value + acc_out[...]).astype(BF16)
        rf = inverse_rms(value)
        d_normed = acc_back[...]
        scaled = d_normed * gain
        d_mixed = (
            ct.astype(F32)
            + rf * scaled
            - value * (rf * rf * rf) * jnp.mean(scaled * value, axis=-1, keepdims=True)
        )
        dgain_ref[...] = jnp.sum(d_normed * value * rf, axis=0, keepdims=True)
        dmix_ref[...] = d_mixed
        branch = d_mixed.astype(BF16)
        datt_ref[...] = dot_nt(branch, wo[...]).astype(BF16)
        for c in range(width // COLS):
            go_ref[c] = dot_tn(att_ref[...], branch[:, c * COLS : (c + 1) * COLS]).astype(BF16)


def feed(plan, x, attended, ct, gains, gate_up, pieces):
    tokens, width = x.shape
    ff = gate_up.shape[1] // 2
    steps = ff // COLS
    const = lambda *block: pl.BlockSpec(block, lambda j: (0,) * len(block))
    if plan.fast:
        lead = (plan.n_dp, plan.n_key // 2)
        rows = width // (plan.n_dp * plan.n_key)
    else:
        lead, rows = (1, 1), width
    grads = jax.ShapeDtypeStruct(lead + (2, rows, ff), BF16)
    return pl.pallas_call(
        functools.partial(feed_kernel, plan, len(pieces)),
        grid=(steps,),
        in_specs=[const(tokens, width)] * 3
        + [
            const(2, width),
            pl.BlockSpec((width, COLS), lambda j: (0, j)),
            pl.BlockSpec((width, COLS), lambda j: (0, j + steps)),
        ]
        + [pl.BlockSpec(memory_space=pl.ANY)] * len(pieces),
        out_specs=[pl.BlockSpec(lead + (2, rows, COLS), lambda j: (0, 0, 0, 0, j))] * plan.halves
        + [
            pl.BlockSpec((width // COLS, COLS, COLS), lambda j: (0, j, 0)),
            const(width // COLS, width, COLS),
            const(tokens, width),
            const(tokens, width),
            const(tokens, width),
            const(1, width),
        ],
        out_shape=[grads] * plan.halves
        + [
            jax.ShapeDtypeStruct((width // COLS, ff, COLS), BF16),
            jax.ShapeDtypeStruct((width // COLS, width, COLS), BF16),
            jax.ShapeDtypeStruct((tokens, width), BF16),
            jax.ShapeDtypeStruct((tokens, width), F32),
            jax.ShapeDtypeStruct((tokens, width), BF16),
            jax.ShapeDtypeStruct((1, width), F32),
        ],
        scratch_shapes=[
            pltpu.VMEM((width, width), BF16),
            pltpu.VMEM((ff, width), BF16),
            pltpu.VMEM((tokens, width), F32),
            pltpu.VMEM((tokens, width), BF16),
            pltpu.VMEM((plan.halves, width // plan.halves, tokens), BF16),
            pltpu.VMEM((tokens, width), F32),
            pltpu.VMEM((tokens, width), F32),
            pltpu.SemaphoreType.DMA((2,)),
        ],
        compiler_params=pltpu.CompilerParams(vmem_limit_bytes=VMEM_LIMIT),
        cost_estimate=pl.CostEstimate(
            flops=18 * tokens * width * ff, bytes_accessed=48 * 2**20, transcendentals=tokens * ff
        ),
        name="feed",
    )(x, attended, ct, gains, gate_up, gate_up, *pieces)


def attend_back_kernel(
    p_loc, p_mem, datt, att, qloc, kloc, v, memory, cos_ref, sin_ref, dq_ref, dk_ref, dv_ref
):
    mem_k, mem_v = memory_of(memory)
    grad = datt[...]
    delta = jnp.sum(grad.astype(F32) * att[...].astype(F32), axis=-1, keepdims=True)
    low_loc = p_loc[0]
    ds_loc = (low_loc.astype(F32) * (dot_nt(grad, v[...]) - delta)).astype(BF16)
    ds_mem = (p_mem[0].astype(F32) * (dot_nt(grad, mem_v) - delta)).astype(BF16)
    cosine, sine = cos_ref[...], sin_ref[...]
    dq_loc = dot(ds_loc, kloc[...]) * SCALE
    dq_mem = dot(ds_mem, mem_k) * SCALE
    dk = dot_tn(ds_loc, qloc[...]) * SCALE
    dq_ref[...] = (dq_mem + turn(dq_loc, cosine, -sine)).astype(BF16)
    dk_ref[...] = turn(dk, cosine, -sine).astype(BF16)
    dv_ref[...] = dot_tn(low_loc, grad).astype(BF16)


def attend_back(p_loc, p_mem, datt, att, qloc, kloc, v, memory, cosine, sine):
    tokens, width = datt.shape
    keys = p_mem.shape[2]
    head = pl.BlockSpec((tokens, HD), lambda h: (0, h))
    table = pl.BlockSpec((tokens, HD), lambda h: (0, 0))
    return pl.pallas_call(
        attend_back_kernel,
        grid=(width // HD,),
        in_specs=[
            pl.BlockSpec((1, tokens, tokens), lambda h: (h, 0, 0)),
            pl.BlockSpec((1, tokens, keys), lambda h: (h, 0, 0)),
        ]
        + [head] * 5
        + [pl.BlockSpec(memory.shape[:2] + (HD,), lambda h: (0, 0, h)), table, table],
        out_specs=[head] * 3,
        out_shape=[jax.ShapeDtypeStruct((tokens, width), BF16)] * 3,
        compiler_params=pltpu.CompilerParams(vmem_limit_bytes=VMEM_LIMIT),
        cost_estimate=pl.CostEstimate(
            flops=4 * tokens * (2 * tokens + keys) * width,
            bytes_accessed=24 * 2**20,
            transcendentals=0,
        ),
        name="attend_back",
    )(p_loc, p_mem, datt, att, qloc, kloc, v, memory, cosine, sine)


def project_back_kernel(plan, n_pieces, x_ref, normed_ref, dmix_ref, gains_ref, dgain_ref, dq, dk, dv, *refs):
    pieces, refs = refs[:n_pieces], refs[n_pieces:]
    n_half = plan.halves
    g_refs, refs = refs[:n_half], refs[n_half:]
    xgrad_ref, again_ref, w_ref, turned, sems = refs
    width = x_ref.shape[1]
    if plan.fast:
        rows = width // plan.n_key
        for m in range(3):
            for copy in place(plan, pieces, GAIN_ROWS + m * rows, rows, w_ref.at[m], sems.at[0]):
                copy.start()
    else:
        pltpu.make_async_copy(pieces[0], w_ref, sems.at[0]).start()
    store_turned(plan, normed_ref[...], turned, True)
    low = (dq, dk, dv)
    for half in range(n_half):
        rows = g_refs[half].shape[2] - GAIN_ROWS
        each = rows // 3
        lead = g_refs[half].shape[:2]
        for m in range(3):
            for c in range(width // COLS):
                cols = slice(c * COLS, (c + 1) * COLS)
                value = dot(turned[half], low[m][:, cols]).astype(BF16)
                g_refs[half][:, :, m * each : (m + 1) * each, cols] = value.reshape(
                    lead + (each, COLS)
                )
    pltpu.make_async_copy(w_ref, w_ref, sems.at[0]).wait()
    d_normed = dot_nt(dq[...], w_ref[0]) + dot_nt(dk[...], w_ref[1]) + dot_nt(dv[...], w_ref[2])
    x = x_ref[...].astype(F32)
    ra = inverse_rms(x)
    scaled = d_normed * gains_ref[0:1, :]
    xgrad_ref[...] = (
        dmix_ref[...]
        + ra * scaled
        - x * (ra * ra * ra) * jnp.mean(scaled * x, axis=-1, keepdims=True)
    )
    attn = jnp.sum(d_normed * x * ra, axis=0, keepdims=True)
    ffn = dgain_ref[...]
    again_ref[0:1, :] = attn
    again_ref[1:2, :] = ffn
    if plan.fast:
        key = lax.axis_index("key")
        core, z = lax.rem(key, 2), key // 2
        span = width // plan.n_key
        fill = jnp.zeros((1, width - 2 * span), F32)
        for zz in range(4):
            both = [
                jnp.concatenate(
                    [
                        attn[:, (zz * 2 + c) * span : (zz * 2 + c + 1) * span],
                        ffn[:, (zz * 2 + c) * span : (zz * 2 + c + 1) * span],
                        fill,
                    ],
                    axis=1,
                )
                for c in range(2)
            ]
            for half in range(2):
                row = jnp.where(core == half, both[0], both[1])
                tile = jnp.broadcast_to(row, (GAIN_ROWS, width)).astype(BF16)
                top = g_refs[half].shape[2] - GAIN_ROWS
                for far in range(4):
                    g_refs[half][far, z ^ zz, top:, :] = tile


def project_back(plan, x, normed, dmix, gains, dgain, dq, dk, dv, pieces):
    tokens, width = x.shape
    whole = pl.BlockSpec(memory_space=pltpu.VMEM)
    if plan.fast:
        lead = (plan.n_dp, plan.n_key // 2)
        rows = width // (plan.n_dp * plan.n_key)
    else:
        lead, rows = (1, 1), width
    grads = jax.ShapeDtypeStruct(lead + (3 * rows + GAIN_ROWS, width), BF16)
    return pl.pallas_call(
        functools.partial(project_back_kernel, plan, len(pieces)),
        in_specs=[whole] * 8 + [pl.BlockSpec(memory_space=pl.ANY)] * len(pieces),
        out_specs=[whole] * (plan.halves + 2),
        out_shape=[grads] * plan.halves
        + [
            jax.ShapeDtypeStruct((tokens, width), F32),
            jax.ShapeDtypeStruct((2, width), F32),
        ],
        scratch_shapes=[
            pltpu.VMEM((3, width, width), BF16),
            pltpu.VMEM((plan.halves, width // plan.halves, tokens), BF16),
            pltpu.SemaphoreType.DMA((1,)),
        ],
        compiler_params=pltpu.CompilerParams(vmem_limit_bytes=VMEM_LIMIT),
        cost_estimate=pl.CostEstimate(
            flops=12 * tokens * width * width, bytes_accessed=24 * 2**20, transcendentals=0
        ),
        name="project_back",
    )(x, normed, dmix, gains, dgain, dq, dk, dv, *pieces)


def add(*parts):
    total = parts[0].astype(F32)
    for part in parts[1:]:
        total = total + part.astype(F32)
    return total.astype(BF16)


def own_rows(natural, blocks, core):
    split = natural.reshape(natural.shape[0], blocks // 2, 2, -1, natural.shape[2])
    return lax.dynamic_index_in_dim(split, core, 2, keepdims=False)


def offloaded_sum(share):
    groups = [[0, 2, 4, 6], [1, 3, 5, 7]]
    share = lax.psum_scatter(share, "dp", scatter_dimension=0, tiled=False)
    share = lax.psum_scatter(
        share, "key", scatter_dimension=0, tiled=False, axis_index_groups=groups
    )
    return lax.all_gather(share, "dp", axis=0)


def swapped_sum(share):
    share = add(share[0], *[swap(share[r], "dp", 4, r) for r in (1, 2, 3)])
    share = add(share[0], *[swap(share[r], "key", 8, 2 * r) for r in (1, 2, 3)])
    held = jnp.stack([share] + [swap(share, "dp", 4, r) for r in (1, 2, 3)])
    return jnp.take(held, jnp.arange(4) ^ lax.axis_index("dp"), axis=0)


def per_device(
    plan,
    inputs,
    positions,
    memory_flag,
    partner,
    cache_keys,
    cache_values,
    query_proj,
    key_proj,
    value_proj,
    out_proj,
    gate_proj,
    up_proj,
    down_proj,
    attn_gain,
    ffn_gain,
    cotangent,
):
    x, ct, token_pos = inputs[0], cotangent[0], positions[0]
    tokens, width = x.shape
    group, slots = cache_keys.shape[0], cache_keys.shape[1]
    key = lax.axis_index("key")
    n_dp = plan.n_dp

    half = HD // 2
    frequency = ROPE_BASE ** (-2.0 * jnp.arange(half, dtype=F32) / HD)
    angles = token_pos.astype(F32)[:, None] * frequency[None, :]
    cosine, sine = jnp.cos(angles), jnp.sin(angles)
    cosine = jnp.concatenate([cosine, cosine], axis=1)
    sine = jnp.concatenate([-sine, sine], axis=1)
    order = jnp.arange(tokens, dtype=jnp.int32)
    valid = (order[None, :] <= order[:, None]) & (
        token_pos[:, None] - token_pos[None, :] == order[:, None] - order[None, :]
    )
    local_bias = jnp.where(valid, 0.0, NEG_FILL).astype(F32)
    self_flag = jnp.take(memory_flag, key)
    place_in_slot = jnp.arange(group * 2 * slots, dtype=jnp.int32) % (2 * slots)
    memory_bias = jnp.where((place_in_slot >= slots) | (self_flag == 1), 0.0, NEG_FILL)
    memory_bias = memory_bias.astype(F32)[None, :]

    outgoing = jnp.concatenate(
        [
            cache_keys,
            jnp.take(cache_keys, partner, axis=0),
            cache_values,
            jnp.take(cache_values, partner, axis=0),
        ],
        axis=1,
    )
    gate_up = jnp.concatenate([gate_proj, up_proj], axis=1)
    if plan.fast:
        share = gate_up.shape[0] // n_dp
        gate_up = lax.dynamic_slice_in_dim(gate_up, lax.axis_index("dp") * share, share, 0)
        gate_up = lax.all_gather(gate_up, ("key", "dp"), axis=0, tiled=True)
        gains = jnp.concatenate([attn_gain, ffn_gain])[None, :]
        first = along_z(
            jnp.concatenate(
                [jnp.broadcast_to(gains, (GAIN_ROWS, COLS))]
                + [own_quarter(w, n_dp) for w in (query_proj, key_proj, value_proj)],
                axis=0,
            )
        )
        second = jnp.concatenate([own_quarter(w, n_dp) for w in (out_proj, down_proj)], axis=0)
        outgoing, second = after((outgoing, second), first)
        first = across(first)
        first = first + other_core(first)
        second = across(along_z(second))
        second = second + other_core(second)
    else:
        whole = lambda w: lax.all_gather(w, "key", axis=0, tiled=True)
        gate_up = whole(gate_up)
        first = [
            jnp.stack([whole(query_proj), whole(key_proj), whole(value_proj)]),
            jnp.stack([whole(attn_gain), whole(ffn_gain)]).astype(F32),
        ]
        second = [whole(out_proj), whole(down_proj)]
    memory = lax.all_to_all(outgoing, "key", split_axis=0, concat_axis=0, tiled=True)

    qmem, qloc, kloc, kraw, v, normed, gains = project(plan, x, cosine, sine, first)
    attended, p_loc, p_mem = attend(qmem, qloc, kloc, v, memory, local_bias, memory_bias)

    run = tokens // group
    fresh = jnp.stack([kraw.reshape(group, run, width), v.reshape(group, run, width)], axis=1)
    fresh = after(fresh, attended)
    arrived = lax.all_to_all(fresh, "key", split_axis=0, concat_axis=0, tiled=True)
    new_keys = jnp.concatenate([cache_keys[:, run:], arrived[:, 0]], axis=1)
    new_values = jnp.concatenate([cache_values[:, run:], arrived[:, 1]], axis=1)

    *g_gu, g_down, g_out, outputs, dmix, datt, dgain = feed(
        plan, x, attended, ct, gains, gate_up, second
    )
    dq, dk, dv = attend_back(p_loc, p_mem, datt, attended, qloc, kloc, v, memory, cosine, sine)
    *g_qkv, input_grad, gain_grads = project_back(
        plan, x, normed, dmix, gains, dgain, dq, dk, dv, first[:8] if plan.fast else first[:1]
    )

    rows = width // plan.n_key
    if plan.fast:
        core = lax.rem(key, 2)
        g_gu = offloaded_sum(add(g_gu[0], swap(g_gu[1], "key", 8, 1)))
        natural = (g_down, g_out)
        mine = jnp.concatenate([own_rows(g, 8, core) for g in natural], axis=2)
        other = jnp.concatenate([own_rows(g, 8, 1 - core) for g in natural], axis=2)
        g_do = offloaded_sum(add(mine, swap(other, "key", 8, 1)))
        g_do = g_do.transpose(1, 0, 2).reshape(-1, width).astype(F32)
        total_down, total_out = g_do[:-rows], g_do[-rows:]
        total_gate = g_gu[:, 0].reshape(rows, -1).astype(F32)
        total_up = g_gu[:, 1].reshape(rows, -1).astype(F32)
        g_qkv = swapped_sum(add(g_qkv[0], swap(g_qkv[1], "key", 8, 1))).astype(F32)
        each = rows // n_dp
        total_query, total_key, total_value = (
            g_qkv[:, m * each : (m + 1) * each].reshape(rows, width) for m in range(3)
        )
        total_attn, total_ffn = g_qkv[0, 3 * each, :rows], g_qkv[0, 3 * each, rows : 2 * rows]
    else:

        def total(g):
            g = lax.psum_scatter(g.astype(F32), "key", scatter_dimension=0, tiled=True)
            return lax.psum(g.astype(BF16), "dp").astype(F32)

        wide = lambda g: g.transpose(1, 0, 2).reshape(g.shape[1], width)
        total_query, total_key, total_value = (
            total(g_qkv[0][0, 0, m * width : (m + 1) * width]) for m in range(3)
        )
        total_gate, total_up = total(g_gu[0][0, 0, 0]), total(g_gu[0][0, 0, 1])
        total_down, total_out = total(wide(g_down)), total(wide(g_out))
        total_attn, total_ffn = total(gain_grads[0]), total(gain_grads[1])
    return (
        outputs[None],
        input_grad[None],
        total_query,
        total_key,
        total_value,
        total_out,
        total_gate,
        total_up,
        total_down,
        total_attn,
        total_ffn,
        new_keys,
        new_values,
    )


def solution(mesh):
    plan = Plan(mesh.shape["dp"], mesh.shape["key"])
    rows, cache = P(("dp", "key"), None, None), P("dp", "key", None)
    weight, gain = P("key", None), P("key")
    return jax.shard_map(
        functools.partial(per_device, plan),
        mesh=mesh,
        in_specs=(rows, P(("dp", "key"), None), P("dp"), P("dp"), cache, cache)
        + (weight,) * 7
        + (gain, gain, rows),
        out_specs=(rows, rows) + (weight,) * 7 + (gain, gain, cache, cache),
        check_vma=False,
    )
```

time: 1200 us -> 599 us (0.50)
  waiting for transfers between devices: 631 us -> 350 us
  blocking collectives: 217 us -> 18.1 us
  matrix products: 161 us -> 0 us
  Pallas kernels: 0 us -> 106 us
  other arithmetic: 114 us -> 35.7 us
  starting transfers between devices: 11.2 us -> 49 us
  local copies, waits for them, and re-layouts: 42.2 us -> 24 us
    reduce_scatter x7 -> x2, waiting for transfers between devices: 484 us -> 0.02 us  [offloaded_sum(): lax.psum_scatter(share, 'key', scatter_dimension=0, tiled=False, axis_ind...]
    ppermute x0 -> x32, waiting for transfers between devices: none -> 287 us  [swap(): return lax.ppermute(values, axis, [(i, i ^ distance) for i in range(size)])]
    dot_general x31 -> x0, matrix products: 161 us -> none  [the longest x7 41.9 us: contract_rows(): lax.dot_general(left, right, (((0,), (0,)), ((), ())), preferred_element_...]
    all_gather x2 -> x1, blocking collectives: 146 us -> 18.1 us  [offloaded_sum(): return lax.all_gather(share, 'dp', axis=0)]
    pallas_call x0 -> x5, Pallas kernels: none -> 106 us  [the longest x1 43.4 us: feed(): pl.pallas_call(functools.partial(feed_kernel, plan, len(pieces)), grid=(s...]
    all_gather x7 -> x2, waiting for transfers between devices: 101 us -> 0.02 us  [the longest x1 0.02 us: per_device(): gate_up = lax.all_gather(gate_up, ('key', 'dp'), axis=0, tiled=True)]
    unnamed x15 -> x8, waiting for transfers between devices: 4.46 us -> 62.6 us
    all_to_all x1 -> x0, blocking collectives: 47.1 us -> none  [per_device(): lax.all_to_all(fresh_keys.reshape(seg_group, fresh_share, model_width), '...]
  transfers between devices with their start and end apart: 17 -> 40, of which waited for: 9 -> 17; matrix products, arithmetic and copies ran while one was open for 16% -> 7% of each run, Pallas kernels for 0% -> 10%
where the time goes in v1:
time: 599 us; the launch traced here: 597 us
  waiting for transfers between devices  350 us (58%)
  Pallas kernels  106 us (18%)
  starting transfers between devices  49 us (8%)
  other arithmetic  35.7 us (6%)
  local copies, waits for them, and re-layouts  24 us (4%)
  blocking collectives  18.1 us (3%)
  between operations  15.3 us (3%)
    ppermute x32, waiting for transfers between devices, swap(): return lax.ppermute(values, axis, [(i, i ^ distance) for i in range(size)])  287 us
    unnamed x8, waiting for transfers between devices  62.6 us
    pallas_call x1, Pallas kernels, feed(): pl.pallas_call(functools.partial(feed_kernel, plan, len(pieces)), grid=(s...  43.4 us
    ppermute x32, starting transfers between devices, swap(): return lax.ppermute(values, axis, [(i, i ^ distance) for i in range(size)])  33.3 us
    pallas_call x1, Pallas kernels, attend(): pl.pallas_call(attend_kernel, grid=(width // HD,), in_specs=[head] * 4 +...  22 us
    convert_element_type x5, other arithmetic, add(): return total.astype(BF16)  19.6 us
    all_gather x1, blocking collectives, offloaded_sum(): return lax.all_gather(share, 'dp', axis=0)  18.1 us
    pallas_call x1, Pallas kernels, attend_back(): pl.pallas_call(attend_back_kernel, grid=(width // HD,), in_specs=[pl.Bloc...  16.3 us
  transfers between devices with their start and end apart: 40, of which 17 were waited for; matrix products, arithmetic and copies ran while one was open for 7% of the time, Pallas kernels for 10%

profile of v1, /device:TPU:0, one launch (start us, length us, event | category | flops | bytes accessed | tf_op | source)
XLA Modules:
  0.0 597.5 jit_solution(15742479338823699778)
XLA Ops:
  7.3 1.9 fusion.8
  12.3 3.0 collective-permute-start
  15.3 2.6 collective-permute-start.1
  19.2 1.8 gather_fusion.2
  21.4 0.9 copy-done.4
  22.7 2.2 pad_maximum_fusion
  25.8 10.8 %collective-permute-done.1 = bf16[400,256]{1,0:T(8,128)(2,1)S(1)} collective-permute-done((bf16[400,256]{1,0:T(8,128)(2,1)}, bf16[400,256]{1,0:T(8,128)(2,1)S(1)}, u32[]{:S(2)}, u32[]{:S(2)}) %collective-permute-start.1) | collective-permute-done | bytes 204832 | tf_op jit(solution)/shard_map/ppermute | solution.py:52
  36.6 1.0 pad_maximum_fusion.5.refs_0_
  37.6 10.4 %all-to-all-start = ((bf16[8,256,1024]{2,1,0:T(8,128)(2,1)}), bf16[8,256,1024]{2,1,0:T(8,128)(2,1)}, u32[]{:S(2)}, u32[]{:S(2)}) async-start(bf16[8,256,1024]{2,1,0:T(8,128)(2,1)} %pad_maximum_fusion), calls=%async_computation | async-start | bytes 8388608 | tf_op jit(solution)/shard_map/all_to_all | solution.py:626
  48.1 2.3 collective-permute-start.10
  50.4 2.0 collective-permute-start.11
  52.5 1.5 collective-permute-start.3
  54.0 1.5 collective-permute-start.4
  55.9 111.9 %collective-permute-done.10 = bf16[480,256]{1,0:T(8,128)(2,1)S(1)} collective-permute-done((bf16[480,256]{1,0:T(8,128)(2,1)S(1)}, bf16[480,256]{1,0:T(8,128)(2,1)S(1)}, u32[]{:S(2)}, u32[]{:S(2)}) %collective-permute-start.10) | collective-permute-done | bytes 245792 | tf_op jit(solution)/shard_map/ppermute | solution.py:52
  167.8 2.6 collective-permute-start.5
  170.3 33.6 %collective-permute-done.11 = bf16[480,256]{1,0:T(8,128)(2,1)S(1)} collective-permute-done((bf16[480,256]{1,0:T(8,128)(2,1)S(1)}, bf16[480,256]{1,0:T(8,128)(2,1)S(1)}, u32[]{:S(2)}, u32[]{:S(2)}) %collective-permute-start.11) | collective-permute-done | bytes 245792 | tf_op jit(solution)/shard_map/ppermute | solution.py:52
  204.1 1.5 collective-permute-start.13
  205.7 1.5 collective-permute-start.14
  210.1 18.6 %collective-permute-done.13.refs_1_ = bf16[4,480,256]{2,1,0:T(8,128)(2,1)S(1)} collective-permute-done((bf16[4,480,256]{2,1,0:T(8,128)(2,1)S(1)}, bf16[4,480,256]{2,1,0:T(8,128)(2,1)S(1)}, u32[]{:S(2)}, u32[]{:S(2)}) %collective-permute-start.13) | collective-permute-done | bytes 983072 | tf_op jit(solution)/shard_map/ppermute | solution.py:52
  228.8 1.0 fusion.9
  229.8 21.0 %collective-permute-done.14.refs_2_ = bf16[4,480,256]{2,1,0:T(8,128)(2,1)} collective-permute-done((bf16[4,480,256]{2,1,0:T(8,128)(2,1)S(1)}, bf16[4,480,256]{2,1,0:T(8,128)(2,1)}, u32[]{:S(2)}, u32[]{:S(2)}) %collective-permute-start.14) | collective-permute-done | bytes 983072 | tf_op jit(solution)/shard_map/ppermute | solution.py:52
  252.4 1.0 pad_maximum_fusion.6
  253.4 1.3 fusion.4.local_bias
  255.6 9.0 %project.1 = (bf16[512,1024]{1,0:T(8,128)(2,1)}, bf16[512,1024]{1,0:T(8,128)(2,1)}, bf16[512,1024]{1,0:T(8,128)(2,1)}, bf16[512,1024]{1,0:T(8,128)(2,1)}, bf16[5...) custom-call(bf16[512,1024]{1,0:T(8,128)(2,1)} %bitcast.118, ...), custom_call_target="tpu_custom_call" | custom-call | flops 3221225472 | bytes 16777216 | tf_op jit(solution)/shard_map/project/pallas_call | solution.py:174
  264.5 22.0 %attend.1 = (bf16[512,1024]{1,0:T(8,128)(2,1)}, bf16[8,512,512]{2,1,0:T(8,128)(2,1)}, bf16[8,512,1024]{2,1,0:T(8,128)(2,1)}) custom-call(bf16[512,1024]{1,0:T(8,128)(2,1)} %get-tuple-element.41.qmem, bf16[512,1024]{1,0:T(8,128)(2,1)} %get-tuple-element.42.qloc, bf16[512,1024]{1,0:T(8,128)(2,1)} %get-tuple-element.43.kloc, ...), custom_call_target="tpu_custom_call" | custom-call | flops 3221225472 | bytes 25165824 | tf_op jit(solution)/shard_map/attend/pallas_call | solution.py:223
  286.6 43.4 %feed.1 = (bf16[4,4,2,32,2816]{4,3,2,1,0:T(8,128)(2,1)}, bf16[4,4,2,32,2816]{4,3,2,1,0:T(8,128)(2,1)}, bf16[4,2816,256]{2,1,0:T(8,128)(2,1)}, bf16[4,1024,256]{2...) custom-call(bf16[512,1024]{1,0:T(8,128)(2,1)} %bitcast.119, ...), custom_call_target="tpu_custom_call" | custom-call | flops 26575110144 | bytes 50331648 | tf_op jit(solution)/shard_map/feed/pallas_call | solution.py:335
  330.3 9.5 %collective-permute-done.31 = bf16[4,4,2,32,2816]{4,3,2,1,0:T(8,128)(2,1)S(1)} collective-permute-done((bf16[4,4,2,32,2816]{4,3,2,1,0:T(8,128)(2,1)}, bf16[4,4,2,32,2816]{4,3,2,1,0:T(8,128)(2,1)S(1)}, u32[]{:S(2)}, u32[]{:S(2)}) %collective-permute-start.31) | collective-permute-done | bytes 5767200 | tf_op jit(solution)/shard_map/ppermute | solution.py:52
  339.7 7.2 %add_convert_fusion = bf16[4,4,2,32,2816]{4,3,2,1,0:T(8,128)(2,1)} fusion(bf16[4,4,2,32,2816]{4,3,2,1,0:T(8,128)(2,1)S(1)} %collective-permute-done.31, bf16[4,4,2,32,2816]{4,3,2,1,0:T(8,128)(2,1)} %get-tuple-element.64), kind=kLoop, calls=%fused_computation.3 | loop fusion | flops 11534336 | bytes 17301504 | tf_op jit(solution)/shard_map/convert_element_type | solution.py:525
  347.3 1.3 copy-done.7
  348.7 3.1 dynamic-slice_bitcast_fusion.1
  352.3 6.6 %collective-permute-done.30 = bf16[4,4,480,256]{3,2,1,0:T(8,128)(2,1)S(1)} collective-permute-done((bf16[4,4,480,256]{3,2,1,0:T(8,128)(2,1)S(1)}, bf16[4,4,480,256]{3,2,1,0:T(8,128)(2,1)S(1)}, u32[]{:S(2)}, u32[]{:S(2)}) %collective-permute-start.30) | collective-permute-done | bytes 3932192 | tf_op jit(solution)/shard_map/ppermute | solution.py:52
  358.9 2.5 add_convert_fusion.1
  361.4 16.3 %attend_back.1 = (bf16[512,1024]{1,0:T(8,128)(2,1)}, bf16[512,1024]{1,0:T(8,128)(2,1)}, bf16[512,1024]{1,0:T(8,128)(2,1)}) custom-call(bf16[8,512,512]{2,1,0:T(8,128)(2,1)} %get-tuple-element.53.p_loc, bf16[8,512,1024]{2,1,0:T(8,128)(2,1)} %get-tuple-element.54.p_mem, bf16[512,1024]{1,0:T(8,128)(2,1)} %get-tuple-element.55.datt, ...), custom_call_target="tpu_custom_call" | custom-call | flops 4294967296 | bytes 25165824 | tf_op jit(solution)/shard_map/attend_back/pallas_call | solution.py:404
  377.8 14.9 %project_back.1 = (bf16[4,4,112,1024]{3,2,1,0:T(8,128)(2,1)}, bf16[4,4,112,1024]{3,2,1,0:T(8,128)(2,1)}, f32[512,1024]{1,0:T(8,128)}, f32[2,1024]{1,0:T(2,128)}) custom-call(bf16[512,1024]{1,0:T(8,128)(2,1)} %bitcast.120, bf16[512,1024]{1,0:T(8,128)(2,1)} %get-tuple-element.50.normed_ref, f32[512,1024]{1,0:T(8,128)} %get-tuple-element.51.dmix_ref, ...), custom_call_target="tpu_custom_call" | custom-call | flops 6442450944 | bytes 25165824 | tf_op jit(solution)/shard_map/project_back/pallas_call | solution.py:499
  392.9 22.0 %reduce-scatter.15.cloned.1.call-done = bf16[1,4,2,32,2816]{4,3,2,1,0:T(8,128)(2,1)} async-done(((bf16[4,4,2,32,2816]{4,3,2,1,0:T(8,128)(2,1)}), bf16[1,4,2,32,2816]{4,3,2,1,0:T(8,128)(2,1)}) %reduce-scatter.15.cloned.1.call-update) | async-done | bytes 1441808
  414.9 1.5 pad_maximum_fusion.2
  416.4 4.6 all-to-all-start.1
  421.1 6.9 %add_convert_fusion.2 = bf16[4,4,112,1024]{3,2,1,0:T(8,128)(2,1)} fusion(bf16[4,4,112,1024]{3,2,1,0:T(8,128)(2,1)} %collective-permute-done.20, bf16[4,4,112,1024]{3,2,1,0:T(8,128)(2,1)} %get-tuple-element.60), kind=kLoop, calls=%fused_computation.5 | loop fusion | flops 7340032 | bytes 11010048 | tf_op jit(solution)/shard_map/convert_element_type | solution.py:525
  427.9 40.6 %reduce-scatter.13.cloned.1.call-done = bf16[1,4,480,256]{3,2,1,0:T(8,128)(2,1)} async-done(((bf16[4,4,480,256]{3,2,1,0:T(8,128)(2,1)}), bf16[1,4,480,256]{3,2,1,0:T(8,128)(2,1)}) %reduce-scatter.13.cloned.1.call-update) | async-done | bytes 983056
  468.8 2.0 slice_bitcast_fusion.5
  470.8 1.4 collective-permute-start.21
  472.9 1.5 collective-permute-start.23
  474.4 19.7 %collective-permute-done.21 = bf16[4,112,1024]{2,1,0:T(8,128)(2,1)S(1)} collective-permute-done((bf16[4,112,1024]{2,1,0:T(8,128)(2,1)S(1)}, bf16[4,112,1024]{2,1,0:T(8,128)(2,1)S(1)}, u32[]{:S(2)}, u32[]{:S(2)}) %collective-permute-start.21) | collective-permute-done | bytes 917536 | tf_op jit(solution)/shard_map/ppermute | solution.py:52
  494.1 19.6 %collective-permute-done.22 = bf16[4,112,1024]{2,1,0:T(8,128)(2,1)S(1)} collective-permute-done((bf16[4,112,1024]{2,1,0:T(8,128)(2,1)S(1)}, bf16[4,112,1024]{2,1,0:T(8,128)(2,1)S(1)}, u32[]{:S(2)}, u32[]{:S(2)}) %collective-permute-start.22) | collective-permute-done | bytes 917536 | tf_op jit(solution)/shard_map/ppermute | solution.py:52
  513.7 1.9 fusion.2
  515.7 0.9 copy-done.6
  516.7 1.5 collective-permute-start.24
  518.2 2.4 collective-permute-start.25
  521.2 16.6 %collective-permute-done.24 = bf16[112,1024]{1,0:T(8,128)(2,1)S(1)} collective-permute-done((bf16[112,1024]{1,0:T(8,128)(2,1)S(1)}, bf16[112,1024]{1,0:T(8,128)(2,1)S(1)}, u32[]{:S(2)}, u32[]{:S(2)}) %collective-permute-start.24) | collective-permute-done | bytes 229408 | tf_op jit(solution)/shard_map/ppermute | solution.py:52
  537.8 2.2 collective-permute-done.25
  540.0 5.5 collective-permute-done.26
  545.5 1.1 fusion.7
  546.6 1.5 collective-permute-start.27
  548.1 1.5 collective-permute-start.28
  550.1 1.6 slice_bitcast_fusion.1
  551.7 5.7 collective-permute-done.27
  557.4 4.9 collective-permute-done.28
  564.6 1.2 fusion.12
  565.8 18.1 %all_gather.10 = bf16[4,480,256]{2,1,0:T(8,128)(2,1)S(1)} all-gather(bf16[1,480,256]{2,1,0:T(8,128)(2,1)} %reduce-scatter.9.cloned.1.call-done), channel_id=1, replica_groups=mesh['dp'=4,'key'=8] {'dp'}, dimensions={0}, use_global_device_ids=true | all-gather | bytes 1228800 | tf_op jit(solution)/shard_map/all_gather | solution.py:539
  584.2 1.3 copy.62
  585.7 1.0 copy.57
  586.7 1.4 fusion.13
  588.1 1.2 bitcast_convert_fusion
  589.4 1.2 bitcast_convert_fusion.1
  (120 shorter events, 17.8 us)
Async XLA Ops:
  7.2 13.9 %copy-start = (bf16[352,1024]{1,0:T(8,128)(2,1)S(1)}, bf16[352,1024]{1,0:T(8,128)(2,1)}, u32[]{:S(2)}) copy-start(bf16[352,1024]{1,0:T(8,128)(2,1)} %param.30) | copy-start | bytes 2162692
  7.2 14.0 %copy-start.17 = (s32[8]{0:T(128)S(1)}, s32[8]{0:T(128)}, u32[]{:S(2)}) copy-start(s32[8]{0:T(128)} %param.21) | copy-start | bytes 100
  7.2 11.4 %copy-start.3 = (bf16[8,64,1024]{2,1,0:T(8,128)(2,1)S(1)}, bf16[8,64,1024]{2,1,0:T(8,128)(2,1)}, u32[]{:S(2)}) copy-start(bf16[8,64,1024]{2,1,0:T(8,128)(2,1)} %param.22) | copy-start | bytes 3145732
  7.2 279.4 %all-gather.3.cloned.1.call-start = ((), (), s32[]{:S(2)}) async-start(), calls=%async_computation.6 | async-start | bytes 11894784 | tf_op jit(solution)/shard_map/all_gather | solution.py:603
  12.3 13.4 %collective-permute-start = (bf16[400,256]{1,0:T(8,128)(2,1)}, bf16[400,256]{1,0:T(8,128)(2,1)S(1)}, u32[]{:S(2)}, u32[]{:S(2)}) collective-permute-start(bf16[400,256]{1,0:T(8,128)(2,1)} %get-tuple-element.138), channel_id=1, source_target_pairs={{0,2},{1,3},{2,0},{3,1},{4,6},{5,7},{6,4},{7,5},{8,10},{9,11},{10,... | collective-permute-start | bytes 614408 | tf_op jit(solution)/shard_map/ppermute | solution.py:52
  15.3 21.2 %collective-permute-start.1 = (bf16[400,256]{1,0:T(8,128)(2,1)}, bf16[400,256]{1,0:T(8,128)(2,1)S(1)}, u32[]{:S(2)}, u32[]{:S(2)}) collective-permute-start(bf16[400,256]{1,0:T(8,128)(2,1)} %get-tuple-element.138), channel_id=1, source_target_pairs={{0,4},{1,5},{2,6},{3,7},{4,0},{5,1},{6,2},{7,3},{8,12},{9,13},{10,... | collective-permute-start | bytes 614408 | tf_op jit(solution)/shard_map/ppermute | solution.py:52
  17.9 18.6 %collective-permute-start.2 = (bf16[400,256]{1,0:T(8,128)(2,1)}, bf16[400,256]{1,0:T(8,128)(2,1)}, u32[]{:S(2)}, u32[]{:S(2)}) collective-permute-start(bf16[400,256]{1,0:T(8,128)(2,1)} %get-tuple-element.138), channel_id=1, source_target_pairs={{0,6},{1,7},{2,4},{3,5},{4,2},{5,3},{6,0},{7,1},{8,14},{9,15},{10,... | collective-permute-start | bytes 614408 | tf_op jit(solution)/shard_map/ppermute | solution.py:52
  21.1 1.3 copy-start.4
  21.1 1.6 copy-start.5
  37.6 166.4 %copy-start.10 = (bf16[4,400,256]{2,1,0:T(8,128)(2,1)}, bf16[4,400,256]{2,1,0:T(8,128)(2,1)S(1)}, u32[]{:S(2)}) copy-start(bf16[4,400,256]{2,1,0:T(8,128)(2,1)S(1)} %pad_maximum_fusion.5.refs_0_) | copy-start | bytes 2457604
  37.6 171.3 %copy-start.11 = (s32[1,512]{1,0:T(1,128)S(1)}, s32[1,512]{1,0:T(1,128)}, u32[]{:S(2)}) copy-start(s32[1,512]{1,0:T(1,128)} %param.19) | copy-start | bytes 6148
  37.6 171.3 %copy-start.18 = (s32[8]{0:T(128)S(1)}, s32[8]{0:T(128)}, u32[]{:S(2)}) copy-start(s32[8]{0:T(128)} %param.20) | copy-start | bytes 100
  37.6 226.9 %all-to-all-start = ((bf16[8,256,1024]{2,1,0:T(8,128)(2,1)}), bf16[8,256,1024]{2,1,0:T(8,128)(2,1)}, u32[]{:S(2)}, u32[]{:S(2)}) async-start(bf16[8,256,1024]{2,1,0:T(8,128)(2,1)} %pad_maximum_fusion), calls=%async_computation | async-start | bytes 8388608 | tf_op jit(solution)/shard_map/all_to_all | solution.py:626
  48.1 366.8 %reduce-scatter.15.cloned.1.call-start = ((), (), s32[]{:S(2)}) async-start(), calls=%async_computation.11 | async-start | bytes 7208960
  48.1 119.6 %collective-permute-start.10 = (bf16[480,256]{1,0:T(8,128)(2,1)S(1)}, bf16[480,256]{1,0:T(8,128)(2,1)S(1)}, u32[]{:S(2)}, u32[]{:S(2)}) collective-permute-start(bf16[480,256]{1,0:T(8,128)(2,1)S(1)} %pad_maximum_fusion.8), channel_id=1, source_target_pairs={{0,2},{1,3},{2,0},{3,1},{4,6},{5,7},{6,4},{7,5},{8,10},{9,11},{10,... | collective-permute-start | bytes 737288 | tf_op jit(solution)/shard_map/ppermute | solution.py:52
  50.4 153.6 %collective-permute-start.11 = (bf16[480,256]{1,0:T(8,128)(2,1)S(1)}, bf16[480,256]{1,0:T(8,128)(2,1)S(1)}, u32[]{:S(2)}, u32[]{:S(2)}) collective-permute-start(bf16[480,256]{1,0:T(8,128)(2,1)S(1)} %pad_maximum_fusion.8), channel_id=1, source_target_pairs={{0,4},{1,5},{2,6},{3,7},{4,0},{5,1},{6,2},{7,3},{8,12},{9,13},{10,... | collective-permute-start | bytes 737288 | tf_op jit(solution)/shard_map/ppermute | solution.py:52
  52.5 153.2 %collective-permute-start.3 = (bf16[4,400,256]{2,1,0:T(8,128)(2,1)S(1)}, bf16[4,400,256]{2,1,0:T(8,128)(2,1)}, u32[]{:S(2)}, u32[]{:S(2)}) collective-permute-start(bf16[4,400,256]{2,1,0:T(8,128)(2,1)S(1)} %pad_maximum_fusion.5.refs_0_), channel_id=1, source_target_pairs={{0,8},{8,0},{16,24},{24,16},{1,9},{9,1},{17,25},{25,17},{2,10},{10... | collective-permute-start | bytes 2457608 | tf_op jit(solution)/shard_map/ppermute | solution.py:52
  54.0 153.2 %collective-permute-start.4 = (bf16[4,400,256]{2,1,0:T(8,128)(2,1)S(1)}, bf16[4,400,256]{2,1,0:T(8,128)(2,1)}, u32[]{:S(2)}, u32[]{:S(2)}) collective-permute-start(bf16[4,400,256]{2,1,0:T(8,128)(2,1)S(1)} %pad_maximum_fusion.5.refs_0_), channel_id=1, source_target_pairs={{0,16},{8,24},{16,0},{24,8},{1,17},{9,25},{17,1},{25,9},{2,18},{10... | collective-permute-start | bytes 2457608 | tf_op jit(solution)/shard_map/ppermute | solution.py:52
  55.5 148.5 %collective-permute-start.12 = (bf16[480,256]{1,0:T(8,128)(2,1)S(1)}, bf16[480,256]{1,0:T(8,128)(2,1)S(1)}, u32[]{:S(2)}, u32[]{:S(2)}) collective-permute-start(bf16[480,256]{1,0:T(8,128)(2,1)S(1)} %pad_maximum_fusion.8), channel_id=1, source_target_pairs={{0,6},{1,7},{2,4},{3,5},{4,2},{5,3},{6,0},{7,1},{8,14},{9,15},{10,... | collective-permute-start | bytes 737288 | tf_op jit(solution)/shard_map/ppermute | solution.py:52
  167.8 40.0 %collective-permute-start.5 = (bf16[4,400,256]{2,1,0:T(8,128)(2,1)S(1)}, bf16[4,400,256]{2,1,0:T(8,128)(2,1)S(1)}, u32[]{:S(2)}, u32[]{:S(2)}) collective-permute-start(bf16[4,400,256]{2,1,0:T(8,128)(2,1)S(1)} %pad_maximum_fusion.5.refs_0_), channel_id=1, source_target_pairs={{0,24},{8,16},{16,8},{24,0},{1,25},{9,17},{17,9},{25,1},{2,26},{10... | collective-permute-start | bytes 2457608 | tf_op jit(solution)/shard_map/ppermute | solution.py:52
  204.0 3.7 collective-permute-start.6
  204.1 60.4 %copy-start.9 = (bf16[4,480,256]{2,1,0:T(8,128)(2,1)}, bf16[4,480,256]{2,1,0:T(8,128)(2,1)S(1)}, u32[]{:S(2)}) copy-start(bf16[4,480,256]{2,1,0:T(8,128)(2,1)S(1)} %pad_maximum_fusion.3.refs_0_) | copy-start | bytes 2949124
  204.1 24.6 %collective-permute-start.13 = (bf16[4,480,256]{2,1,0:T(8,128)(2,1)S(1)}, bf16[4,480,256]{2,1,0:T(8,128)(2,1)S(1)}, u32[]{:S(2)}, u32[]{:S(2)}) collective-permute-start(bf16[4,480,256]{2,1,0:T(8,128)(2,1)S(1)} %pad_maximum_fusion.3.refs_0_), channel_id=1, source_target_pairs={{0,8},{8,0},{16,24},{24,16},{1,9},{9,1},{17,25},{25,17},{2,10},{10... | collective-permute-start | bytes 2949128 | tf_op jit(solution)/shard_map/ppermute | solution.py:52
  205.7 45.1 %collective-permute-start.14 = (bf16[4,480,256]{2,1,0:T(8,128)(2,1)S(1)}, bf16[4,480,256]{2,1,0:T(8,128)(2,1)}, u32[]{:S(2)}, u32[]{:S(2)}) collective-permute-start(bf16[4,480,256]{2,1,0:T(8,128)(2,1)S(1)} %pad_maximum_fusion.3.refs_0_), channel_id=1, source_target_pairs={{0,16},{8,24},{16,0},{24,8},{1,17},{9,25},{17,1},{25,9},{2,18},{10... | collective-permute-start | bytes 2949128 | tf_op jit(solution)/shard_map/ppermute | solution.py:52
  207.2 43.6 %collective-permute-start.15 = (bf16[4,480,256]{2,1,0:T(8,128)(2,1)S(1)}, bf16[4,480,256]{2,1,0:T(8,128)(2,1)}, u32[]{:S(2)}, u32[]{:S(2)}) collective-permute-start(bf16[4,480,256]{2,1,0:T(8,128)(2,1)S(1)} %pad_maximum_fusion.3.refs_0_), channel_id=1, source_target_pairs={{0,24},{8,16},{16,8},{24,0},{1,25},{9,17},{17,9},{25,1},{2,26},{10... | collective-permute-start | bytes 2949128 | tf_op jit(solution)/shard_map/ppermute | solution.py:52
  207.7 0.9 copy-start.13
  207.7 43.5 %collective-permute-start.7 = (bf16[4,400,256]{2,1,0:T(8,128)(2,1)}, bf16[4,400,256]{2,1,0:T(8,128)(2,1)}, u32[]{:S(2)}, u32[]{:S(2)}) collective-permute-start(bf16[4,400,256]{2,1,0:T(8,128)(2,1)} %collective-permute-done.3.refs_1_), channel_id=1, source_target_pairs={{0,1},{1,0},{2,3},{3,2},{4,5},{5,4},{6,7},{7,6},{8,9},{9,8},{10,11... | collective-permute-start | bytes 2457608 | tf_op jit(solution)/shard_map/ppermute | solution.py:52
  207.7 1.2 copy-start.14
  207.7 43.6 %collective-permute-start.8 = (bf16[4,400,256]{2,1,0:T(8,128)(2,1)}, bf16[4,400,256]{2,1,0:T(8,128)(2,1)S(1)}, u32[]{:S(2)}, u32[]{:S(2)}) collective-permute-start(bf16[4,400,256]{2,1,0:T(8,128)(2,1)} %collective-permute-done.4.refs_2_), channel_id=1, source_target_pairs={{0,1},{1,0},{2,3},{3,2},{4,5},{5,4},{6,7},{7,6},{8,9},{9,8},{10,11... | collective-permute-start | bytes 2457608 | tf_op jit(solution)/shard_map/ppermute | solution.py:52
  228.8 35.8 %copy-start.12 = (bf16[4,480,256]{2,1,0:T(8,128)(2,1)}, bf16[4,480,256]{2,1,0:T(8,128)(2,1)S(1)}, u32[]{:S(2)}) copy-start(bf16[4,480,256]{2,1,0:T(8,128)(2,1)S(1)} %collective-permute-done.13.refs_1_) | copy-start | bytes 2949124
  228.8 25.9 %collective-permute-start.9 = (bf16[4,400,256]{2,1,0:T(8,128)(2,1)}, bf16[4,400,256]{2,1,0:T(8,128)(2,1)S(1)}, u32[]{:S(2)}, u32[]{:S(2)}) collective-permute-start(bf16[4,400,256]{2,1,0:T(8,128)(2,1)} %copy-done.13), channel_id=1, source_target_pairs={{0,1},{1,0},{2,3},{3,2},{4,5},{5,4},{6,7},{7,6},{8,9},{9,8},{10,11... | collective-permute-start | bytes 2457608 | tf_op jit(solution)/shard_map/ppermute | solution.py:52
  250.7 35.8 %collective-permute-start.16 = (bf16[4,480,256]{2,1,0:T(8,128)(2,1)S(1)}, bf16[4,480,256]{2,1,0:T(8,128)(2,1)}, u32[]{:S(2)}, u32[]{:S(2)}) collective-permute-start(bf16[4,480,256]{2,1,0:T(8,128)(2,1)S(1)} %pad_maximum_fusion.3.refs_0_), channel_id=1, source_target_pairs={{0,1},{1,0},{2,3},{3,2},{4,5},{5,4},{6,7},{7,6},{8,9},{9,8},{10,11... | collective-permute-start | bytes 2949128 | tf_op jit(solution)/shard_map/ppermute | solution.py:52
  250.7 35.8 %collective-permute-start.17 = (bf16[4,480,256]{2,1,0:T(8,128)(2,1)S(1)}, bf16[4,480,256]{2,1,0:T(8,128)(2,1)}, u32[]{:S(2)}, u32[]{:S(2)}) collective-permute-start(bf16[4,480,256]{2,1,0:T(8,128)(2,1)S(1)} %collective-permute-done.13.refs_1_), channel_id=1, source_target_pairs={{0,1},{1,0},{2,3},{3,2},{4,5},{5,4},{6,7},{7,6},{8,9},{9,8},{10,11... | collective-permute-start | bytes 2949128 | tf_op jit(solution)/shard_map/ppermute | solution.py:52
  251.3 35.3 %collective-permute-start.18 = (bf16[4,480,256]{2,1,0:T(8,128)(2,1)}, bf16[4,480,256]{2,1,0:T(8,128)(2,1)}, u32[]{:S(2)}, u32[]{:S(2)}) collective-permute-start(bf16[4,480,256]{2,1,0:T(8,128)(2,1)} %collective-permute-done.14.refs_2_), channel_id=1, source_target_pairs={{0,1},{1,0},{2,3},{3,2},{4,5},{5,4},{6,7},{7,6},{8,9},{9,8},{10,11... | collective-permute-start | bytes 2949128 | tf_op jit(solution)/shard_map/ppermute | solution.py:52
  251.3 3.3 copy-start.15
  251.3 35.3 %collective-permute-start.19 = (bf16[4,480,256]{2,1,0:T(8,128)(2,1)}, bf16[4,480,256]{2,1,0:T(8,128)(2,1)}, u32[]{:S(2)}, u32[]{:S(2)}) collective-permute-start(bf16[4,480,256]{2,1,0:T(8,128)(2,1)} %collective-permute-done.15.refs_3_), channel_id=1, source_target_pairs={{0,1},{1,0},{2,3},{3,2},{4,5},{5,4},{6,7},{7,6},{8,9},{9,8},{10,11... | collective-permute-start | bytes 2949128 | tf_op jit(solution)/shard_map/ppermute | solution.py:52
  254.6 0.9 copy-start.16
  330.1 9.7 %collective-permute-start.31 = (bf16[4,4,2,32,2816]{4,3,2,1,0:T(8,128)(2,1)}, bf16[4,4,2,32,2816]{4,3,2,1,0:T(8,128)(2,1)S(1)}, u32[]{:S(2)}, u32[]{:S(2)}) collective-permute-start(bf16[4,4,2,32,2816]{4,3,2,1,0:T(8,128)(2,1)} %get-tuple-element.65), channel_id=1, source_target_pairs={{0,1},{1,0},{2,3},{3,2},{4,5},{5,4},{6,7},{7,6},{8,9},{9,8},{10,11... | collective-permute-start | bytes 17301512 | tf_op jit(solution)/shard_map/ppermute | solution.py:52
  347.0 1.6 copy-start.7
  347.0 121.5 %reduce-scatter.13.cloned.1.call-start = ((), (), s32[]{:S(2)}) async-start(), calls=%async_computation.10 | async-start | bytes 4915200
  352.1 6.8 %collective-permute-start.30 = (bf16[4,4,480,256]{3,2,1,0:T(8,128)(2,1)S(1)}, bf16[4,4,480,256]{3,2,1,0:T(8,128)(2,1)S(1)}, u32[]{:S(2)}, u32[]{:S(2)}) collective-permute-start(bf16[4,4,480,256]{3,2,1,0:T(8,128)(2,1)S(1)} %pad_maximum_fusion.1), channel_id=1, source_target_pairs={{0,1},{1,0},{2,3},{3,2},{4,5},{5,4},{6,7},{7,6},{8,9},{9,8},{10,11... | collective-permute-start | bytes 11796488 | tf_op jit(solution)/shard_map/ppermute | solution.py:52
  361.4 159.8 %reduce-scatter.11.cloned.1.call-start = ((), (), s32[]{:S(2)}) async-start(), calls=%async_computation.8 | async-start | bytes 1802240 | tf_op jit(solution)/shard_map/reduce_scatter | solution.py:536
  377.7 37.2 %copy-start.2 = (bf16[512,1024]{1,0:T(8,128)(2,1)S(1)}, bf16[512,1024]{1,0:T(8,128)(2,1)}, u32[]{:S(2)}) copy-start(bf16[512,1024]{1,0:T(8,128)(2,1)} %get-tuple-element.44.v) | copy-start | bytes 3145732
  377.7 37.2 %copy-start.8 = (bf16[512,1024]{1,0:T(8,128)(2,1)S(1)}, bf16[512,1024]{1,0:T(8,128)(2,1)}, u32[]{:S(2)}) copy-start(bf16[512,1024]{1,0:T(8,128)(2,1)} %get-tuple-element.66) | copy-start | bytes 3145732
  392.7 28.4 %collective-permute-start.20 = (bf16[4,4,112,1024]{3,2,1,0:T(8,128)(2,1)}, bf16[4,4,112,1024]{3,2,1,0:T(8,128)(2,1)}, u32[]{:S(2)}, u32[]{:S(2)}) collective-permute-start(bf16[4,4,112,1024]{3,2,1,0:T(8,128)(2,1)} %get-tuple-element.61), channel_id=1, source_target_pairs={{0,1},{1,0},{2,3},{3,2},{4,5},{5,4},{6,7},{7,6},{8,9},{9,8},{10,11... | collective-permute-start | bytes 11010056 | tf_op jit(solution)/shard_map/ppermute | solution.py:52
  416.4 133.7 %all-to-all-start.1 = ((bf16[8,2,64,1024]{3,2,1,0:T(8,128)(2,1)}), bf16[8,2,64,1024]{3,2,1,0:T(8,128)(2,1)S(1)}, u32[]{:S(2)}, u32[]{:S(2)}) async-start(bf16[8,2,64,1024]{3,2,1,0:T(8,128)(2,1)} %pad_maximum_fusion.2), calls=%async_computation.3 | async-start | bytes 4194304 | tf_op jit(solution)/shard_map/all_to_all | solution.py:634
  421.0 144.7 %reduce-scatter.9.cloned.1.call-start = ((), (), s32[]{:S(2)}) async-start(), calls=%async_computation.7 | async-start | bytes 1228800 | tf_op jit(solution)/shard_map/reduce_scatter | solution.py:536
  468.5 118.2 %all-gather.5.cloned.1.call-start = ((), (), s32[]{:S(2)}) async-start(), calls=%async_computation.9 | async-start | bytes 1802240 | tf_op jit(solution)/shard_map/all_gather | solution.py:539
  470.8 23.3 %collective-permute-start.21 = (bf16[4,112,1024]{2,1,0:T(8,128)(2,1)S(1)}, bf16[4,112,1024]{2,1,0:T(8,128)(2,1)S(1)}, u32[]{:S(2)}, u32[]{:S(2)}) collective-permute-start(bf16[4,112,1024]{2,1,0:T(8,128)(2,1)S(1)} %get-tuple-element.120), channel_id=1, source_target_pairs={{0,8},{8,0},{16,24},{24,16},{1,9},{9,1},{17,25},{25,17},{2,10},{10... | collective-permute-start | bytes 2752520 | tf_op jit(solution)/shard_map/ppermute | solution.py:52
  472.3 41.5 %collective-permute-start.22 = (bf16[4,112,1024]{2,1,0:T(8,128)(2,1)S(1)}, bf16[4,112,1024]{2,1,0:T(8,128)(2,1)S(1)}, u32[]{:S(2)}, u32[]{:S(2)}) collective-permute-start(bf16[4,112,1024]{2,1,0:T(8,128)(2,1)S(1)} %get-tuple-element.122), channel_id=1, source_target_pairs={{0,16},{8,24},{16,0},{24,8},{1,17},{9,25},{17,1},{25,9},{2,18},{10... | collective-permute-start | bytes 2752520 | tf_op jit(solution)/shard_map/ppermute | solution.py:52
  472.9 40.8 %collective-permute-start.23 = (bf16[4,112,1024]{2,1,0:T(8,128)(2,1)S(1)}, bf16[4,112,1024]{2,1,0:T(8,128)(2,1)S(1)}, u32[]{:S(2)}, u32[]{:S(2)}) collective-permute-start(bf16[4,112,1024]{2,1,0:T(8,128)(2,1)S(1)} %get-tuple-element.121), channel_id=1, source_target_pairs={{0,24},{8,16},{16,8},{24,0},{1,25},{9,17},{17,9},{25,1},{2,26},{10... | collective-permute-start | bytes 2752520 | tf_op jit(solution)/shard_map/ppermute | solution.py:52
  515.7 0.9 copy-start.6
  516.7 21.2 %collective-permute-start.24 = (bf16[112,1024]{1,0:T(8,128)(2,1)S(1)}, bf16[112,1024]{1,0:T(8,128)(2,1)S(1)}, u32[]{:S(2)}, u32[]{:S(2)}) collective-permute-start(bf16[112,1024]{1,0:T(8,128)(2,1)S(1)} %get-tuple-element.134), channel_id=1, source_target_pairs={{0,2},{1,3},{2,0},{3,1},{4,6},{5,7},{6,4},{7,5},{8,10},{9,11},{10,... | collective-permute-start | bytes 688136 | tf_op jit(solution)/shard_map/ppermute | solution.py:52
  518.2 21.8 %collective-permute-start.25 = (bf16[112,1024]{1,0:T(8,128)(2,1)S(1)}, bf16[112,1024]{1,0:T(8,128)(2,1)S(1)}, u32[]{:S(2)}, u32[]{:S(2)}) collective-permute-start(bf16[112,1024]{1,0:T(8,128)(2,1)S(1)} %get-tuple-element.136), channel_id=1, source_target_pairs={{0,4},{1,5},{2,6},{3,7},{4,0},{5,1},{6,2},{7,3},{8,12},{9,13},{10,... | collective-permute-start | bytes 688136 | tf_op jit(solution)/shard_map/ppermute | solution.py:52
  520.6 24.9 %collective-permute-start.26 = (bf16[112,1024]{1,0:T(8,128)(2,1)S(1)}, bf16[112,1024]{1,0:T(8,128)(2,1)S(1)}, u32[]{:S(2)}, u32[]{:S(2)}) collective-permute-start(bf16[112,1024]{1,0:T(8,128)(2,1)S(1)} %get-tuple-element.135), channel_id=1, source_target_pairs={{0,6},{1,7},{2,4},{3,5},{4,2},{5,3},{6,0},{7,1},{8,14},{9,15},{10,... | collective-permute-start | bytes 688136 | tf_op jit(solution)/shard_map/ppermute | solution.py:52
  546.6 10.9 %collective-permute-start.27 = (bf16[112,1024]{1,0:T(8,128)(2,1)S(1)}, bf16[112,1024]{1,0:T(8,128)(2,1)S(1)}, u32[]{:S(2)}, u32[]{:S(2)}) collective-permute-start(bf16[112,1024]{1,0:T(8,128)(2,1)S(1)} %fusion.7), channel_id=1, source_target_pairs={{0,8},{8,0},{16,24},{24,16},{1,9},{9,1},{17,25},{25,17},{2,10},{10... | collective-permute-start | bytes 688136 | tf_op jit(solution)/shard_map/ppermute | solution.py:52
  548.1 14.2 %collective-permute-start.28 = (bf16[112,1024]{1,0:T(8,128)(2,1)S(1)}, bf16[112,1024]{1,0:T(8,128)(2,1)S(1)}, u32[]{:S(2)}, u32[]{:S(2)}) collective-permute-start(bf16[112,1024]{1,0:T(8,128)(2,1)S(1)} %fusion.7), channel_id=1, source_target_pairs={{0,16},{8,24},{16,0},{24,8},{1,17},{9,25},{17,1},{25,9},{2,18},{10... | collective-permute-start | bytes 688136 | tf_op jit(solution)/shard_map/ppermute | solution.py:52
  549.6 13.6 %collective-permute-start.29 = (bf16[112,1024]{1,0:T(8,128)(2,1)S(1)}, bf16[112,1024]{1,0:T(8,128)(2,1)S(1)}, u32[]{:S(2)}, u32[]{:S(2)}) collective-permute-start(bf16[112,1024]{1,0:T(8,128)(2,1)S(1)} %fusion.7), channel_id=1, source_target_pairs={{0,24},{8,16},{16,8},{24,0},{1,25},{9,17},{17,9},{25,1},{2,26},{10... | collective-permute-start | bytes 688136 | tf_op jit(solution)/shard_map/ppermute | solution.py:52
  585.7 4.9 copy-start.1
Sparse Core Ops, SparseCore 0:
  11.5 177.7 all-gather.2
  347.1 67.7 reduce-scatter.14
  417.9 50.5 reduce-scatter.12
  470.7 33.2 reduce-scatter.10
  506.1 34.5 reduce-scatter.8
  542.6 39.1 all-gather.4

commit v2 on v1

v2 whole, which is shorter than its diff:
```python
import functools
import math

import jax
import jax.numpy as jnp
from jax import lax
from jax.experimental import pallas as pl
from jax.experimental.pallas import tpu as pltpu
from jax.sharding import PartitionSpec as P

H = 8
HD = 128
EPSILON = 1e-05
ROPE_BASE = 10000.0
NEG_FILL = -1e30
SCALE = 1.0 / math.sqrt(HD)
BF16 = jnp.bfloat16
F32 = jnp.float32
COLS = 256
GAIN_ROWS = 16
KEY = ("z", "core")
VMEM_LIMIT = 58 * 1024 * 1024


def dot(left, right):
    return jnp.dot(left, right, preferred_element_type=F32)


def dot_nt(left, right):
    return lax.dot_general(left, right, (((1,), (1,)), ((), ())), preferred_element_type=F32)


def dot_tn(left, right):
    return lax.dot_general(left, right, (((0,), (0,)), ((), ())), preferred_element_type=F32)


def inverse_rms(values):
    return lax.rsqrt(jnp.mean(values * values, axis=-1, keepdims=True) + EPSILON)


def turn(values, cosine, sine):
    return values * cosine + pltpu.roll(values, HD // 2, 1) * sine


def cost(flops):
    return pl.CostEstimate(flops=flops, bytes_accessed=24 * 2**20, transcendentals=0)


class Plan:
    def __init__(self, n_dp, n_key):
        self.n_dp, self.n_key = n_dp, n_key
        self.fast = n_dp == 4 and n_key == 8
        self.halves = 2 if self.fast else 1


def swap(values, axis, size, distance):
    return lax.ppermute(values, axis, [(i, i ^ distance) for i in range(size)])


def own_quarter(weight, n_dp):
    width = weight.shape[1] // n_dp
    return lax.dynamic_slice_in_dim(weight, lax.axis_index("dp") * width, width, 1)


def along_z(quarter):
    return [quarter] + [swap(quarter, KEY, 8, 2 * r) for r in (1, 2, 3)]


def across(held):
    x, y = swap(held, "dp", 4, 1), swap(held, "dp", 4, 2)
    return [held, x, y, swap(x[:2], "dp", 4, 2), swap(y[2:], "dp", 4, 1)]


def other_core(pieces):
    return [swap(piece, KEY, 8, 1) for piece in pieces]


def after(values, token):
    return lax.optimization_barrier((values, token))[0]


def place(plan, pieces, first_row, rows, target, sem):
    copies = []
    q, key = lax.axis_index("dp"), lax.axis_index(KEY)
    for core in range(2):
        own, x, y, far_low, far_high = pieces[core * 5 : core * 5 + 5]
        for far in range(4):
            for zr in range(4):
                if far < 3:
                    source = (own, x, y)[far].at[zr]
                else:
                    source = far_low.at[zr] if zr < 2 else far_high.at[zr - 2]
                row = pl.multiple_of((key ^ (2 * zr + core)) * rows, 16)
                column = pl.multiple_of((q ^ far) * COLS, COLS)
                copies.append(
                    pltpu.make_async_copy(
                        source.at[pl.ds(first_row, rows)],
                        target.at[pl.ds(row, rows), pl.ds(column, COLS)],
                        sem,
                    )
                )
    return copies


def place_rows(plan, held, target, sem):
    z = lax.axis_index("z")
    rows = held.shape[3]
    return [
        pltpu.make_async_copy(
            held.at[far, core, zr],
            target.at[
                pl.ds(pl.multiple_of((((z ^ zr) * 2 + core) * 4 + far) * rows, 16), rows)
            ],
            sem,
        )
        for core in range(2)
        for far in range(4)
        for zr in range(4)
    ]


def slot(far, zr):
    half = zr // 2
    return half, ((0, 1, 2, 3), (0, 2, 1, 3))[half][far], zr % 2


def store_turned(plan, values, flat, target, relative):
    if not plan.fast:
        target[...] = values.T.reshape(target.shape)
        return
    flat[...] = values.T
    q, key = lax.axis_index("dp"), lax.axis_index(KEY)
    z = lax.axis_index("z")
    rows = flat.shape[0] // 32
    for core in range(2):
        for far in range(4):
            for zr in range(4):
                if relative:
                    block = (key ^ (2 * zr + core)) * 4 + (q ^ far)
                    half, pos, low = slot(far, zr)
                    row = ((half * 4 + pos) * 2 + low) * rows
                    place_at = (core, slice(row, row + rows))
                else:
                    block = ((z ^ zr) * 2 + core) * 4 + far
                    row = ((far * 2 + core) * 4 + zr) * rows
                    place_at = slice(row, row + rows)
                target[place_at] = flat[pl.ds(pl.multiple_of(block * rows, rows), rows), :]


def project_kernel(plan, n_pieces, x_ref, cos_ref, sin_ref, *refs):
    pieces, refs = refs[:n_pieces], refs[n_pieces:]
    qmem_ref, qloc_ref, kloc_ref, kraw_ref, v_ref, normed_ref, gains_ref, w_ref, g_ref, sems = refs
    width = x_ref.shape[1]
    if plan.fast:
        rows = width // plan.n_key
        copies = []
        for m in range(3):
            copies += place(plan, pieces, GAIN_ROWS + m * rows, rows, w_ref.at[m], sems.at[0])
        key = lax.axis_index(KEY)
        for core in range(2):
            for zr in range(4):
                copies.append(
                    pltpu.make_async_copy(
                        pieces[core * 5].at[zr, pl.ds(0, GAIN_ROWS)],
                        g_ref.at[key ^ (2 * zr + core)],
                        sems.at[1],
                    )
                )
        for copy in copies:
            copy.start()
        pltpu.make_async_copy(g_ref, g_ref, sems.at[1]).wait()
        lead = [g_ref[k][0:1, :].astype(F32) for k in range(plan.n_key)]
        attn_gain = jnp.concatenate([row[:, :rows] for row in lead], axis=1)
        ffn_gain = jnp.concatenate([row[:, rows:] for row in lead], axis=1)
    else:
        copy = pltpu.make_async_copy(pieces[0], w_ref, sems.at[0])
        copy.start()
        attn_gain = pieces[1][0:1, :]
        ffn_gain = pieces[1][1:2, :]
    gains_ref[0:1, :] = attn_gain
    gains_ref[1:2, :] = ffn_gain
    x = x_ref[...].astype(F32)
    normed = (x * inverse_rms(x) * attn_gain).astype(BF16)
    normed_ref[...] = normed
    pltpu.make_async_copy(w_ref, w_ref, sems.at[0]).wait()
    cosine, sine = cos_ref[...], sin_ref[...]
    for m in range(3):
        for c in range(width // COLS):
            cols = slice(c * COLS, (c + 1) * COLS)
            raw = dot(normed, w_ref[m, :, cols])
            low = raw.astype(BF16)
            if m == 2:
                v_ref[:, cols] = low
                continue
            (qmem_ref if m == 0 else kraw_ref)[:, cols] = low
            out = qloc_ref if m == 0 else kloc_ref
            for h in range(COLS // HD):
                part = raw[:, h * HD : (h + 1) * HD]
                start = c * COLS + h * HD
                out[:, start : start + HD] = turn(part, cosine, sine).astype(BF16)


def project(plan, x, cosine, sine, pieces):
    tokens, width = x.shape
    whole = pl.BlockSpec(memory_space=pltpu.VMEM)
    anywhere = pl.BlockSpec(memory_space=pl.ANY)
    row = jax.ShapeDtypeStruct((tokens, width), BF16)
    return pl.pallas_call(
        functools.partial(project_kernel, plan, len(pieces)),
        out_shape=[row] * 6 + [jax.ShapeDtypeStruct((2, width), F32)],
        in_specs=[whole] * 3 + ([anywhere] * len(pieces) if plan.fast else [anywhere, whole]),
        out_specs=[whole] * 7,
        scratch_shapes=[
            pltpu.VMEM((3, width, width), BF16),
            pltpu.VMEM((plan.n_key, GAIN_ROWS, COLS), BF16),
            pltpu.SemaphoreType.DMA((2,)),
        ],
        compiler_params=pltpu.CompilerParams(vmem_limit_bytes=VMEM_LIMIT),
        cost_estimate=cost(6 * tokens * width * width),
        name="project",
    )(x, cosine, sine, *pieces)


def flat_rows(ref):
    block = ref[...]
    return block.reshape(block.shape[0] * block.shape[1], block.shape[2])


def weigh_kernel(qmem, qloc, kloc, mem_k, local_bias, memory_bias, p_loc, p_mem):
    s_loc = dot_nt(qloc[...], kloc[...]) * SCALE + local_bias[...]
    s_mem = dot_nt(qmem[...], flat_rows(mem_k)) * SCALE + memory_bias[...]
    largest = jnp.maximum(
        jnp.max(s_loc, axis=-1, keepdims=True), jnp.max(s_mem, axis=-1, keepdims=True)
    )
    e_loc = jnp.exp(s_loc - largest)
    e_mem = jnp.exp(s_mem - largest)
    total = jnp.sum(e_loc, axis=-1, keepdims=True) + jnp.sum(e_mem, axis=-1, keepdims=True)
    inverse = 1.0 / total
    p_loc[0] = (e_loc * inverse).astype(BF16)
    p_mem[0] = (e_mem * inverse).astype(BF16)


def head_spec(tokens):
    return pl.BlockSpec((tokens, HD), lambda h: (0, h))


def memory_spec(memory):
    return pl.BlockSpec(memory.shape[:2] + (HD,), lambda h: (0, 0, h))


def prob_specs(tokens, keys):
    return [
        pl.BlockSpec((1, tokens, tokens), lambda h: (h, 0, 0)),
        pl.BlockSpec((1, tokens, keys), lambda h: (h, 0, 0)),
    ]


def weigh(qmem, qloc, kloc, mem_k, local_bias, memory_bias):
    tokens, width = qmem.shape
    keys = memory_bias.shape[1]
    return pl.pallas_call(
        weigh_kernel,
        grid=(width // HD,),
        in_specs=[head_spec(tokens)] * 3
        + [
            memory_spec(mem_k),
            pl.BlockSpec((tokens, tokens), lambda h: (0, 0)),
            pl.BlockSpec((1, keys), lambda h: (0, 0)),
        ],
        out_specs=prob_specs(tokens, keys),
        out_shape=[
            jax.ShapeDtypeStruct((width // HD, tokens, tokens), BF16),
            jax.ShapeDtypeStruct((width // HD, tokens, keys), BF16),
        ],
        compiler_params=pltpu.CompilerParams(vmem_limit_bytes=VMEM_LIMIT),
        cost_estimate=cost(4 * tokens * (tokens + keys) * width),
        name="weigh",
    )(qmem, qloc, kloc, mem_k, local_bias, memory_bias)


def attend_kernel(p_loc, p_mem, v, mem_v, out):
    out[...] = (dot(p_loc[0], v[...]) + dot(p_mem[0], flat_rows(mem_v))).astype(BF16)


def attend(p_loc, p_mem, v, mem_v):
    tokens, width = v.shape
    keys = p_mem.shape[2]
    return pl.pallas_call(
        attend_kernel,
        grid=(width // HD,),
        in_specs=prob_specs(tokens, keys) + [head_spec(tokens), memory_spec(mem_v)],
        out_specs=head_spec(tokens),
        out_shape=jax.ShapeDtypeStruct((tokens, width), BF16),
        compiler_params=pltpu.CompilerParams(vmem_limit_bytes=VMEM_LIMIT),
        cost_estimate=cost(2 * tokens * (tokens + keys) * width),
        name="attend",
    )(p_loc, p_mem, v, mem_v)


def feed_kernel(plan, n_pieces, x_ref, att_ref, ct_ref, gains_ref, *refs):
    pieces, refs = refs[:n_pieces], refs[n_pieces:]
    n_half = plan.halves
    gu_ref, do_refs, refs = refs[0], refs[1 : 1 + n_half], refs[1 + n_half :]
    out_ref, dmix_ref, datt_ref = refs[:3]
    wo, wd, wgu, mixed, normed, flat, turned, acc_out, acc_back, g_down, g_out, sems = refs[3:]
    step = pl.program_id(0)
    tokens, width = x_ref.shape
    ff = wd.shape[0]
    gain = gains_ref[1:2, :]

    @pl.when(step == 0)
    def _():
        if plan.fast:
            rows = width // plan.n_key
            copies = place(plan, pieces, 0, rows, wo, sems.at[0])
            copies += place_rows(plan, pieces[-1], wgu, sems.at[1])
            copies += place(plan, pieces, rows, ff // plan.n_key, wd, sems.at[2])
        else:
            copies = [
                pltpu.make_async_copy(piece, held, sems.at[i])
                for i, (piece, held) in enumerate(zip(pieces, (wo, wgu, wd)))
            ]
        for copy in copies:
            copy.start()
        pltpu.make_async_copy(wo, wo, sems.at[0]).wait()
        mixed[...] = x_ref[...].astype(F32) + dot(att_ref[...], wo[...])
        value = mixed[...]
        low = (value * inverse_rms(value) * gain).astype(BF16)
        normed[...] = low
        store_turned(plan, low, flat, turned, False)
        acc_out[...] = jnp.zeros_like(acc_out)
        acc_back[...] = jnp.zeros_like(acc_back)
        pltpu.make_async_copy(wgu, wgu, sems.at[1]).wait()
        pltpu.make_async_copy(wd, wd, sems.at[2]).wait()

    ct = ct_ref[...]
    first = pl.multiple_of(step * COLS, COLS)
    down = wd[pl.ds(first, COLS), :]
    w_gate = wgu[:, pl.ds(first, COLS)]
    w_up = wgu[:, pl.ds(first + ff, COLS)]
    gate = dot(normed[...], w_gate)
    up = dot(normed[...], w_up)
    back = dot_nt(ct, down)
    sigma = 1.0 / (1.0 + jnp.exp(-gate))
    swish = gate * sigma
    hidden = (swish * up).astype(BF16)
    d_gate = (back * up * (sigma * (1.0 + gate * (1.0 - sigma)))).astype(BF16)
    d_up = (back * swish).astype(BF16)
    acc_out[...] += dot(hidden, down)
    acc_back[...] += dot_nt(d_gate, w_gate) + dot_nt(d_up, w_up)
    grad_down = dot_tn(hidden, ct).astype(BF16)
    for c in range(width // COLS):
        g_down[c, pl.ds(first, COLS), :] = grad_down[:, c * COLS : (c + 1) * COLS]
    lead = gu_ref.shape[:3]
    for i, grad in enumerate((d_gate, d_up)):
        value = dot(turned[...], grad).astype(BF16)
        gu_ref[:, :, :, i] = value.reshape(lead + (-1, COLS))

    @pl.when(step == pl.num_programs(0) - 1)
    def _():
        copies = []

        def send(source, offset):
            if not plan.fast:
                n = source.shape[1]
                for c in range(width // COLS):
                    copies.append(
                        pltpu.make_async_copy(
                            source.at[c], do_refs[0].at[c, pl.ds(offset, n)], sems.at[0]
                        )
                    )
            else:
                q, key = lax.axis_index("dp"), lax.axis_index(KEY)
                n = source.shape[1] // plan.n_key
                for core in range(2):
                    for far in range(4):
                        for zr in range(4):
                            row = pl.multiple_of((key ^ (2 * zr + core)) * n, 16)
                            copies.append(
                                pltpu.make_async_copy(
                                    source.at[q ^ far, pl.ds(row, n)],
                                    do_refs[core].at[slot(far, zr)].at[pl.ds(offset, n)],
                                    sems.at[0],
                                )
                            )

        send(g_down, 0)
        for copy in copies:
            copy.start()
        value = mixed[...]
        out_ref[...] = (value + acc_out[...]).astype(BF16)
        rf = inverse_rms(value)
        d_normed = acc_back[...]
        scaled = d_normed * gain
        d_mixed = (
            ct.astype(F32)
            + rf * scaled
            - value * (rf * rf * rf) * jnp.mean(scaled * value, axis=-1, keepdims=True)
        )
        dmix_ref[...] = d_mixed
        branch = d_mixed.astype(BF16)
        for c in range(width // COLS):
            g_out[c] = dot_tn(att_ref[...], branch[:, c * COLS : (c + 1) * COLS]).astype(BF16)
        started = len(copies)
        send(g_out, (ff if not plan.fast else ff // plan.n_key))
        for copy in copies[started:]:
            copy.start()
        datt_ref[...] = dot_nt(branch, wo[...]).astype(BF16)
        for copy in copies:
            copy.wait()


def feed(plan, x, attended, ct, gains, pieces, ff):
    tokens, width = x.shape
    steps = ff // COLS
    const = lambda *block: pl.BlockSpec(block, lambda j: (0,) * len(block))
    anywhere = pl.BlockSpec(memory_space=pl.ANY)
    if plan.fast:
        lead = (plan.n_dp, 2, plan.n_key // 2)
        rows = width // (plan.n_dp * plan.n_key)
        do_shape = (2, 4, 2, (ff + width) // plan.n_key, COLS)
    else:
        lead, rows = (1, 1, 1), width
        do_shape = (width // COLS, ff + width, COLS)
    return pl.pallas_call(
        functools.partial(feed_kernel, plan, len(pieces)),
        grid=(steps,),
        in_specs=[const(tokens, width)] * 3 + [const(2, width)] + [anywhere] * len(pieces),
        out_specs=[pl.BlockSpec(lead + (2, rows, COLS), lambda j: (0, 0, 0, 0, 0, j))]
        + [anywhere] * plan.halves
        + [const(tokens, width)] * 3,
        out_shape=[jax.ShapeDtypeStruct(lead + (2, rows, ff), BF16)]
        + [jax.ShapeDtypeStruct(do_shape, BF16)] * plan.halves
        + [
            jax.ShapeDtypeStruct((tokens, width), BF16),
            jax.ShapeDtypeStruct((tokens, width), F32),
            jax.ShapeDtypeStruct((tokens, width), BF16),
        ],
        scratch_shapes=[
            pltpu.VMEM((width, width), BF16),
            pltpu.VMEM((ff, width), BF16),
            pltpu.VMEM((width, 2 * ff), BF16),
            pltpu.VMEM((tokens, width), F32),
            pltpu.VMEM((tokens, width), BF16),
            pltpu.VMEM((width, tokens), BF16),
            pltpu.VMEM((width, tokens), BF16),
            pltpu.VMEM((tokens, width), F32),
            pltpu.VMEM((tokens, width), F32),
            pltpu.VMEM((width // COLS, ff, COLS), BF16),
            pltpu.VMEM((width // COLS, width, COLS), BF16),
            pltpu.SemaphoreType.DMA((3,)),
        ],
        compiler_params=pltpu.CompilerParams(vmem_limit_bytes=VMEM_LIMIT),
        cost_estimate=cost(18 * tokens * width * ff),
        name="feed",
    )(x, attended, ct, gains, *pieces)


def attend_back_kernel(
    p_loc, p_mem, datt, att, qloc, kloc, v, mem_k, mem_v, cos_ref, sin_ref, dq_ref, dk_ref, dv_ref
):
    grad = datt[...]
    delta = jnp.sum(grad.astype(F32) * att[...].astype(F32), axis=-1, keepdims=True)
    low_loc = p_loc[0]
    ds_loc = (low_loc.astype(F32) * (dot_nt(grad, v[...]) - delta)).astype(BF16)
    ds_mem = (p_mem[0].astype(F32) * (dot_nt(grad, flat_rows(mem_v)) - delta)).astype(BF16)
    cosine, sine = cos_ref[...], sin_ref[...]
    dq_loc = dot(ds_loc, kloc[...]) * SCALE
    dq_mem = dot(ds_mem, flat_rows(mem_k)) * SCALE
    dk = dot_tn(ds_loc, qloc[...]) * SCALE
    dq_ref[...] = (dq_mem + turn(dq_loc, cosine, -sine)).astype(BF16)
    dk_ref[...] = turn(dk, cosine, -sine).astype(BF16)
    dv_ref[...] = dot_tn(low_loc, grad).astype(BF16)


def attend_back(p_loc, p_mem, datt, att, qloc, kloc, v, mem_k, mem_v, cosine, sine):
    tokens, width = datt.shape
    keys = p_mem.shape[2]
    table = pl.BlockSpec((tokens, HD), lambda h: (0, 0))
    return pl.pallas_call(
        attend_back_kernel,
        grid=(width // HD,),
        in_specs=prob_specs(tokens, keys)
        + [head_spec(tokens)] * 5
        + [memory_spec(mem_k), memory_spec(mem_v), table, table],
        out_specs=[head_spec(tokens)] * 3,
        out_shape=[jax.ShapeDtypeStruct((tokens, width), BF16)] * 3,
        compiler_params=pltpu.CompilerParams(vmem_limit_bytes=VMEM_LIMIT),
        cost_estimate=cost(4 * tokens * (2 * tokens + keys) * width),
        name="attend_back",
    )(p_loc, p_mem, datt, att, qloc, kloc, v, mem_k, mem_v, cosine, sine)


def project_grads_kernel(plan, normed_ref, dq, dk, dv, *refs):
    n_half = plan.halves
    g_refs, (flat, turned) = refs[:n_half], refs[n_half:]
    width = normed_ref.shape[1]
    store_turned(plan, normed_ref[...], flat, turned, True)
    low = (dq, dk, dv)
    for half in range(n_half):
        each = g_refs[half].shape[-2] // 3
        lead = g_refs[half].shape[:-2]
        for m in range(3):
            for c in range(width // COLS):
                cols = slice(c * COLS, (c + 1) * COLS)
                value = dot(turned[half], low[m][:, cols]).astype(BF16)
                g_refs[half][..., m * each : (m + 1) * each, cols] = value.reshape(
                    lead + (each, COLS)
                )


def project_grads(plan, normed, dq, dk, dv):
    tokens, width = normed.shape
    whole = pl.BlockSpec(memory_space=pltpu.VMEM)
    if plan.fast:
        lead, rows = (2, 4, 2), width // (plan.n_dp * plan.n_key)
    else:
        lead, rows = (1, 1), width
    return pl.pallas_call(
        functools.partial(project_grads_kernel, plan),
        in_specs=[whole] * 4,
        out_specs=[whole] * plan.halves,
        out_shape=[jax.ShapeDtypeStruct(lead + (3 * rows, width), BF16)] * plan.halves,
        scratch_shapes=[
            pltpu.VMEM((width, tokens), BF16),
            pltpu.VMEM((plan.halves, width // plan.halves, tokens), BF16),
        ],
        compiler_params=pltpu.CompilerParams(vmem_limit_bytes=VMEM_LIMIT),
        cost_estimate=cost(2**20),
        name="project_grads",
    )(normed, dq, dk, dv)


def project_back_kernel(plan, n_pieces, x_ref, dmix_ref, gains_ref, dq, dk, dv, *refs):
    pieces, refs = refs[:n_pieces], refs[n_pieces:]
    xgrad_ref, w_ref, sems = refs
    if plan.fast:
        rows = x_ref.shape[1] // plan.n_key
        for m in range(3):
            for copy in place(plan, pieces, GAIN_ROWS + m * rows, rows, w_ref.at[m], sems.at[0]):
                copy.start()
    else:
        pltpu.make_async_copy(pieces[0], w_ref, sems.at[0]).start()
    x = x_ref[...].astype(F32)
    ra = inverse_rms(x)
    pltpu.make_async_copy(w_ref, w_ref, sems.at[0]).wait()
    d_normed = dot_nt(dq[...], w_ref[0]) + dot_nt(dk[...], w_ref[1]) + dot_nt(dv[...], w_ref[2])
    scaled = d_normed * gains_ref[0:1, :]
    xgrad_ref[...] = (
        dmix_ref[...]
        + ra * scaled
        - x * (ra * ra * ra) * jnp.mean(scaled * x, axis=-1, keepdims=True)
    )


def project_back(plan, x, dmix, gains, dq, dk, dv, pieces):
    tokens, width = x.shape
    whole = pl.BlockSpec(memory_space=pltpu.VMEM)
    return pl.pallas_call(
        functools.partial(project_back_kernel, plan, len(pieces)),
        in_specs=[whole] * 6 + [pl.BlockSpec(memory_space=pl.ANY)] * len(pieces),
        out_specs=whole,
        out_shape=jax.ShapeDtypeStruct((tokens, width), F32),
        scratch_shapes=[pltpu.VMEM((3, width, width), BF16), pltpu.SemaphoreType.DMA((1,))],
        compiler_params=pltpu.CompilerParams(vmem_limit_bytes=VMEM_LIMIT),
        cost_estimate=cost(2**20),
        name="project_back",
    )(x, dmix, gains, dq, dk, dv, *pieces)


def add(*parts):
    total = parts[0].astype(F32)
    for part in parts[1:]:
        total = total + part.astype(F32)
    return total.astype(BF16)


def both_cores(own, other):
    return add(own, swap(other, KEY, 8, 1))


def over_dp_first(share, token=None):
    from_y = swap(share[0, 2:], "dp", 4, 2)
    from_x = swap(share[1, 2:], "dp", 4, 1)
    if token is not None:
        from_y, from_x = after((from_y, from_x), token)
    mine = share[0, 0], from_y[0], share[1, 0], from_x[0]
    return mine, (add(share[0, 1], from_y[1]), add(share[1, 1], from_x[1]))


def over_dp_second(mine, passed, token):
    low, high = swap(passed[0], "dp", 4, 1), swap(passed[1], "dp", 4, 2)
    low, high = after((low, high), token)
    low, high = add(*mine[:2], low), add(*mine[2:], high)
    return [low[0], low[1], high[0], high[1]]


def over_z(parts, token=None):
    come = [swap(parts[r], KEY, 8, 2 * r) for r in (1, 2, 3)]
    if token is not None:
        come = after(come, token)
    return add(parts[0], *come)


def from_dp(share):
    held = jnp.stack([share] + [swap(share, "dp", 4, r) for r in (1, 2, 3)])
    return jnp.take(held, jnp.arange(4) ^ lax.axis_index("dp"), axis=0)


def per_device(
    plan,
    inputs,
    positions,
    memory_flag,
    partner,
    cache_keys,
    cache_values,
    query_proj,
    key_proj,
    value_proj,
    out_proj,
    gate_proj,
    up_proj,
    down_proj,
    attn_gain,
    ffn_gain,
    cotangent,
):
    x, ct, token_pos = inputs[0], cotangent[0], positions[0]
    tokens, width = x.shape
    group, slots = cache_keys.shape[0], cache_keys.shape[1]
    key = lax.axis_index(KEY)
    n_dp = plan.n_dp

    half = HD // 2
    frequency = ROPE_BASE ** (-2.0 * jnp.arange(half, dtype=F32) / HD)
    angles = token_pos.astype(F32)[:, None] * frequency[None, :]
    cosine, sine = jnp.cos(angles), jnp.sin(angles)
    cosine = jnp.concatenate([cosine, cosine], axis=1)
    sine = jnp.concatenate([-sine, sine], axis=1)
    order = jnp.arange(tokens, dtype=jnp.int32)
    valid = (order[None, :] <= order[:, None]) & (
        token_pos[:, None] - token_pos[None, :] == order[:, None] - order[None, :]
    )
    local_bias = jnp.where(valid, 0.0, NEG_FILL).astype(F32)
    self_flag = jnp.take(memory_flag, key)
    place_in_slot = jnp.arange(group * 2 * slots, dtype=jnp.int32) % (2 * slots)
    memory_bias = jnp.where((place_in_slot >= slots) | (self_flag == 1), 0.0, NEG_FILL)
    memory_bias = memory_bias.astype(F32)[None, :]

    out_k, out_v = (
        jnp.concatenate([cache, jnp.take(cache, partner, axis=0)], axis=1)
        for cache in (cache_keys, cache_values)
    )
    rows = width // plan.n_key
    if plan.fast:
        gains = jnp.concatenate([attn_gain, ffn_gain])[None, :]
        project_in = jnp.concatenate(
            [jnp.broadcast_to(gains, (GAIN_ROWS, COLS))]
            + [own_quarter(w, n_dp) for w in (query_proj, key_proj, value_proj)],
            axis=0,
        )
        project_out = jnp.concatenate([own_quarter(w, n_dp) for w in (out_proj, down_proj)], axis=0)
        share = rows // n_dp
        gate_up = jnp.concatenate(
            [
                lax.dynamic_slice_in_dim(w, lax.axis_index("dp") * share, share, 0)
                for w in (gate_proj, up_proj)
            ],
            axis=1,
        )
        gate_up = along_z(gate_up)
        gate_up = after(gate_up, (project_in, project_out, out_k, out_v))
        project_in = along_z(after(project_in, gate_up))
        project_out = along_z(after(project_out, project_in))
        out_k = after(out_k, project_out)
        gate_up = lax.all_gather(jnp.stack(gate_up), ("dp", "core"), axis=0, tiled=False)
        gate_up = gate_up.reshape((n_dp, 2) + gate_up.shape[1:])
        project_in = across(jnp.stack(project_in))
        project_out = across(jnp.stack(after(project_out, project_in)))
        out_v = after(out_v, project_in)
        first = project_in + other_core(project_in)
        second = project_out + other_core(project_out) + [gate_up]
    else:
        whole = lambda w: lax.all_gather(w, KEY, axis=0, tiled=True)
        first = [
            jnp.stack([whole(query_proj), whole(key_proj), whole(value_proj)]),
            jnp.stack([whole(attn_gain), whole(ffn_gain)]).astype(F32),
        ]
        second = [
            whole(out_proj),
            whole(jnp.concatenate([gate_proj, up_proj], axis=1)),
            whole(down_proj),
        ]
    mem_k = lax.all_to_all(out_k, KEY, split_axis=0, concat_axis=0, tiled=True)
    out_v = after(out_v, mem_k)
    mem_v = lax.all_to_all(out_v, KEY, split_axis=0, concat_axis=0, tiled=True)

    qmem, qloc, kloc, kraw, v, normed, gains = project(plan, x, cosine, sine, first)
    p_loc, p_mem = weigh(qmem, qloc, kloc, mem_k, local_bias, memory_bias)
    attended = attend(p_loc, p_mem, v, mem_v)

    run = tokens // group
    fresh = jnp.stack([kraw.reshape(group, run, width), v.reshape(group, run, width)], axis=1)
    fresh = after(fresh, attended)
    arrived = lax.all_to_all(fresh, KEY, split_axis=0, concat_axis=0, tiled=True)
    new_keys = jnp.concatenate([cache_keys[:, run:], arrived[:, 0]], axis=1)
    new_values = jnp.concatenate([cache_values[:, run:], arrived[:, 1]], axis=1)

    n_half, ff = plan.halves, gate_proj.shape[1]
    results = feed(plan, x, attended, ct, gains, second, ff)
    g_gu, g_do, (outputs, dmix, datt) = (
        results[0],
        results[1 : 1 + n_half],
        results[1 + n_half :],
    )
    if plan.fast:
        g_gu = g_gu.reshape((8,) + g_gu.shape[2:])
        g_gu = lax.psum_scatter(g_gu, ("dp", "core"), scatter_dimension=0, tiled=True)
        g_gu = lax.optimization_barrier(g_gu)
    if plan.fast:
        g_do = both_cores(*g_do)
        datt = after(datt, g_do)
    dq, dk, dv = attend_back(
        p_loc, p_mem, datt, attended, qloc, kloc, v, mem_k, mem_v, cosine, sine
    )
    if plan.fast:
        do_mine, do_passed = over_dp_first(g_do, dq)
        dq = after(dq, do_passed)
    g_qkv = project_grads(plan, normed, dq, dk, dv)
    dq = after(dq, g_qkv)
    if plan.fast:
        do_blocks = over_dp_second(do_mine, do_passed, g_qkv)
        dq = after(dq, do_blocks)
    input_grad = project_back(
        plan, x, dmix, gains, dq, dk, dv, first if plan.fast else first[:1]
    )

    if plan.fast:
        own, swapped = g_qkv[0], swap(g_qkv[1], KEY, 8, 1)
        g_qkv = add(*after((own, swapped), (input_grad, arrived)))
        g_do = over_z(do_blocks, g_qkv)
        g_gu = after(g_gu, g_do)[0]
        mine, passed = over_dp_first(g_qkv, g_gu)
        g_gu = over_z(g_gu, passed)
        blocks = over_dp_second(mine, passed, g_gu)
        g_do = from_dp(g_do)
        g_qkv = over_z(blocks)
        g_gu = from_dp(g_gu)
        g_qkv = from_dp(g_qkv).astype(F32)
        g_do = g_do.transpose(1, 0, 2).reshape(-1, width).astype(F32)
        total_down, total_out = g_do[:-rows], g_do[-rows:]
        total_gate = g_gu[:, 0].reshape(rows, -1).astype(F32)
        total_up = g_gu[:, 1].reshape(rows, -1).astype(F32)
        each = rows // n_dp
        total_query, total_key, total_value = (
            g_qkv[:, m * each : (m + 1) * each].reshape(rows, width) for m in range(3)
        )
    else:

        def total(g):
            g = lax.psum_scatter(g.astype(F32), KEY, scatter_dimension=0, tiled=True)
            return lax.psum(g.astype(BF16), "dp").astype(F32)

        wide = lambda g: g.transpose(1, 0, 2).reshape(g.shape[1], width)
        total_query, total_key, total_value = (
            total(g_qkv[0][0, 0, m * width : (m + 1) * width]) for m in range(3)
        )
        total_gate, total_up = total(g_gu[0, 0, 0, 0]), total(g_gu[0, 0, 0, 1])
        total_down, total_out = total(wide(g_do[0][:, :ff])), total(wide(g_do[0][:, ff:]))

    def of_gain(gain, *pairs):
        terms = sum(jnp.sum(w.astype(F32) * g, axis=1) for w, g in pairs)
        return terms / gain.astype(F32)

    total_attn = of_gain(
        attn_gain, (query_proj, total_query), (key_proj, total_key), (value_proj, total_value)
    )
    total_ffn = of_gain(ffn_gain, (gate_proj, total_gate), (up_proj, total_up))
    return (
        outputs[None],
        input_grad[None],
        total_query,
        total_key,
        total_value,
        total_out,
        total_gate,
        total_up,
        total_down,
        total_attn,
        total_ffn,
        new_keys,
        new_values,
    )


def solution(mesh):
    n_dp, n_key = mesh.shape["dp"], mesh.shape["key"]
    plan = Plan(n_dp, n_key)
    fine = jax.sharding.Mesh(mesh.devices.reshape(n_dp, n_key // 2, 2), ("dp",) + KEY)
    rows, cache = P(("dp",) + KEY, None, None), P("dp", KEY, None)
    weight, gain = P(KEY, None), P(KEY)
    return jax.shard_map(
        functools.partial(per_device, plan),
        mesh=fine,
        in_specs=(rows, P(("dp",) + KEY, None), P("dp"), P("dp"), cache, cache)
        + (weight,) * 7
        + (gain, gain, rows),
        out_specs=(rows, rows) + (weight,) * 7 + (gain, gain, cache, cache),
        check_vma=False,
    )
```

time: 599 us -> 491 us (0.82); the launches traced: 597 us -> 482 us
  waiting for transfers between devices: 350 us -> 195 us
  starting transfers between devices: 49 us -> 85.2 us
  blocking collectives: 18.1 us -> 0 us
  Pallas kernels: 106 us -> 114 us
  other arithmetic: 35.7 us -> 43.3 us
    ppermute x32 -> x55, waiting for transfers between devices: 287 us -> 195 us  [swap(): return lax.ppermute(values, axis, [(i, i ^ distance) for i in range(size)])]
    unnamed x8 -> x2, waiting for transfers between devices: 62.6 us -> 0.03 us
    ppermute x32 -> x55, starting transfers between devices: 33.3 us -> 70.6 us  [swap(): return lax.ppermute(values, axis, [(i, i ^ distance) for i in range(size)])]
    all_gather x1 -> x0, blocking collectives: 18.1 us -> none  [offloaded_sum(): return lax.all_gather(share, 'dp', axis=0)]
    pallas_call x2 -> x4, Pallas kernels: 38.3 us -> 49.3 us  [the longest x1 16.4 us: attend_back(): pl.pallas_call(attend_back_kernel, grid=(width // HD,), in_specs=prob_spe...]
    another operation x4 -> x6, other arithmetic: 1.99 us -> 8.49 us  [the longest x3 3.59 us: from_dp(): held = jnp.stack([share] + [swap(share, 'dp', 4, r) for r in (1, 2, 3)])]
    convert_element_type x5 -> x9, other arithmetic: 19.6 us -> 20.6 us  [add(): return total.astype(BF16)]
    all_to_all x2 -> x3, starting transfers between devices: 15 us -> 14.5 us  [the longest x1 5.33 us: per_device(): mem_k = lax.all_to_all(out_k, KEY, split_axis=0, concat_axis=0, tiled=True)]
  transfers between devices with their start and end apart: 40 -> 60, of which waited for: 17 -> 27; matrix products, arithmetic and copies ran while one was open for 7% -> 12% of each run, Pallas kernels for 10% -> 14%
where the time goes in v2:
time: 491 us; the launch traced here: 482 us
  waiting for transfers between devices  195 us (40%)
  Pallas kernels  114 us (23%)
  starting transfers between devices  85.2 us (17%)
  other arithmetic  43.3 us (9%)
  local copies, waits for them, and re-layouts  28.7 us (6%)
  between operations  15.9 us (3%)
    ppermute x55, waiting for transfers between devices, swap(): return lax.ppermute(values, axis, [(i, i ^ distance) for i in range(size)])  195 us
    ppermute x55, starting transfers between devices, swap(): return lax.ppermute(values, axis, [(i, i ^ distance) for i in range(size)])  70.6 us
    pallas_call x1, Pallas kernels, feed(): pl.pallas_call(functools.partial(feed_kernel, plan, len(pieces)), grid=(s...  45.2 us
    convert_element_type x9, other arithmetic, add(): return total.astype(BF16)  20.6 us
    pallas_call x1, Pallas kernels, attend_back(): pl.pallas_call(attend_back_kernel, grid=(width // HD,), in_specs=prob_spe...  16.4 us
    pallas_call x1, Pallas kernels, weigh(): pl.pallas_call(weigh_kernel, grid=(width // HD,), in_specs=[head_spec(tok...  14.3 us
    pallas_call x1, Pallas kernels, project_back(): pl.pallas_call(functools.partial(project_back_kernel, plan, len(pieces)),...  10.8 us
    unnamed x92, local copies, waits for them, and re-layouts  10.1 us
  transfers between devices with their start and end apart: 60, of which 27 were waited for; matrix products, arithmetic and copies ran while one was open for 12% of the time, Pallas kernels for 14%

profile of v2, /device:TPU:0, one launch (start us, length us, event | category | flops | bytes accessed | tf_op | source)
XLA Modules:
  0.0 482.2 jit_solution(3951813160055636442)
XLA Ops:
  8.4 3.1 collective-permute-start
  11.5 2.6 collective-permute-start.1
  16.1 1.8 gather_fusion.4
  21.4 2.4 pad_maximum_fusion
  23.8 3.2 collective-permute-done
  27.0 12.3 %collective-permute-done.1 = bf16[32,5632]{1,0:T(8,128)(2,1)} collective-permute-done((bf16[32,5632]{1,0:T(8,128)(2,1)S(1)}, bf16[32,5632]{1,0:T(8,128)(2,1)}, u32[]{:S(2)}, u32[]{:S(2)}) %collective-permute-start.1) | collective-permute-done | bytes 360480 | tf_op jit(solution)/shard_map/ppermute | solution.py:57
  39.3 2.5 pad_maximum_fusion.3
  41.8 6.9 %collective-permute-start.3 = (bf16[400,256]{1,0:T(8,128)(2,1)S(1)}, bf16[400,256]{1,0:T(8,128)(2,1)S(1)}, u32[]{:S(2)}, u32[]{:S(2)}) collective-permute-start(bf16[400,256]{1,0:T(8,128)(2,1)S(1)} %pad_maximum_fusion.13), channel_id=1, source_target_pairs={{0,2},{1,3},{2,0},{3,1},{4,6},{5,7},{6,4},{7,5},{8,10},{9,11},{10,... | collective-permute-start | bytes 614408 | tf_op jit(solution)/shard_map/ppermute | solution.py:57
  51.2 4.1 collective-permute-done.3
  55.4 10.7 %collective-permute-done.4 = bf16[400,256]{1,0:T(8,128)(2,1)S(1)} collective-permute-done((bf16[400,256]{1,0:T(8,128)(2,1)S(1)}, bf16[400,256]{1,0:T(8,128)(2,1)S(1)}, u32[]{:S(2)}, u32[]{:S(2)}) %collective-permute-start.4) | collective-permute-done | bytes 204832 | tf_op jit(solution)/shard_map/ppermute | solution.py:57
  66.1 2.8 collective-permute-start.15
  69.8 1.5 collective-permute-start.17
  71.3 5.0 %collective-permute-done.15 = bf16[480,256]{1,0:T(8,128)(2,1)S(1)} collective-permute-done((bf16[480,256]{1,0:T(8,128)(2,1)S(1)}, bf16[480,256]{1,0:T(8,128)(2,1)S(1)}, u32[]{:S(2)}, u32[]{:S(2)}) %collective-permute-start.15) | collective-permute-done | bytes 245792 | tf_op jit(solution)/shard_map/ppermute | solution.py:57
  76.3 12.2 %collective-permute-done.16 = bf16[480,256]{1,0:T(8,128)(2,1)S(1)} collective-permute-done((bf16[480,256]{1,0:T(8,128)(2,1)S(1)}, bf16[480,256]{1,0:T(8,128)(2,1)S(1)}, u32[]{:S(2)}, u32[]{:S(2)}) %collective-permute-start.16) | collective-permute-done | bytes 245792 | tf_op jit(solution)/shard_map/ppermute | solution.py:57
  89.2 5.3 %all-to-all-start = ((bf16[8,128,1024]{2,1,0:T(8,128)(2,1)}), bf16[8,128,1024]{2,1,0:T(8,128)(2,1)S(1)}, u32[]{:S(2)}, u32[]{:S(2)}) async-start(bf16[8,128,1024]{2,1,0:T(8,128)(2,1)} %get-tuple-element.78), calls=%async_computation | async-start | bytes 4194304 | tf_op jit(solution)/shard_map/all_to_all | solution.py:695
  95.8 1.6 collective-permute-start.6
  97.4 1.5 collective-permute-start.7
  98.9 31.7 %collective-permute-done.6.refs_1_ = bf16[4,400,256]{2,1,0:T(8,128)(2,1)S(1)} collective-permute-done((bf16[4,400,256]{2,1,0:T(8,128)(2,1)S(1)}, bf16[4,400,256]{2,1,0:T(8,128)(2,1)S(1)}, u32[]{:S(2)}, u32[]{:S(2)}) %collective-permute-start.6) | collective-permute-done | bytes 819232 | tf_op jit(solution)/shard_map/ppermute | solution.py:57
  130.6 1.5 collective-permute-start.8
  132.8 9.2 %collective-permute-done.8.refs_3_ = bf16[2,400,256]{2,1,0:T(8,128)(2,1)S(1)} collective-permute-done((bf16[2,400,256]{2,1,0:T(8,128)(2,1)S(1)}, bf16[2,400,256]{2,1,0:T(8,128)(2,1)S(1)}, u32[]{:S(2)}, u32[]{:S(2)}) %collective-permute-start.8) | collective-permute-done | bytes 409632 | tf_op jit(solution)/shard_map/ppermute | solution.py:57
  144.9 4.3 all-to-all-start.1
  151.4 1.5 collective-permute-start.19
  153.4 21.3 %collective-permute-done.18.refs_1_ = bf16[4,480,256]{2,1,0:T(8,128)(2,1)S(1)} collective-permute-done((bf16[4,480,256]{2,1,0:T(8,128)(2,1)S(1)}, bf16[4,480,256]{2,1,0:T(8,128)(2,1)S(1)}, u32[]{:S(2)}, u32[]{:S(2)}) %collective-permute-start.18) | collective-permute-done | bytes 983072 | tf_op jit(solution)/shard_map/ppermute | solution.py:57
  184.2 5.5 %collective-permute-done.20.refs_3_ = bf16[2,480,256]{2,1,0:T(8,128)(2,1)} collective-permute-done((bf16[2,480,256]{2,1,0:T(8,128)(2,1)S(1)}, bf16[2,480,256]{2,1,0:T(8,128)(2,1)}, u32[]{:S(2)}, u32[]{:S(2)}) %collective-permute-start.20) | collective-permute-done | bytes 491552 | tf_op jit(solution)/shard_map/ppermute | solution.py:57
  189.7 1.5 collective-permute-done.21.refs_4_
  191.2 8.9 %project.1 = (bf16[512,1024]{1,0:T(8,128)(2,1)}, bf16[512,1024]{1,0:T(8,128)(2,1)}, bf16[512,1024]{1,0:T(8,128)(2,1)}, bf16[512,1024]{1,0:T(8,128)(2,1)}, bf16[5...) custom-call(bf16[512,1024]{1,0:T(8,128)(2,1)} %bitcast.176, ...), custom_call_target="tpu_custom_call" | custom-call | flops 3221225472 | bytes 25165824 | tf_op jit(solution)/shard_map/project/pallas_call | solution.py:208
  200.1 14.3 %weigh.1 = (bf16[8,512,512]{2,1,0:T(8,128)(2,1)}, bf16[8,512,1024]{2,1,0:T(8,128)(2,1)}) custom-call(bf16[512,1024]{1,0:T(8,128)(2,1)} %get-tuple-element.74.qmem, bf16[512,1024]{1,0:T(8,128)(2,1)} %get-tuple-element.75.qloc, bf16[512,1024]{1,0:T(8,128)(2,1)} %get-tuple-element.76.kloc, bf16[8,128,1024]{2,1,0:T(8,128)(2,1)} %copy-done.5, ...), custom_call_target="tpu_custom_call" | custom-call | flops 3221225472 | bytes 25165824 | tf_op jit(solution)/shard_map/weigh/pallas_call | solution.py:261
  215.7 10.1 %attend.1.att_ref.att = bf16[512,1024]{1,0:T(8,128)(2,1)} custom-call(bf16[8,512,512]{2,1,0:T(8,128)(2,1)} %get-tuple-element.79.p_loc, bf16[8,512,1024]{2,1,0:T(8,128)(2,1)} %get-tuple-element.80.p_mem, bf16[512,1024]{1,0:T(8,128)(2,1)} %get-tuple-element.81.v, bf16[8,128,1024]{2,1,0:T(8,128)(2,1)} %copy-done.2), custom_call_target="tpu_custom_call" | custom-call | flops 1610612736 | bytes 25165824 | tf_op jit(solution)/shard_map/attend/pallas_call | solution.py:288
  226.8 45.2 %feed.1 = (bf16[4,2,4,2,32,2816]{5,4,3,2,1,0:T(8,128)(2,1)}, bf16[2,4,2,480,256]{4,3,2,1,0:T(8,128)(2,1)}, bf16[2,4,2,480,256]{4,3,2,1,0:T(8,128)(2,1)}, bf16[51...) custom-call(bf16[512,1024]{1,0:T(8,128)(2,1)} %bitcast.177, ...), custom_call_target="tpu_custom_call" | custom-call | flops 26575110144 | bytes 25165824 | tf_op jit(solution)/shard_map/feed/pallas_call | solution.py:425
  273.5 1.5 pad_maximum_fusion.2
  275.0 4.9 %all-to-all-start.2 = ((bf16[8,2,64,1024]{3,2,1,0:T(8,128)(2,1)}), bf16[8,2,64,1024]{3,2,1,0:T(8,128)(2,1)S(1)}, u32[]{:S(2)}, u32[]{:S(2)}) async-start(bf16[8,2,64,1024]{3,2,1,0:T(8,128)(2,1)} %pad_maximum_fusion.2), calls=%async_computation.2 | async-start | bytes 4194304 | tf_op jit(solution)/shard_map/all_to_all | solution.py:706
  279.9 6.2 %add_convert_fusion = bf16[2,4,2,480,256]{4,3,2,1,0:T(8,128)(2,1)S(1)} fusion(bf16[2,4,2,480,256]{4,3,2,1,0:T(8,128)(2,1)} %collective-permute-done.27, bf16[2,4,2,480,256]{4,3,2,1,0:T(8,128)(2,1)} %get-tuple-element.92), kind=kLoop, calls=%fused_computation.5 | loop fusion | flops 7864320 | bytes 11796480 | tf_op jit(solution)/shard_map/convert_element_type | solution.py:575
  286.1 1.5 slice_bitcast_fusion.3
  289.1 16.4 %attend_back.1 = (bf16[512,1024]{1,0:T(8,128)(2,1)}, bf16[512,1024]{1,0:T(8,128)(2,1)}, bf16[512,1024]{1,0:T(8,128)(2,1)}) custom-call(bf16[8,512,512]{2,1,0:T(8,128)(2,1)} %get-tuple-element.79.p_loc, bf16[8,512,1024]{2,1,0:T(8,128)(2,1)} %get-tuple-element.80.p_mem, bf16[512,1024]{1,0:T(8,128)(2,1)} %get-tuple-element.94.datt, ...), custom_call_target="tpu_custom_call" | custom-call | flops 4294967296 | bytes 25165824 | tf_op jit(solution)/shard_map/attend_back/pallas_call | solution.py:480
  305.5 17.2 %collective-permute-done.28 = bf16[2,2,480,256]{3,2,1,0:T(8,128)(2,1)} collective-permute-done((bf16[2,2,480,256]{3,2,1,0:T(8,128)(2,1)}, bf16[2,2,480,256]{3,2,1,0:T(8,128)(2,1)}, u32[]{:S(2)}, u32[]{:S(2)}) %collective-permute-start.28) | collective-permute-done | bytes 983072 | tf_op jit(solution)/shard_map/ppermute | solution.py:57
  323.0 2.3 fusion.6
  325.4 8.5 %project_grads.1 = (bf16[2,4,2,96,1024]{4,3,2,1,0:T(8,128)(2,1)}, bf16[2,4,2,96,1024]{4,3,2,1,0:T(8,128)(2,1)}) custom-call(bf16[512,1024]{1,0:T(8,128)(2,1)} %get-tuple-element.99.normed_ref, bf16[512,1024]{1,0:T(8,128)(2,1)} %get-tuple-element.107.dq, bf16[512,1024]{1,0:T(8,128)(2,1)} %get-tuple-element.100.dk, bf16[512,1024]{1,0:T(8,128)(2,1)} %get-tuple-element.101.dv), custom_call_target="tpu_custom_call" | custom-call | flops 1048576 | bytes 25165824 | tf_op jit(solution)/shard_map/project_grads/pallas_call | solution.py:519
  333.9 2.0 collective-permute-start.30
  336.2 1.5 slice_bitcast_fusion.1
  337.8 15.9 %collective-permute-done.30 = bf16[2,480,256]{2,1,0:T(8,128)(2,1)} collective-permute-done((bf16[2,480,256]{2,1,0:T(8,128)(2,1)S(1)}, bf16[2,480,256]{2,1,0:T(8,128)(2,1)}, u32[]{:S(2)}, u32[]{:S(2)}) %collective-permute-start.30) | collective-permute-done | bytes 491552 | tf_op jit(solution)/shard_map/ppermute | solution.py:57
  353.7 2.4 fusion.3
  356.1 2.4 collective-permute-start.38
  358.5 1.5 collective-permute-start.39
  360.1 10.8 %project_back.1 = f32[512,1024]{1,0:T(8,128)} custom-call(bf16[512,1024]{1,0:T(8,128)(2,1)} %bitcast.178, f32[512,1024]{1,0:T(8,128)} %get-tuple-element.90.dmix_ref, f32[2,1024]{1,0:T(2,128)} %get-tuple-element.84.gains_ref, bf16[512,1024]{1,0:T(8,128)(2,1)} %get-tuple-element.107.dq, bf16[512,1024]{1,0:T(8,128)(2,1)} %get-tuple-element.100.dk, ...), custom_call_target="tpu_custom_call" | custom-call | flops 1048576 | bytes 25165824 | tf_op jit(solution)/shard_map/project_back/pallas_call | solution.py:559
  370.9 4.6 add_convert_fusion.1
  378.9 1.4 collective-permute-start.51
  381.7 1.7 collective-permute-start.33
  383.8 2.0 collective-permute-done.49
  385.8 5.9 %collective-permute-done.50 = bf16[480,256]{1,0:T(8,128)(2,1)S(1)} collective-permute-done((bf16[480,256]{1,0:T(8,128)(2,1)S(1)}, bf16[480,256]{1,0:T(8,128)(2,1)S(1)}, u32[]{:S(2)}, u32[]{:S(2)}) %collective-permute-start.50) | collective-permute-done | bytes 245792 | tf_op jit(solution)/shard_map/ppermute | solution.py:57
  393.2 2.8 gather_fusion.1
  397.3 4.6 collective-permute-start.40
  401.9 2.0 collective-permute-start.41
  406.4 1.4 fusion.10
  408.5 1.7 collective-permute-start.36
  410.2 4.9 %collective-permute-done.40 = bf16[2,32,2816]{2,1,0:T(8,128)(2,1)S(1)} collective-permute-done((bf16[2,32,2816]{2,1,0:T(8,128)(2,1)S(1)}, bf16[2,32,2816]{2,1,0:T(8,128)(2,1)S(1)}, u32[]{:S(2)}, u32[]{:S(2)}) %collective-permute-start.40) | collective-permute-done | bytes 360480 | tf_op jit(solution)/shard_map/ppermute | solution.py:57
  415.1 14.5 %collective-permute-done.41 = bf16[2,32,2816]{2,1,0:T(8,128)(2,1)S(1)} collective-permute-done((bf16[2,32,2816]{2,1,0:T(8,128)(2,1)S(1)}, bf16[2,32,2816]{2,1,0:T(8,128)(2,1)S(1)}, u32[]{:S(2)}, u32[]{:S(2)}) %collective-permute-start.41) | collective-permute-done | bytes 360480 | tf_op jit(solution)/shard_map/ppermute | solution.py:57
  429.6 1.9 fusion.16
  432.4 1.4 collective-permute-start.53
  435.1 1.5 fusion.13
  436.6 7.1 %collective-permute-start.44 = (bf16[96,1024]{1,0:T(8,128)(2,1)S(1)}, bf16[96,1024]{1,0:T(8,128)(2,1)S(1)}, u32[]{:S(2)}, u32[]{:S(2)}) collective-permute-start(bf16[96,1024]{1,0:T(8,128)(2,1)S(1)} %get-tuple-element.189), channel_id=1, source_target_pairs={{0,4},{1,5},{2,6},{3,7},{4,0},{5,1},{6,2},{7,3},{8,12},{9,13},{10,... | collective-permute-start | bytes 589832 | tf_op jit(solution)/shard_map/ppermute | solution.py:57
  444.2 10.7 %collective-permute-done.44 = bf16[96,1024]{1,0:T(8,128)(2,1)S(1)} collective-permute-done((bf16[96,1024]{1,0:T(8,128)(2,1)S(1)}, bf16[96,1024]{1,0:T(8,128)(2,1)S(1)}, u32[]{:S(2)}, u32[]{:S(2)}) %collective-permute-start.44) | collective-permute-done | bytes 196640 | tf_op jit(solution)/shard_map/ppermute | solution.py:57
  457.8 3.0 collective-permute-done.43
  462.6 1.9 collective-permute-start.48
  464.5 1.5 pad_maximum_fusion.4
  (230 shorter events, 60.1 us)
Async XLA Ops:
  7.2 218.7 %all-gather.3.cloned.1.call-start = ((), (), s32[]{:S(2)}) async-start(), calls=%async_computation.5 | async-start | bytes 12976128 | tf_op jit(solution)/shard_map/all_gather | solution.py:677
  8.4 18.6 %collective-permute-start = (bf16[32,5632]{1,0:T(8,128)(2,1)S(1)}, bf16[32,5632]{1,0:T(8,128)(2,1)}, u32[]{:S(2)}, u32[]{:S(2)}) collective-permute-start(bf16[32,5632]{1,0:T(8,128)(2,1)S(1)} %pad_maximum_fusion.9), channel_id=1, source_target_pairs={{0,2},{1,3},{2,0},{3,1},{4,6},{5,7},{6,4},{7,5},{8,10},{9,11},{10,... | collective-permute-start | bytes 1081352 | tf_op jit(solution)/shard_map/ppermute | solution.py:57
  11.5 27.8 %collective-permute-start.1 = (bf16[32,5632]{1,0:T(8,128)(2,1)S(1)}, bf16[32,5632]{1,0:T(8,128)(2,1)}, u32[]{:S(2)}, u32[]{:S(2)}) collective-permute-start(bf16[32,5632]{1,0:T(8,128)(2,1)S(1)} %pad_maximum_fusion.9), channel_id=1, source_target_pairs={{0,4},{1,5},{2,6},{3,7},{4,0},{5,1},{6,2},{7,3},{8,12},{9,13},{10,... | collective-permute-start | bytes 1081352 | tf_op jit(solution)/shard_map/ppermute | solution.py:57
  14.1 25.2 %collective-permute-start.2 = (bf16[32,5632]{1,0:T(8,128)(2,1)S(1)}, bf16[32,5632]{1,0:T(8,128)(2,1)}, u32[]{:S(2)}, u32[]{:S(2)}) collective-permute-start(bf16[32,5632]{1,0:T(8,128)(2,1)S(1)} %pad_maximum_fusion.9), channel_id=1, source_target_pairs={{0,6},{1,7},{2,4},{3,5},{4,2},{5,3},{6,0},{7,1},{8,14},{9,15},{10,... | collective-permute-start | bytes 1081352 | tf_op jit(solution)/shard_map/ppermute | solution.py:57
  41.8 13.6 %collective-permute-start.3 = (bf16[400,256]{1,0:T(8,128)(2,1)S(1)}, bf16[400,256]{1,0:T(8,128)(2,1)S(1)}, u32[]{:S(2)}, u32[]{:S(2)}) collective-permute-start(bf16[400,256]{1,0:T(8,128)(2,1)S(1)} %pad_maximum_fusion.13), channel_id=1, source_target_pairs={{0,2},{1,3},{2,0},{3,1},{4,6},{5,7},{6,4},{7,5},{8,10},{9,11},{10,... | collective-permute-start | bytes 614408 | tf_op jit(solution)/shard_map/ppermute | solution.py:57
  48.8 17.3 %collective-permute-start.4 = (bf16[400,256]{1,0:T(8,128)(2,1)S(1)}, bf16[400,256]{1,0:T(8,128)(2,1)S(1)}, u32[]{:S(2)}, u32[]{:S(2)}) collective-permute-start(bf16[400,256]{1,0:T(8,128)(2,1)S(1)} %pad_maximum_fusion.13), channel_id=1, source_target_pairs={{0,4},{1,5},{2,6},{3,7},{4,0},{5,1},{6,2},{7,3},{8,12},{9,13},{10,... | collective-permute-start | bytes 614408 | tf_op jit(solution)/shard_map/ppermute | solution.py:57
  49.9 16.2 %collective-permute-start.5 = (bf16[400,256]{1,0:T(8,128)(2,1)S(1)}, bf16[400,256]{1,0:T(8,128)(2,1)S(1)}, u32[]{:S(2)}, u32[]{:S(2)}) collective-permute-start(bf16[400,256]{1,0:T(8,128)(2,1)S(1)} %pad_maximum_fusion.13), channel_id=1, source_target_pairs={{0,6},{1,7},{2,4},{3,5},{4,2},{5,3},{6,0},{7,1},{8,14},{9,15},{10,... | collective-permute-start | bytes 614408 | tf_op jit(solution)/shard_map/ppermute | solution.py:57
  51.2 43.3 %copy-start.22 = (bf16[400,256]{1,0:T(8,128)(2,1)S(1)}, bf16[400,256]{1,0:T(8,128)(2,1)}, u32[]{:S(2)}) copy-start(bf16[400,256]{1,0:T(8,128)(2,1)} %copy-done.21) | copy-start | bytes 614404
  66.1 10.2 %collective-permute-start.15 = (bf16[480,256]{1,0:T(8,128)(2,1)S(1)}, bf16[480,256]{1,0:T(8,128)(2,1)S(1)}, u32[]{:S(2)}, u32[]{:S(2)}) collective-permute-start(bf16[480,256]{1,0:T(8,128)(2,1)S(1)} %pad_maximum_fusion.12), channel_id=1, source_target_pairs={{0,2},{1,3},{2,0},{3,1},{4,6},{5,7},{6,4},{7,5},{8,10},{9,11},{10,... | collective-permute-start | bytes 737288 | tf_op jit(solution)/shard_map/ppermute | solution.py:57
  68.8 19.7 %collective-permute-start.16 = (bf16[480,256]{1,0:T(8,128)(2,1)S(1)}, bf16[480,256]{1,0:T(8,128)(2,1)S(1)}, u32[]{:S(2)}, u32[]{:S(2)}) collective-permute-start(bf16[480,256]{1,0:T(8,128)(2,1)S(1)} %pad_maximum_fusion.12), channel_id=1, source_target_pairs={{0,4},{1,5},{2,6},{3,7},{4,0},{5,1},{6,2},{7,3},{8,12},{9,13},{10,... | collective-permute-start | bytes 737288 | tf_op jit(solution)/shard_map/ppermute | solution.py:57
  69.8 19.4 %collective-permute-start.17 = (bf16[480,256]{1,0:T(8,128)(2,1)S(1)}, bf16[480,256]{1,0:T(8,128)(2,1)}, u32[]{:S(2)}, u32[]{:S(2)}) collective-permute-start(bf16[480,256]{1,0:T(8,128)(2,1)S(1)} %pad_maximum_fusion.12), channel_id=1, source_target_pairs={{0,6},{1,7},{2,4},{3,5},{4,2},{5,3},{6,0},{7,1},{8,14},{9,15},{10,... | collective-permute-start | bytes 737288 | tf_op jit(solution)/shard_map/ppermute | solution.py:57
  89.2 54.4 %all-to-all-start = ((bf16[8,128,1024]{2,1,0:T(8,128)(2,1)}), bf16[8,128,1024]{2,1,0:T(8,128)(2,1)S(1)}, u32[]{:S(2)}, u32[]{:S(2)}) async-start(bf16[8,128,1024]{2,1,0:T(8,128)(2,1)} %get-tuple-element.78), calls=%async_computation | async-start | bytes 4194304 | tf_op jit(solution)/shard_map/all_to_all | solution.py:695
  95.8 57.1 %copy-start.11 = (bf16[4,400,256]{2,1,0:T(8,128)(2,1)}, bf16[4,400,256]{2,1,0:T(8,128)(2,1)S(1)}, u32[]{:S(2)}) copy-start(bf16[4,400,256]{2,1,0:T(8,128)(2,1)S(1)} %pad_maximum_fusion.7.refs_0_) | copy-start | bytes 2457604
  95.8 34.7 %collective-permute-start.6 = (bf16[4,400,256]{2,1,0:T(8,128)(2,1)S(1)}, bf16[4,400,256]{2,1,0:T(8,128)(2,1)S(1)}, u32[]{:S(2)}, u32[]{:S(2)}) collective-permute-start(bf16[4,400,256]{2,1,0:T(8,128)(2,1)S(1)} %pad_maximum_fusion.7.refs_0_), channel_id=1, source_target_pairs={{0,8},{8,0},{16,24},{24,16},{1,9},{9,1},{17,25},{25,17},{2,10},{10... | collective-permute-start | bytes 2457608 | tf_op jit(solution)/shard_map/ppermute | solution.py:57
  97.4 34.8 %collective-permute-start.7 = (bf16[4,400,256]{2,1,0:T(8,128)(2,1)S(1)}, bf16[4,400,256]{2,1,0:T(8,128)(2,1)S(1)}, u32[]{:S(2)}, u32[]{:S(2)}) collective-permute-start(bf16[4,400,256]{2,1,0:T(8,128)(2,1)S(1)} %pad_maximum_fusion.7.refs_0_), channel_id=1, source_target_pairs={{0,16},{8,24},{16,0},{24,8},{1,17},{9,25},{17,1},{25,9},{2,18},{10... | collective-permute-start | bytes 2457608 | tf_op jit(solution)/shard_map/ppermute | solution.py:57
  130.6 11.4 %collective-permute-start.8 = (bf16[2,400,256]{2,1,0:T(8,128)(2,1)S(1)}, bf16[2,400,256]{2,1,0:T(8,128)(2,1)S(1)}, u32[]{:S(2)}, u32[]{:S(2)}) collective-permute-start(bf16[2,400,256]{2,1,0:T(8,128)(2,1)S(1)} %slice.207), channel_id=1, source_target_pairs={{0,16},{8,24},{16,0},{24,8},{1,17},{9,25},{17,1},{25,9},{2,18},{10... | collective-permute-start | bytes 1228808 | tf_op jit(solution)/shard_map/ppermute | solution.py:57
  132.2 42.5 %copy-start.39 = (s32[1,512]{1,0:T(1,128)S(1)}, s32[1,512]{1,0:T(1,128)}, u32[]{:S(2)}) copy-start(s32[1,512]{1,0:T(1,128)} %param.19) | copy-start | bytes 6148
  132.2 11.2 %collective-permute-start.9 = (bf16[2,400,256]{2,1,0:T(8,128)(2,1)S(1)}, bf16[2,400,256]{2,1,0:T(8,128)(2,1)}, u32[]{:S(2)}, u32[]{:S(2)}) collective-permute-start(bf16[2,400,256]{2,1,0:T(8,128)(2,1)S(1)} %slice.208), channel_id=1, source_target_pairs={{0,8},{8,0},{16,24},{24,16},{1,9},{9,1},{17,25},{25,17},{2,10},{10... | collective-permute-start | bytes 1228808 | tf_op jit(solution)/shard_map/ppermute | solution.py:57
  144.9 69.5 %all-to-all-start.1 = ((bf16[8,128,1024]{2,1,0:T(8,128)(2,1)}), bf16[8,128,1024]{2,1,0:T(8,128)(2,1)S(1)}, u32[]{:S(2)}, u32[]{:S(2)}) async-start(bf16[8,128,1024]{2,1,0:T(8,128)(2,1)} %get-tuple-element.83), calls=%async_computation.1 | async-start | bytes 4194304 | tf_op jit(solution)/shard_map/all_to_all | solution.py:697
  149.2 246.7 %reduce-scatter.2.cloned.1.call-start = ((), (), s32[]{:S(2)}) async-start(), calls=%async_computation.4 | async-start | bytes 12976128 | tf_op jit(solution)/shard_map/reduce_scatter | solution.py:719
  150.5 24.2 %collective-permute-start.18 = (bf16[4,480,256]{2,1,0:T(8,128)(2,1)S(1)}, bf16[4,480,256]{2,1,0:T(8,128)(2,1)S(1)}, u32[]{:S(2)}, u32[]{:S(2)}) collective-permute-start(bf16[4,480,256]{2,1,0:T(8,128)(2,1)S(1)} %pad_maximum_fusion.5.refs_0_), channel_id=1, source_target_pairs={{0,8},{8,0},{16,24},{24,16},{1,9},{9,1},{17,25},{25,17},{2,10},{10... | collective-permute-start | bytes 2949128 | tf_op jit(solution)/shard_map/ppermute | solution.py:57
  151.4 23.7 %collective-permute-start.19 = (bf16[4,480,256]{2,1,0:T(8,128)(2,1)S(1)}, bf16[4,480,256]{2,1,0:T(8,128)(2,1)S(1)}, u32[]{:S(2)}, u32[]{:S(2)}) collective-permute-start(bf16[4,480,256]{2,1,0:T(8,128)(2,1)S(1)} %pad_maximum_fusion.5.refs_0_), channel_id=1, source_target_pairs={{0,16},{8,24},{16,0},{24,8},{1,17},{9,25},{17,1},{25,9},{2,18},{10... | collective-permute-start | bytes 2949128 | tf_op jit(solution)/shard_map/ppermute | solution.py:57
  152.9 23.3 %collective-permute-start.10 = (bf16[4,400,256]{2,1,0:T(8,128)(2,1)S(1)}, bf16[4,400,256]{2,1,0:T(8,128)(2,1)S(1)}, u32[]{:S(2)}, u32[]{:S(2)}) collective-permute-start(bf16[4,400,256]{2,1,0:T(8,128)(2,1)S(1)} %pad_maximum_fusion.7.refs_0_), channel_id=1, source_target_pairs={{0,1},{1,0},{2,3},{3,2},{4,5},{5,4},{6,7},{7,6},{8,9},{9,8},{10,11... | collective-permute-start | bytes 2457608 | tf_op jit(solution)/shard_map/ppermute | solution.py:57
  152.9 24.6 %collective-permute-start.13 = (bf16[2,400,256]{2,1,0:T(8,128)(2,1)}, bf16[2,400,256]{2,1,0:T(8,128)(2,1)S(1)}, u32[]{:S(2)}, u32[]{:S(2)}) collective-permute-start(bf16[2,400,256]{2,1,0:T(8,128)(2,1)} %copy-done.26), channel_id=1, source_target_pairs={{0,1},{1,0},{2,3},{3,2},{4,5},{5,4},{6,7},{7,6},{8,9},{9,8},{10,11... | collective-permute-start | bytes 1228808 | tf_op jit(solution)/shard_map/ppermute | solution.py:57
  153.4 28.9 %collective-permute-start.11 = (bf16[4,400,256]{2,1,0:T(8,128)(2,1)}, bf16[4,400,256]{2,1,0:T(8,128)(2,1)}, u32[]{:S(2)}, u32[]{:S(2)}) collective-permute-start(bf16[4,400,256]{2,1,0:T(8,128)(2,1)} %copy-done.15), channel_id=1, source_target_pairs={{0,1},{1,0},{2,3},{3,2},{4,5},{5,4},{6,7},{7,6},{8,9},{9,8},{10,11... | collective-permute-start | bytes 2457608 | tf_op jit(solution)/shard_map/ppermute | solution.py:57
  174.7 8.2 %collective-permute-start.12 = (bf16[4,400,256]{2,1,0:T(8,128)(2,1)}, bf16[4,400,256]{2,1,0:T(8,128)(2,1)}, u32[]{:S(2)}, u32[]{:S(2)}) collective-permute-start(bf16[4,400,256]{2,1,0:T(8,128)(2,1)} %copy-done.16), channel_id=1, source_target_pairs={{0,1},{1,0},{2,3},{3,2},{4,5},{5,4},{6,7},{7,6},{8,9},{9,8},{10,11... | collective-permute-start | bytes 2457608 | tf_op jit(solution)/shard_map/ppermute | solution.py:57
  175.1 7.2 %collective-permute-start.14 = (bf16[2,400,256]{2,1,0:T(8,128)(2,1)}, bf16[2,400,256]{2,1,0:T(8,128)(2,1)}, u32[]{:S(2)}, u32[]{:S(2)}) collective-permute-start(bf16[2,400,256]{2,1,0:T(8,128)(2,1)} %collective-permute-done.9.refs_4_), channel_id=1, source_target_pairs={{0,1},{1,0},{2,3},{3,2},{4,5},{5,4},{6,7},{7,6},{8,9},{9,8},{10,11... | collective-permute-start | bytes 1228808 | tf_op jit(solution)/shard_map/ppermute | solution.py:57
  176.2 13.5 %collective-permute-start.20 = (bf16[2,480,256]{2,1,0:T(8,128)(2,1)S(1)}, bf16[2,480,256]{2,1,0:T(8,128)(2,1)}, u32[]{:S(2)}, u32[]{:S(2)}) collective-permute-start(bf16[2,480,256]{2,1,0:T(8,128)(2,1)S(1)} %slice.209), channel_id=1, source_target_pairs={{0,16},{8,24},{16,0},{24,8},{1,17},{9,25},{17,1},{25,9},{2,18},{10... | collective-permute-start | bytes 1474568 | tf_op jit(solution)/shard_map/ppermute | solution.py:57
  177.5 13.7 %collective-permute-start.21 = (bf16[2,480,256]{2,1,0:T(8,128)(2,1)}, bf16[2,480,256]{2,1,0:T(8,128)(2,1)}, u32[]{:S(2)}, u32[]{:S(2)}) collective-permute-start(bf16[2,480,256]{2,1,0:T(8,128)(2,1)} %slice.210), channel_id=1, source_target_pairs={{0,8},{8,0},{16,24},{24,16},{1,9},{9,1},{17,25},{25,17},{2,10},{10... | collective-permute-start | bytes 1474568 | tf_op jit(solution)/shard_map/ppermute | solution.py:57
  182.3 43.5 %collective-permute-start.22 = (bf16[4,480,256]{2,1,0:T(8,128)(2,1)}, bf16[4,480,256]{2,1,0:T(8,128)(2,1)}, u32[]{:S(2)}, u32[]{:S(2)}) collective-permute-start(bf16[4,480,256]{2,1,0:T(8,128)(2,1)} %copy-done.20), channel_id=1, source_target_pairs={{0,1},{1,0},{2,3},{3,2},{4,5},{5,4},{6,7},{7,6},{8,9},{9,8},{10,11... | collective-permute-start | bytes 2949128 | tf_op jit(solution)/shard_map/ppermute | solution.py:57
  182.3 43.5 %collective-permute-start.23 = (bf16[4,480,256]{2,1,0:T(8,128)(2,1)}, bf16[4,480,256]{2,1,0:T(8,128)(2,1)}, u32[]{:S(2)}, u32[]{:S(2)}) collective-permute-start(bf16[4,480,256]{2,1,0:T(8,128)(2,1)} %copy-done.31), channel_id=1, source_target_pairs={{0,1},{1,0},{2,3},{3,2},{4,5},{5,4},{6,7},{7,6},{8,9},{9,8},{10,11... | collective-permute-start | bytes 2949128 | tf_op jit(solution)/shard_map/ppermute | solution.py:57
  182.8 43.0 %collective-permute-start.24 = (bf16[4,480,256]{2,1,0:T(8,128)(2,1)}, bf16[4,480,256]{2,1,0:T(8,128)(2,1)}, u32[]{:S(2)}, u32[]{:S(2)}) collective-permute-start(bf16[4,480,256]{2,1,0:T(8,128)(2,1)} %copy-done.32), channel_id=1, source_target_pairs={{0,1},{1,0},{2,3},{3,2},{4,5},{5,4},{6,7},{7,6},{8,9},{9,8},{10,11... | collective-permute-start | bytes 2949128 | tf_op jit(solution)/shard_map/ppermute | solution.py:57
  189.6 36.2 %collective-permute-start.25 = (bf16[2,480,256]{2,1,0:T(8,128)(2,1)}, bf16[2,480,256]{2,1,0:T(8,128)(2,1)S(1)}, u32[]{:S(2)}, u32[]{:S(2)}) collective-permute-start(bf16[2,480,256]{2,1,0:T(8,128)(2,1)} %collective-permute-done.20.refs_3_), channel_id=1, source_target_pairs={{0,1},{1,0},{2,3},{3,2},{4,5},{5,4},{6,7},{7,6},{8,9},{9,8},{10,11... | collective-permute-start | bytes 1474568 | tf_op jit(solution)/shard_map/ppermute | solution.py:57
  191.2 34.7 %collective-permute-start.26 = (bf16[2,480,256]{2,1,0:T(8,128)(2,1)}, bf16[2,480,256]{2,1,0:T(8,128)(2,1)S(1)}, u32[]{:S(2)}, u32[]{:S(2)}) collective-permute-start(bf16[2,480,256]{2,1,0:T(8,128)(2,1)} %collective-permute-done.21.refs_4_), channel_id=1, source_target_pairs={{0,1},{1,0},{2,3},{3,2},{4,5},{5,4},{6,7},{7,6},{8,9},{9,8},{10,11... | collective-permute-start | bytes 1474568 | tf_op jit(solution)/shard_map/ppermute | solution.py:57
  272.0 7.9 %collective-permute-start.27 = (bf16[2,4,2,480,256]{4,3,2,1,0:T(8,128)(2,1)}, bf16[2,4,2,480,256]{4,3,2,1,0:T(8,128)(2,1)}, u32[]{:S(2)}, u32[]{:S(2)}) collective-permute-start(bf16[2,4,2,480,256]{4,3,2,1,0:T(8,128)(2,1)} %get-tuple-element.93), channel_id=1, source_target_pairs={{0,1},{1,0},{2,3},{3,2},{4,5},{5,4},{6,7},{7,6},{8,9},{9,8},{10,11... | collective-permute-start | bytes 11796488 | tf_op jit(solution)/shard_map/ppermute | solution.py:57
  275.0 61.2 %all-to-all-start.2 = ((bf16[8,2,64,1024]{3,2,1,0:T(8,128)(2,1)}), bf16[8,2,64,1024]{3,2,1,0:T(8,128)(2,1)S(1)}, u32[]{:S(2)}, u32[]{:S(2)}) async-start(bf16[8,2,64,1024]{3,2,1,0:T(8,128)(2,1)} %pad_maximum_fusion.2), calls=%async_computation.2 | async-start | bytes 4194304 | tf_op jit(solution)/shard_map/all_to_all | solution.py:706
  287.6 35.1 %collective-permute-start.28 = (bf16[2,2,480,256]{3,2,1,0:T(8,128)(2,1)}, bf16[2,2,480,256]{3,2,1,0:T(8,128)(2,1)}, u32[]{:S(2)}, u32[]{:S(2)}) collective-permute-start(bf16[2,2,480,256]{3,2,1,0:T(8,128)(2,1)} %get-tuple-element.170), channel_id=1, source_target_pairs={{0,16},{8,24},{16,0},{24,8},{1,17},{9,25},{17,1},{25,9},{2,18},{10... | collective-permute-start | bytes 2949128 | tf_op jit(solution)/shard_map/ppermute | solution.py:57
  288.0 35.1 %collective-permute-start.29 = (bf16[2,2,480,256]{3,2,1,0:T(8,128)(2,1)}, bf16[2,2,480,256]{3,2,1,0:T(8,128)(2,1)}, u32[]{:S(2)}, u32[]{:S(2)}) collective-permute-start(bf16[2,2,480,256]{3,2,1,0:T(8,128)(2,1)} %get-tuple-element.169), channel_id=1, source_target_pairs={{0,8},{8,0},{16,24},{24,16},{1,9},{9,1},{17,25},{25,17},{2,10},{10... | collective-permute-start | bytes 2949128 | tf_op jit(solution)/shard_map/ppermute | solution.py:57
  333.9 37.1 %collective-permute-start.32 = (bf16[2,4,2,96,1024]{4,3,2,1,0:T(8,128)(2,1)}, bf16[2,4,2,96,1024]{4,3,2,1,0:T(8,128)(2,1)}, u32[]{:S(2)}, u32[]{:S(2)}) collective-permute-start(bf16[2,4,2,96,1024]{4,3,2,1,0:T(8,128)(2,1)} %get-tuple-element.103), channel_id=1, source_target_pairs={{0,1},{1,0},{2,3},{3,2},{4,5},{5,4},{6,7},{7,6},{8,9},{9,8},{10,11... | collective-permute-start | bytes 9437192 | tf_op jit(solution)/shard_map/ppermute | solution.py:57
  333.9 19.8 %collective-permute-start.30 = (bf16[2,480,256]{2,1,0:T(8,128)(2,1)S(1)}, bf16[2,480,256]{2,1,0:T(8,128)(2,1)}, u32[]{:S(2)}, u32[]{:S(2)}) collective-permute-start(bf16[2,480,256]{2,1,0:T(8,128)(2,1)S(1)} %copy-done.25), channel_id=1, source_target_pairs={{0,8},{8,0},{16,24},{24,16},{1,9},{9,1},{17,25},{25,17},{2,10},{10... | collective-permute-start | bytes 1474568 | tf_op jit(solution)/shard_map/ppermute | solution.py:57
  335.9 17.8 %collective-permute-start.31 = (bf16[2,480,256]{2,1,0:T(8,128)(2,1)S(1)}, bf16[2,480,256]{2,1,0:T(8,128)(2,1)}, u32[]{:S(2)}, u32[]{:S(2)}) collective-permute-start(bf16[2,480,256]{2,1,0:T(8,128)(2,1)S(1)} %copy-done.24), channel_id=1, source_target_pairs={{0,16},{8,24},{16,0},{24,8},{1,17},{9,25},{17,1},{25,9},{2,18},{10... | collective-permute-start | bytes 1474568 | tf_op jit(solution)/shard_map/ppermute | solution.py:57
  356.1 20.4 %collective-permute-start.38 = (bf16[480,256]{1,0:T(8,128)(2,1)S(1)}, bf16[480,256]{1,0:T(8,128)(2,1)S(1)}, u32[]{:S(2)}, u32[]{:S(2)}) collective-permute-start(bf16[480,256]{1,0:T(8,128)(2,1)S(1)} %get-tuple-element.188), channel_id=1, source_target_pairs={{0,4},{1,5},{2,6},{3,7},{4,0},{5,1},{6,2},{7,3},{8,12},{9,13},{10,... | collective-permute-start | bytes 737288 | tf_op jit(solution)/shard_map/ppermute | solution.py:57
  358.5 18.0 %collective-permute-start.39 = (bf16[480,256]{1,0:T(8,128)(2,1)S(1)}, bf16[480,256]{1,0:T(8,128)(2,1)S(1)}, u32[]{:S(2)}, u32[]{:S(2)}) collective-permute-start(bf16[480,256]{1,0:T(8,128)(2,1)S(1)} %get-tuple-element.187), channel_id=1, source_target_pairs={{0,6},{1,7},{2,4},{3,5},{4,2},{5,3},{6,0},{7,1},{8,14},{9,15},{10,... | collective-permute-start | bytes 737288 | tf_op jit(solution)/shard_map/ppermute | solution.py:57
  360.0 16.6 %collective-permute-start.37 = (bf16[480,256]{1,0:T(8,128)(2,1)S(1)}, bf16[480,256]{1,0:T(8,128)(2,1)S(1)}, u32[]{:S(2)}, u32[]{:S(2)}) collective-permute-start(bf16[480,256]{1,0:T(8,128)(2,1)S(1)} %slice_bitcast_fusion.20), channel_id=1, source_target_pairs={{0,2},{1,3},{2,0},{3,1},{4,6},{5,7},{6,4},{7,5},{8,10},{9,11},{10,... | collective-permute-start | bytes 737288 | tf_op jit(solution)/shard_map/ppermute | solution.py:57
  376.8 9.0 %collective-permute-start.49 = (bf16[480,256]{1,0:T(8,128)(2,1)S(1)}, bf16[480,256]{1,0:T(8,128)(2,1)S(1)}, u32[]{:S(2)}, u32[]{:S(2)}) collective-permute-start(bf16[480,256]{1,0:T(8,128)(2,1)S(1)} %add_convert_fusion.2), channel_id=1, source_target_pairs={{0,8},{8,0},{16,24},{24,16},{1,9},{9,1},{17,25},{25,17},{2,10},{10... | collective-permute-start | bytes 737288 | tf_op jit(solution)/shard_map/ppermute | solution.py:57
  378.0 13.6 %collective-permute-start.50 = (bf16[480,256]{1,0:T(8,128)(2,1)S(1)}, bf16[480,256]{1,0:T(8,128)(2,1)S(1)}, u32[]{:S(2)}, u32[]{:S(2)}) collective-permute-start(bf16[480,256]{1,0:T(8,128)(2,1)S(1)} %add_convert_fusion.2), channel_id=1, source_target_pairs={{0,16},{8,24},{16,0},{24,8},{1,17},{9,25},{17,1},{25,9},{2,18},{10... | collective-permute-start | bytes 737288 | tf_op jit(solution)/shard_map/ppermute | solution.py:57
  378.9 13.2 %collective-permute-start.51 = (bf16[480,256]{1,0:T(8,128)(2,1)S(1)}, bf16[480,256]{1,0:T(8,128)(2,1)S(1)}, u32[]{:S(2)}, u32[]{:S(2)}) collective-permute-start(bf16[480,256]{1,0:T(8,128)(2,1)S(1)} %add_convert_fusion.2), channel_id=1, source_target_pairs={{0,24},{8,16},{16,8},{24,0},{1,25},{9,17},{17,9},{25,1},{2,26},{10... | collective-permute-start | bytes 737288 | tf_op jit(solution)/shard_map/ppermute | solution.py:57
  381.7 24.7 %collective-permute-start.33 = (bf16[2,2,96,1024]{3,2,1,0:T(8,128)(2,1)}, bf16[2,2,96,1024]{3,2,1,0:T(8,128)(2,1)}, u32[]{:S(2)}, u32[]{:S(2)}) collective-permute-start(bf16[2,2,96,1024]{3,2,1,0:T(8,128)(2,1)} %get-tuple-element.176), channel_id=1, source_target_pairs={{0,16},{8,24},{16,0},{24,8},{1,17},{9,25},{17,1},{25,9},{2,18},{10... | collective-permute-start | bytes 2359304 | tf_op jit(solution)/shard_map/ppermute | solution.py:57
  383.4 23.1 %collective-permute-start.34 = (bf16[2,2,96,1024]{3,2,1,0:T(8,128)(2,1)}, bf16[2,2,96,1024]{3,2,1,0:T(8,128)(2,1)}, u32[]{:S(2)}, u32[]{:S(2)}) collective-permute-start(bf16[2,2,96,1024]{3,2,1,0:T(8,128)(2,1)} %get-tuple-element.175), channel_id=1, source_target_pairs={{0,8},{8,0},{16,24},{24,16},{1,9},{9,1},{17,25},{25,17},{2,10},{10... | collective-permute-start | bytes 2359304 | tf_op jit(solution)/shard_map/ppermute | solution.py:57
  397.3 17.8 %collective-permute-start.40 = (bf16[2,32,2816]{2,1,0:T(8,128)(2,1)S(1)}, bf16[2,32,2816]{2,1,0:T(8,128)(2,1)S(1)}, u32[]{:S(2)}, u32[]{:S(2)}) collective-permute-start(bf16[2,32,2816]{2,1,0:T(8,128)(2,1)S(1)} %get-tuple-element.186), channel_id=1, source_target_pairs={{0,2},{1,3},{2,0},{3,1},{4,6},{5,7},{6,4},{7,5},{8,10},{9,11},{10,... | collective-permute-start | bytes 1081352 | tf_op jit(solution)/shard_map/ppermute | solution.py:57
  401.9 27.7 %collective-permute-start.41 = (bf16[2,32,2816]{2,1,0:T(8,128)(2,1)S(1)}, bf16[2,32,2816]{2,1,0:T(8,128)(2,1)S(1)}, u32[]{:S(2)}, u32[]{:S(2)}) collective-permute-start(bf16[2,32,2816]{2,1,0:T(8,128)(2,1)S(1)} %get-tuple-element.185), channel_id=1, source_target_pairs={{0,4},{1,5},{2,6},{3,7},{4,0},{5,1},{6,2},{7,3},{8,12},{9,13},{10,... | collective-permute-start | bytes 1081352 | tf_op jit(solution)/shard_map/ppermute | solution.py:57
  403.9 25.7 %collective-permute-start.42 = (bf16[2,32,2816]{2,1,0:T(8,128)(2,1)S(1)}, bf16[2,32,2816]{2,1,0:T(8,128)(2,1)S(1)}, u32[]{:S(2)}, u32[]{:S(2)}) collective-permute-start(bf16[2,32,2816]{2,1,0:T(8,128)(2,1)S(1)} %get-tuple-element.184), channel_id=1, source_target_pairs={{0,6},{1,7},{2,4},{3,5},{4,2},{5,3},{6,0},{7,1},{8,14},{9,15},{10,... | collective-permute-start | bytes 1081352 | tf_op jit(solution)/shard_map/ppermute | solution.py:57
  405.5 49.8 %copy-start.6 = (f32[480,4,256]{2,0,1:T(8,128)}, f32[480,4,256]{2,0,1:T(8,128)S(1)}, u32[]{:S(2)}) copy-start(f32[480,4,256]{2,0,1:T(8,128)S(1)} %convert_bitcast_fusion) | copy-start | bytes 5898244
  407.8 27.2 %collective-permute-start.35 = (bf16[2,96,1024]{2,1,0:T(8,128)(2,1)S(1)}, bf16[2,96,1024]{2,1,0:T(8,128)(2,1)S(1)}, u32[]{:S(2)}, u32[]{:S(2)}) collective-permute-start(bf16[2,96,1024]{2,1,0:T(8,128)(2,1)S(1)} %get-tuple-element.174), channel_id=1, source_target_pairs={{0,8},{8,0},{16,24},{24,16},{1,9},{9,1},{17,25},{25,17},{2,10},{10... | collective-permute-start | bytes 1179656 | tf_op jit(solution)/shard_map/ppermute | solution.py:57
  408.5 26.6 %collective-permute-start.36 = (bf16[2,96,1024]{2,1,0:T(8,128)(2,1)S(1)}, bf16[2,96,1024]{2,1,0:T(8,128)(2,1)S(1)}, u32[]{:S(2)}, u32[]{:S(2)}) collective-permute-start(bf16[2,96,1024]{2,1,0:T(8,128)(2,1)S(1)} %get-tuple-element.173), channel_id=1, source_target_pairs={{0,16},{8,24},{16,0},{24,8},{1,17},{9,25},{17,1},{25,9},{2,18},{10... | collective-permute-start | bytes 1179656 | tf_op jit(solution)/shard_map/ppermute | solution.py:57
  431.6 31.1 %collective-permute-start.52 = (bf16[2,32,2816]{2,1,0:T(8,128)(2,1)}, bf16[2,32,2816]{2,1,0:T(8,128)(2,1)}, u32[]{:S(2)}, u32[]{:S(2)}) collective-permute-start(bf16[2,32,2816]{2,1,0:T(8,128)(2,1)} %fusion.16), channel_id=1, source_target_pairs={{0,8},{8,0},{16,24},{24,16},{1,9},{9,1},{17,25},{25,17},{2,10},{10... | collective-permute-start | bytes 1081352 | tf_op jit(solution)/shard_map/ppermute | solution.py:57
  432.4 32.1 %collective-permute-start.53 = (bf16[2,32,2816]{2,1,0:T(8,128)(2,1)}, bf16[2,32,2816]{2,1,0:T(8,128)(2,1)}, u32[]{:S(2)}, u32[]{:S(2)}) collective-permute-start(bf16[2,32,2816]{2,1,0:T(8,128)(2,1)} %fusion.16), channel_id=1, source_target_pairs={{0,16},{8,24},{16,0},{24,8},{1,17},{9,25},{17,1},{25,9},{2,18},{10... | collective-permute-start | bytes 1081352 | tf_op jit(solution)/shard_map/ppermute | solution.py:57
  433.9 30.7 %collective-permute-start.54 = (bf16[2,32,2816]{2,1,0:T(8,128)(2,1)}, bf16[2,32,2816]{2,1,0:T(8,128)(2,1)}, u32[]{:S(2)}, u32[]{:S(2)}) collective-permute-start(bf16[2,32,2816]{2,1,0:T(8,128)(2,1)} %fusion.16), channel_id=1, source_target_pairs={{0,24},{8,16},{16,8},{24,0},{1,25},{9,17},{17,9},{25,1},{2,26},{10... | collective-permute-start | bytes 1081352 | tf_op jit(solution)/shard_map/ppermute | solution.py:57
  436.6 18.3 %collective-permute-start.44 = (bf16[96,1024]{1,0:T(8,128)(2,1)S(1)}, bf16[96,1024]{1,0:T(8,128)(2,1)S(1)}, u32[]{:S(2)}, u32[]{:S(2)}) collective-permute-start(bf16[96,1024]{1,0:T(8,128)(2,1)S(1)} %get-tuple-element.189), channel_id=1, source_target_pairs={{0,4},{1,5},{2,6},{3,7},{4,0},{5,1},{6,2},{7,3},{8,12},{9,13},{10,... | collective-permute-start | bytes 589832 | tf_op jit(solution)/shard_map/ppermute | solution.py:57
  443.7 14.1 %collective-permute-start.45 = (bf16[96,1024]{1,0:T(8,128)(2,1)S(1)}, bf16[96,1024]{1,0:T(8,128)(2,1)S(1)}, u32[]{:S(2)}, u32[]{:S(2)}) collective-permute-start(bf16[96,1024]{1,0:T(8,128)(2,1)S(1)} %get-tuple-element.190), channel_id=1, source_target_pairs={{0,6},{1,7},{2,4},{3,5},{4,2},{5,3},{6,0},{7,1},{8,14},{9,15},{10,... | collective-permute-start | bytes 589832 | tf_op jit(solution)/shard_map/ppermute | solution.py:57
  454.9 5.9 %collective-permute-start.43 = (bf16[96,1024]{1,0:T(8,128)(2,1)S(1)}, bf16[96,1024]{1,0:T(8,128)(2,1)S(1)}, u32[]{:S(2)}, u32[]{:S(2)}) collective-permute-start(bf16[96,1024]{1,0:T(8,128)(2,1)S(1)} %slice_bitcast_fusion.24), channel_id=1, source_target_pairs={{0,2},{1,3},{2,0},{3,1},{4,6},{5,7},{6,4},{7,5},{8,10},{9,11},{10,... | collective-permute-start | bytes 589832 | tf_op jit(solution)/shard_map/ppermute | solution.py:57
  461.0 10.2 %collective-permute-start.46 = (bf16[96,1024]{1,0:T(8,128)(2,1)S(1)}, bf16[96,1024]{1,0:T(8,128)(2,1)S(1)}, u32[]{:S(2)}, u32[]{:S(2)}) collective-permute-start(bf16[96,1024]{1,0:T(8,128)(2,1)S(1)} %fusion.19), channel_id=1, source_target_pairs={{0,8},{8,0},{16,24},{24,16},{1,9},{9,1},{17,25},{25,17},{2,10},{10... | collective-permute-start | bytes 589832 | tf_op jit(solution)/shard_map/ppermute | solution.py:57
  461.5 9.7 %collective-permute-start.47 = (bf16[96,1024]{1,0:T(8,128)(2,1)S(1)}, bf16[96,1024]{1,0:T(8,128)(2,1)S(1)}, u32[]{:S(2)}, u32[]{:S(2)}) collective-permute-start(bf16[96,1024]{1,0:T(8,128)(2,1)S(1)} %fusion.19), channel_id=1, source_target_pairs={{0,16},{8,24},{16,0},{24,8},{1,17},{9,25},{17,1},{25,9},{2,18},{10... | collective-permute-start | bytes 589832 | tf_op jit(solution)/shard_map/ppermute | solution.py:57
  462.6 8.5 %collective-permute-start.48 = (bf16[96,1024]{1,0:T(8,128)(2,1)S(1)}, bf16[96,1024]{1,0:T(8,128)(2,1)}, u32[]{:S(2)}, u32[]{:S(2)}) collective-permute-start(bf16[96,1024]{1,0:T(8,128)(2,1)S(1)} %fusion.19), channel_id=1, source_target_pairs={{0,24},{8,16},{16,8},{24,0},{1,25},{9,17},{17,9},{25,1},{2,26},{10... | collective-permute-start | bytes 589832 | tf_op jit(solution)/shard_map/ppermute | solution.py:57
  (42 other events, 365.7 us)
Sparse Core Ops, SparseCore 0:
  42.0 86.8 all-gather.2
  272.2 102.3 reduce-scatter.1

commit v3 on v2

--- a/solution.py
+++ b/solution.py
@@ -66,9 +66,12 @@
     return [quarter] + [swap(quarter, KEY, 8, 2 * r) for r in (1, 2, 3)]
 
 
-def across(held):
-    x, y = swap(held, "dp", 4, 1), swap(held, "dp", 4, 2)
-    return [held, x, y, swap(x[:2], "dp", 4, 2), swap(y[2:], "dp", 4, 1)]
+def across_first(held):
+    return [held, swap(held, "dp", 4, 1), swap(held, "dp", 4, 2)]
+
+
+def across_second(near):
+    return near + [swap(near[1][:2], "dp", 4, 2), swap(near[2][2:], "dp", 4, 1)]
 
 
 def other_core(pieces):
@@ -602,8 +605,11 @@
     return add(parts[0], *come)
 
 
-def from_dp(share):
-    held = jnp.stack([share] + [swap(share, "dp", 4, r) for r in (1, 2, 3)])
+def from_dp(share, token=None):
+    held = [share] + [swap(share, "dp", 4, r) for r in (1, 2, 3)]
+    if token is not None:
+        held = after(held, token)
+    held = jnp.stack(held)
     return jnp.take(held, jnp.arange(4) ^ lax.axis_index("dp"), axis=0)
 
 
@@ -676,11 +682,10 @@
         out_k = after(out_k, project_out)
         gate_up = lax.all_gather(jnp.stack(gate_up), ("dp", "core"), axis=0, tiled=False)
         gate_up = gate_up.reshape((n_dp, 2) + gate_up.shape[1:])
-        project_in = across(jnp.stack(project_in))
-        project_out = across(jnp.stack(after(project_out, project_in)))
+        project_in = across_second(across_first(jnp.stack(project_in)))
+        project_out = across_first(jnp.stack(after(project_out, project_in)))
         out_v = after(out_v, project_in)
         first = project_in + other_core(project_in)
-        second = project_out + other_core(project_out) + [gate_up]
     else:
         whole = lambda w: lax.all_gather(w, KEY, axis=0, tiled=True)
         first = [
@@ -698,6 +703,9 @@
 
     qmem, qloc, kloc, kraw, v, normed, gains = project(plan, x, cosine, sine, first)
     p_loc, p_mem = weigh(qmem, qloc, kloc, mem_k, local_bias, memory_bias)
+    if plan.fast:
+        project_out = across_second(after(project_out, p_loc))
+        second = project_out + other_core(project_out) + [gate_up]
     attended = attend(p_loc, p_mem, v, mem_v)
 
     run = tokens // group
@@ -744,9 +752,9 @@
         mine, passed = over_dp_first(g_qkv, g_gu)
         g_gu = over_z(g_gu, passed)
         blocks = over_dp_second(mine, passed, g_gu)
-        g_do = from_dp(g_do)
+        g_do = from_dp(g_do, blocks)
         g_qkv = over_z(blocks)
-        g_gu = from_dp(g_gu)
+        g_gu = from_dp(g_gu, g_qkv)
         g_qkv = from_dp(g_qkv).astype(F32)
         g_do = g_do.transpose(1, 0, 2).reshape(-1, width).astype(F32)
         total_down, total_out = g_do[:-rows], g_do[-rows:]

time: 491 us -> 470 us (0.957)
  waiting for transfers between devices: 195 us -> 173 us
    ppermute x55, waiting for transfers between devices: 195 us -> 173 us  [swap(): return lax.ppermute(values, axis, [(i, i ^ distance) for i in range(size)])]
    unnamed x92 -> x90, local copies, waits for them, and re-layouts: 10.1 us -> 13.9 us
  transfers between devices with their start and end apart: 60 -> 60, of which waited for: 27 -> 22; matrix products, arithmetic and copies ran while one was open for 12% -> 12% of each run, Pallas kernels for 14% -> 15%
where the time goes in v3:
time: 470 us; the launch traced here: 462 us
  waiting for transfers between devices  173 us (37%)
  Pallas kernels  114 us (24%)
  starting transfers between devices  83.3 us (18%)
  other arithmetic  43.5 us (9%)
  local copies, waits for them, and re-layouts  32.4 us (7%)
  between operations  16 us (3%)
    ppermute x55, waiting for transfers between devices, swap(): return lax.ppermute(values, axis, [(i, i ^ distance) for i in range(size)])  173 us
    ppermute x55, starting transfers between devices, swap(): return lax.ppermute(values, axis, [(i, i ^ distance) for i in range(size)])  68.8 us
    pallas_call x1, Pallas kernels, feed(): pl.pallas_call(functools.partial(feed_kernel, plan, len(pieces)), grid=(s...  45.2 us
    convert_element_type x9, other arithmetic, add(): return total.astype(BF16)  19.9 us
    pallas_call x1, Pallas kernels, attend_back(): pl.pallas_call(attend_back_kernel, grid=(width // HD,), in_specs=prob_spe...  16.2 us
    pallas_call x1, Pallas kernels, weigh(): pl.pallas_call(weigh_kernel, grid=(width // HD,), in_specs=[head_spec(tok...  14.3 us
    unnamed x90, local copies, waits for them, and re-layouts  13.9 us
    pallas_call x1, Pallas kernels, project_back(): pl.pallas_call(functools.partial(project_back_kernel, plan, len(pieces)),...  10.8 us
  transfers between devices with their start and end apart: 60, of which 22 were waited for; matrix products, arithmetic and copies ran while one was open for 12% of the time, Pallas kernels for 15%

profile of v3, /device:TPU:0, one launch (start us, length us, event | category | flops | bytes accessed | tf_op | source)
XLA Modules:
  0.0 461.9 jit_solution(11174437284362656783)
XLA Ops:
  8.4 3.1 collective-permute-start
  11.5 2.6 collective-permute-start.1
  16.1 1.8 gather_fusion.4
  21.4 2.4 pad_maximum_fusion
  23.8 3.2 collective-permute-done
  27.0 12.3 %collective-permute-done.1 = bf16[32,5632]{1,0:T(8,128)(2,1)} collective-permute-done((bf16[32,5632]{1,0:T(8,128)(2,1)S(1)}, bf16[32,5632]{1,0:T(8,128)(2,1)}, u32[]{:S(2)}, u32[]{:S(2)}) %collective-permute-start.1) | collective-permute-done | bytes 360480 | tf_op jit(solution)/shard_map/ppermute | solution.py:57
  39.3 2.5 pad_maximum_fusion.3
  41.8 6.9 %collective-permute-start.3 = (bf16[400,256]{1,0:T(8,128)(2,1)S(1)}, bf16[400,256]{1,0:T(8,128)(2,1)S(1)}, u32[]{:S(2)}, u32[]{:S(2)}) collective-permute-start(bf16[400,256]{1,0:T(8,128)(2,1)S(1)} %pad_maximum_fusion.13), channel_id=1, source_target_pairs={{0,2},{1,3},{2,0},{3,1},{4,6},{5,7},{6,4},{7,5},{8,10},{9,11},{10,... | collective-permute-start | bytes 614408 | tf_op jit(solution)/shard_map/ppermute | solution.py:57
  51.2 4.1 collective-permute-done.3
  55.4 10.7 %collective-permute-done.4 = bf16[400,256]{1,0:T(8,128)(2,1)S(1)} collective-permute-done((bf16[400,256]{1,0:T(8,128)(2,1)S(1)}, bf16[400,256]{1,0:T(8,128)(2,1)S(1)}, u32[]{:S(2)}, u32[]{:S(2)}) %collective-permute-start.4) | collective-permute-done | bytes 204832 | tf_op jit(solution)/shard_map/ppermute | solution.py:57
  66.1 2.8 collective-permute-start.15
  69.8 1.5 collective-permute-start.17
  71.3 5.0 %collective-permute-done.15 = bf16[480,256]{1,0:T(8,128)(2,1)S(1)} collective-permute-done((bf16[480,256]{1,0:T(8,128)(2,1)S(1)}, bf16[480,256]{1,0:T(8,128)(2,1)S(1)}, u32[]{:S(2)}, u32[]{:S(2)}) %collective-permute-start.15) | collective-permute-done | bytes 245792 | tf_op jit(solution)/shard_map/ppermute | solution.py:57
  76.3 12.2 %collective-permute-done.16 = bf16[480,256]{1,0:T(8,128)(2,1)S(1)} collective-permute-done((bf16[480,256]{1,0:T(8,128)(2,1)S(1)}, bf16[480,256]{1,0:T(8,128)(2,1)S(1)}, u32[]{:S(2)}, u32[]{:S(2)}) %collective-permute-start.16) | collective-permute-done | bytes 245792 | tf_op jit(solution)/shard_map/ppermute | solution.py:57
  89.2 5.3 %all-to-all-start = ((bf16[8,128,1024]{2,1,0:T(8,128)(2,1)}), bf16[8,128,1024]{2,1,0:T(8,128)(2,1)S(1)}, u32[]{:S(2)}, u32[]{:S(2)}) async-start(bf16[8,128,1024]{2,1,0:T(8,128)(2,1)} %get-tuple-element.89), calls=%async_computation | async-start | bytes 4194304 | tf_op jit(solution)/shard_map/all_to_all | solution.py:700
  95.8 1.6 collective-permute-start.6
  97.4 1.5 collective-permute-start.7
  98.9 31.7 %collective-permute-done.6.refs_1_ = bf16[4,400,256]{2,1,0:T(8,128)(2,1)S(1)} collective-permute-done((bf16[4,400,256]{2,1,0:T(8,128)(2,1)S(1)}, bf16[4,400,256]{2,1,0:T(8,128)(2,1)S(1)}, u32[]{:S(2)}, u32[]{:S(2)}) %collective-permute-start.6) | collective-permute-done | bytes 819232 | tf_op jit(solution)/shard_map/ppermute | solution.py:57
  130.6 1.5 collective-permute-start.8
  132.8 9.2 %collective-permute-done.8.refs_3_ = bf16[2,400,256]{2,1,0:T(8,128)(2,1)S(1)} collective-permute-done((bf16[2,400,256]{2,1,0:T(8,128)(2,1)S(1)}, bf16[2,400,256]{2,1,0:T(8,128)(2,1)S(1)}, u32[]{:S(2)}, u32[]{:S(2)}) %collective-permute-start.8) | collective-permute-done | bytes 409632 | tf_op jit(solution)/shard_map/ppermute | solution.py:57
  144.9 4.3 all-to-all-start.1
  152.8 2.2 pad_maximum_fusion.5.refs_0_
  155.7 1.5 collective-permute-start.19
  161.4 8.9 %project.1 = (bf16[512,1024]{1,0:T(8,128)(2,1)}, bf16[512,1024]{1,0:T(8,128)(2,1)}, bf16[512,1024]{1,0:T(8,128)(2,1)}, bf16[512,1024]{1,0:T(8,128)(2,1)}, bf16[5...) custom-call(bf16[512,1024]{1,0:T(8,128)(2,1)} %bitcast.175, ...), custom_call_target="tpu_custom_call" | custom-call | flops 3221225472 | bytes 25165824 | tf_op jit(solution)/shard_map/project/pallas_call | solution.py:211
  170.3 14.3 %weigh.1 = (bf16[8,512,512]{2,1,0:T(8,128)(2,1)}, bf16[8,512,1024]{2,1,0:T(8,128)(2,1)}) custom-call(bf16[512,1024]{1,0:T(8,128)(2,1)} %get-tuple-element.85.qmem, bf16[512,1024]{1,0:T(8,128)(2,1)} %get-tuple-element.86.qloc, bf16[512,1024]{1,0:T(8,128)(2,1)} %get-tuple-element.87.kloc, bf16[8,128,1024]{2,1,0:T(8,128)(2,1)} %copy-done.8, ...), custom_call_target="tpu_custom_call" | custom-call | flops 3221225472 | bytes 25165824 | tf_op jit(solution)/shard_map/weigh/pallas_call | solution.py:264
  188.5 11.3 %collective-permute-done.20.refs_3_ = bf16[2,480,256]{2,1,0:T(8,128)(2,1)} collective-permute-done((bf16[2,480,256]{2,1,0:T(8,128)(2,1)S(1)}, bf16[2,480,256]{2,1,0:T(8,128)(2,1)}, u32[]{:S(2)}, u32[]{:S(2)}) %collective-permute-start.20) | collective-permute-done | bytes 491552 | tf_op jit(solution)/shard_map/ppermute | solution.py:57
  201.6 10.1 %attend.1.att_ref.att = bf16[512,1024]{1,0:T(8,128)(2,1)} custom-call(bf16[8,512,512]{2,1,0:T(8,128)(2,1)} %get-tuple-element.90.p_loc, bf16[8,512,1024]{2,1,0:T(8,128)(2,1)} %get-tuple-element.91.p_mem, bf16[512,1024]{1,0:T(8,128)(2,1)} %get-tuple-element.92.v, bf16[8,128,1024]{2,1,0:T(8,128)(2,1)} %copy-done.2), custom_call_target="tpu_custom_call" | custom-call | flops 1610612736 | bytes 25165824 | tf_op jit(solution)/shard_map/attend/pallas_call | solution.py:291
  211.8 45.2 %feed.1 = (bf16[4,2,4,2,32,2816]{5,4,3,2,1,0:T(8,128)(2,1)}, bf16[2,4,2,480,256]{4,3,2,1,0:T(8,128)(2,1)}, bf16[2,4,2,480,256]{4,3,2,1,0:T(8,128)(2,1)}, bf16[51...) custom-call(bf16[512,1024]{1,0:T(8,128)(2,1)} %bitcast.176, ...), custom_call_target="tpu_custom_call" | custom-call | flops 26575110144 | bytes 25165824 | tf_op jit(solution)/shard_map/feed/pallas_call | solution.py:428
  257.4 6.7 %collective-permute-done.27 = bf16[2,4,2,480,256]{4,3,2,1,0:T(8,128)(2,1)S(1)} collective-permute-done((bf16[2,4,2,480,256]{4,3,2,1,0:T(8,128)(2,1)}, bf16[2,4,2,480,256]{4,3,2,1,0:T(8,128)(2,1)S(1)}, u32[]{:S(2)}, u32[]{:S(2)}) %collective-permute-start.27) | collective-permute-done | bytes 3932192 | tf_op jit(solution)/shard_map/ppermute | solution.py:57
  264.1 3.3 add_convert_fusion
  267.4 2.4 copy-done.3
  271.2 1.5 collective-permute-start.28
  273.5 1.5 pad_maximum_fusion.2
  275.0 4.8 %all-to-all-start.2 = ((bf16[8,2,64,1024]{3,2,1,0:T(8,128)(2,1)}), bf16[8,2,64,1024]{3,2,1,0:T(8,128)(2,1)S(1)}, u32[]{:S(2)}, u32[]{:S(2)}) async-start(bf16[8,2,64,1024]{3,2,1,0:T(8,128)(2,1)} %pad_maximum_fusion.2), calls=%async_computation.2 | async-start | bytes 4194304 | tf_op jit(solution)/shard_map/all_to_all | solution.py:714
  279.8 16.2 %attend_back.1 = (bf16[512,1024]{1,0:T(8,128)(2,1)}, bf16[512,1024]{1,0:T(8,128)(2,1)}, bf16[512,1024]{1,0:T(8,128)(2,1)}) custom-call(bf16[8,512,512]{2,1,0:T(8,128)(2,1)} %get-tuple-element.90.p_loc, bf16[8,512,1024]{2,1,0:T(8,128)(2,1)} %get-tuple-element.91.p_mem, bf16[512,1024]{1,0:T(8,128)(2,1)} %get-tuple-element.108.datt, ...), custom_call_target="tpu_custom_call" | custom-call | flops 4294967296 | bytes 25165824 | tf_op jit(solution)/shard_map/attend_back/pallas_call | solution.py:483
  295.9 8.4 %collective-permute-done.28 = bf16[2,2,480,256]{3,2,1,0:T(8,128)(2,1)} collective-permute-done((bf16[2,2,480,256]{3,2,1,0:T(8,128)(2,1)}, bf16[2,2,480,256]{3,2,1,0:T(8,128)(2,1)}, u32[]{:S(2)}, u32[]{:S(2)}) %collective-permute-start.28) | collective-permute-done | bytes 983072 | tf_op jit(solution)/shard_map/ppermute | solution.py:57
  304.4 2.6 collective-permute-done.29
  306.9 2.3 fusion.6
  309.3 8.5 %project_grads.1 = (bf16[2,4,2,96,1024]{4,3,2,1,0:T(8,128)(2,1)}, bf16[2,4,2,96,1024]{4,3,2,1,0:T(8,128)(2,1)}) custom-call(bf16[512,1024]{1,0:T(8,128)(2,1)} %get-tuple-element.113.normed_ref, bf16[512,1024]{1,0:T(8,128)(2,1)} %get-tuple-element.121.dq, bf16[512,1024]{1,0:T(8,128)(2,1)} %get-tuple-element.114.dk, bf16[512,1024]{1,0:T(8,128)(2,1)} %get-tuple-element.115.dv), custom_call_target="tpu_custom_call" | custom-call | flops 1048576 | bytes 25165824 | tf_op jit(solution)/shard_map/project_grads/pallas_call | solution.py:522
  319.5 18.5 %collective-permute-done.30 = bf16[2,480,256]{2,1,0:T(8,128)(2,1)S(1)} collective-permute-done((bf16[2,480,256]{2,1,0:T(8,128)(2,1)}, bf16[2,480,256]{2,1,0:T(8,128)(2,1)S(1)}, u32[]{:S(2)}, u32[]{:S(2)}) %collective-permute-start.30) | collective-permute-done | bytes 491552 | tf_op jit(solution)/shard_map/ppermute | solution.py:57
  338.0 1.6 fusion.3
  340.5 2.9 collective-permute-start.38
  343.4 1.4 collective-permute-start.39
  345.6 10.8 %project_back.1 = f32[512,1024]{1,0:T(8,128)} custom-call(bf16[512,1024]{1,0:T(8,128)(2,1)} %bitcast.177, f32[512,1024]{1,0:T(8,128)} %get-tuple-element.104.dmix_ref, f32[2,1024]{1,0:T(2,128)} %get-tuple-element.95.gains_ref, bf16[512,1024]{1,0:T(8,128)(2,1)} %get-tuple-element.121.dq, bf16[512,1024]{1,0:T(8,128)(2,1)} %get-tuple-element.114.dk, ...), custom_call_target="tpu_custom_call" | custom-call | flops 1048576 | bytes 25165824 | tf_op jit(solution)/shard_map/project_back/pallas_call | solution.py:562
  357.7 4.7 %add_convert_fusion.1 = bf16[2,4,2,96,1024]{4,3,2,1,0:T(8,128)(2,1)S(1)} fusion(bf16[2,4,2,96,1024]{4,3,2,1,0:T(8,128)(2,1)} %collective-permute-done.32, bf16[2,4,2,96,1024]{4,3,2,1,0:T(8,128)(2,1)} %get-tuple-element.124), kind=kLoop, calls=%fused_computation.6 | loop fusion | flops 6291456 | bytes 9437184 | tf_op jit(solution)/shard_map/convert_element_type | solution.py:578
  365.6 2.0 add_convert_fusion.2
  369.0 4.0 collective-permute-start.40
  373.0 2.0 collective-permute-start.41
  376.4 1.5 slice_bitcast_fusion.1
  377.9 5.1 %collective-permute-done.33 = bf16[2,2,96,1024]{3,2,1,0:T(8,128)(2,1)} collective-permute-done((bf16[2,2,96,1024]{3,2,1,0:T(8,128)(2,1)}, bf16[2,2,96,1024]{3,2,1,0:T(8,128)(2,1)}, u32[]{:S(2)}, u32[]{:S(2)}) %collective-permute-start.33) | collective-permute-done | bytes 786464 | tf_op jit(solution)/shard_map/ppermute | solution.py:57
  386.1 2.1 collective-permute-done.40
  388.2 1.7 collective-permute-start.51
  389.9 10.7 %collective-permute-done.41 = bf16[2,32,2816]{2,1,0:T(8,128)(2,1)S(1)} collective-permute-done((bf16[2,32,2816]{2,1,0:T(8,128)(2,1)S(1)}, bf16[2,32,2816]{2,1,0:T(8,128)(2,1)S(1)}, u32[]{:S(2)}, u32[]{:S(2)}) %collective-permute-start.41) | collective-permute-done | bytes 360480 | tf_op jit(solution)/shard_map/ppermute | solution.py:57
  401.4 1.5 collective-permute-start.36
  403.0 1.9 fusion.16
  404.9 6.5 %collective-permute-done.35 = bf16[2,96,1024]{2,1,0:T(8,128)(2,1)S(1)} collective-permute-done((bf16[2,96,1024]{2,1,0:T(8,128)(2,1)S(1)}, bf16[2,96,1024]{2,1,0:T(8,128)(2,1)S(1)}, u32[]{:S(2)}, u32[]{:S(2)}) %collective-permute-start.35) | collective-permute-done | bytes 393248 | tf_op jit(solution)/shard_map/ppermute | solution.py:57
  411.4 1.5 collective-permute-start.52
  413.4 1.5 fusion.13
  415.0 5.8 %collective-permute-start.44 = (bf16[96,1024]{1,0:T(8,128)(2,1)S(1)}, bf16[96,1024]{1,0:T(8,128)(2,1)S(1)}, u32[]{:S(2)}, u32[]{:S(2)}) collective-permute-start(bf16[96,1024]{1,0:T(8,128)(2,1)S(1)} %get-tuple-element.211), channel_id=1, source_target_pairs={{0,4},{1,5},{2,6},{3,7},{4,0},{5,1},{6,2},{7,3},{8,12},{9,13},{10,... | collective-permute-start | bytes 589832 | tf_op jit(solution)/shard_map/ppermute | solution.py:57
  423.4 9.4 %collective-permute-done.44 = bf16[96,1024]{1,0:T(8,128)(2,1)S(1)} collective-permute-done((bf16[96,1024]{1,0:T(8,128)(2,1)S(1)}, bf16[96,1024]{1,0:T(8,128)(2,1)S(1)}, u32[]{:S(2)}, u32[]{:S(2)}) %collective-permute-start.44) | collective-permute-done | bytes 196640 | tf_op jit(solution)/shard_map/ppermute | solution.py:57
  432.8 1.7 collective-permute-start.54
  439.0 1.5 collective-permute-start.46
  441.1 1.4 collective-permute-start.48
  442.6 1.8 collective-permute-done.54
  (227 shorter events, 64.5 us)
Async XLA Ops:
  7.2 204.6 %all-gather.3.cloned.1.call-start = ((), (), s32[]{:S(2)}) async-start(), calls=%async_computation.5 | async-start | bytes 12976128 | tf_op jit(solution)/shard_map/all_gather | solution.py:683
  8.4 18.6 %collective-permute-start = (bf16[32,5632]{1,0:T(8,128)(2,1)S(1)}, bf16[32,5632]{1,0:T(8,128)(2,1)}, u32[]{:S(2)}, u32[]{:S(2)}) collective-permute-start(bf16[32,5632]{1,0:T(8,128)(2,1)S(1)} %pad_maximum_fusion.9), channel_id=1, source_target_pairs={{0,2},{1,3},{2,0},{3,1},{4,6},{5,7},{6,4},{7,5},{8,10},{9,11},{10,... | collective-permute-start | bytes 1081352 | tf_op jit(solution)/shard_map/ppermute | solution.py:57
  11.5 27.8 %collective-permute-start.1 = (bf16[32,5632]{1,0:T(8,128)(2,1)S(1)}, bf16[32,5632]{1,0:T(8,128)(2,1)}, u32[]{:S(2)}, u32[]{:S(2)}) collective-permute-start(bf16[32,5632]{1,0:T(8,128)(2,1)S(1)} %pad_maximum_fusion.9), channel_id=1, source_target_pairs={{0,4},{1,5},{2,6},{3,7},{4,0},{5,1},{6,2},{7,3},{8,12},{9,13},{10,... | collective-permute-start | bytes 1081352 | tf_op jit(solution)/shard_map/ppermute | solution.py:57
  14.1 25.2 %collective-permute-start.2 = (bf16[32,5632]{1,0:T(8,128)(2,1)S(1)}, bf16[32,5632]{1,0:T(8,128)(2,1)}, u32[]{:S(2)}, u32[]{:S(2)}) collective-permute-start(bf16[32,5632]{1,0:T(8,128)(2,1)S(1)} %pad_maximum_fusion.9), channel_id=1, source_target_pairs={{0,6},{1,7},{2,4},{3,5},{4,2},{5,3},{6,0},{7,1},{8,14},{9,15},{10,... | collective-permute-start | bytes 1081352 | tf_op jit(solution)/shard_map/ppermute | solution.py:57
  20.1 29.7 %copy-start.23 = (bf16[400,256]{1,0:T(8,128)(2,1)}, bf16[400,256]{1,0:T(8,128)(2,1)S(1)}, u32[]{:S(2)}) copy-start(bf16[400,256]{1,0:T(8,128)(2,1)S(1)} %pad_maximum_fusion.13) | copy-start | bytes 614404
  41.8 13.6 %collective-permute-start.3 = (bf16[400,256]{1,0:T(8,128)(2,1)S(1)}, bf16[400,256]{1,0:T(8,128)(2,1)S(1)}, u32[]{:S(2)}, u32[]{:S(2)}) collective-permute-start(bf16[400,256]{1,0:T(8,128)(2,1)S(1)} %pad_maximum_fusion.13), channel_id=1, source_target_pairs={{0,2},{1,3},{2,0},{3,1},{4,6},{5,7},{6,4},{7,5},{8,10},{9,11},{10,... | collective-permute-start | bytes 614408 | tf_op jit(solution)/shard_map/ppermute | solution.py:57
  48.8 17.3 %collective-permute-start.4 = (bf16[400,256]{1,0:T(8,128)(2,1)S(1)}, bf16[400,256]{1,0:T(8,128)(2,1)S(1)}, u32[]{:S(2)}, u32[]{:S(2)}) collective-permute-start(bf16[400,256]{1,0:T(8,128)(2,1)S(1)} %pad_maximum_fusion.13), channel_id=1, source_target_pairs={{0,4},{1,5},{2,6},{3,7},{4,0},{5,1},{6,2},{7,3},{8,12},{9,13},{10,... | collective-permute-start | bytes 614408 | tf_op jit(solution)/shard_map/ppermute | solution.py:57
  49.9 16.2 %collective-permute-start.5 = (bf16[400,256]{1,0:T(8,128)(2,1)S(1)}, bf16[400,256]{1,0:T(8,128)(2,1)S(1)}, u32[]{:S(2)}, u32[]{:S(2)}) collective-permute-start(bf16[400,256]{1,0:T(8,128)(2,1)S(1)} %pad_maximum_fusion.13), channel_id=1, source_target_pairs={{0,6},{1,7},{2,4},{3,5},{4,2},{5,3},{6,0},{7,1},{8,14},{9,15},{10,... | collective-permute-start | bytes 614408 | tf_op jit(solution)/shard_map/ppermute | solution.py:57
  51.2 43.3 %copy-start.24 = (bf16[400,256]{1,0:T(8,128)(2,1)S(1)}, bf16[400,256]{1,0:T(8,128)(2,1)}, u32[]{:S(2)}) copy-start(bf16[400,256]{1,0:T(8,128)(2,1)} %copy-done.23) | copy-start | bytes 614404
  55.4 39.1 %copy-start.36 = (bf16[400,256]{1,0:T(8,128)(2,1)}, bf16[400,256]{1,0:T(8,128)(2,1)S(1)}, u32[]{:S(2)}) copy-start(bf16[400,256]{1,0:T(8,128)(2,1)S(1)} %collective-permute-done.3) | copy-start | bytes 614404
  66.1 10.2 %collective-permute-start.15 = (bf16[480,256]{1,0:T(8,128)(2,1)S(1)}, bf16[480,256]{1,0:T(8,128)(2,1)S(1)}, u32[]{:S(2)}, u32[]{:S(2)}) collective-permute-start(bf16[480,256]{1,0:T(8,128)(2,1)S(1)} %pad_maximum_fusion.12), channel_id=1, source_target_pairs={{0,2},{1,3},{2,0},{3,1},{4,6},{5,7},{6,4},{7,5},{8,10},{9,11},{10,... | collective-permute-start | bytes 737288 | tf_op jit(solution)/shard_map/ppermute | solution.py:57
  68.8 19.7 %collective-permute-start.16 = (bf16[480,256]{1,0:T(8,128)(2,1)S(1)}, bf16[480,256]{1,0:T(8,128)(2,1)S(1)}, u32[]{:S(2)}, u32[]{:S(2)}) collective-permute-start(bf16[480,256]{1,0:T(8,128)(2,1)S(1)} %pad_maximum_fusion.12), channel_id=1, source_target_pairs={{0,4},{1,5},{2,6},{3,7},{4,0},{5,1},{6,2},{7,3},{8,12},{9,13},{10,... | collective-permute-start | bytes 737288 | tf_op jit(solution)/shard_map/ppermute | solution.py:57
  69.8 19.4 %collective-permute-start.17 = (bf16[480,256]{1,0:T(8,128)(2,1)S(1)}, bf16[480,256]{1,0:T(8,128)(2,1)}, u32[]{:S(2)}, u32[]{:S(2)}) collective-permute-start(bf16[480,256]{1,0:T(8,128)(2,1)S(1)} %pad_maximum_fusion.12), channel_id=1, source_target_pairs={{0,6},{1,7},{2,4},{3,5},{4,2},{5,3},{6,0},{7,1},{8,14},{9,15},{10,... | collective-permute-start | bytes 737288 | tf_op jit(solution)/shard_map/ppermute | solution.py:57
  89.2 54.4 %all-to-all-start = ((bf16[8,128,1024]{2,1,0:T(8,128)(2,1)}), bf16[8,128,1024]{2,1,0:T(8,128)(2,1)S(1)}, u32[]{:S(2)}, u32[]{:S(2)}) async-start(bf16[8,128,1024]{2,1,0:T(8,128)(2,1)} %get-tuple-element.89), calls=%async_computation | async-start | bytes 4194304 | tf_op jit(solution)/shard_map/all_to_all | solution.py:700
  95.8 53.5 %copy-start.12 = (bf16[4,400,256]{2,1,0:T(8,128)(2,1)}, bf16[4,400,256]{2,1,0:T(8,128)(2,1)S(1)}, u32[]{:S(2)}) copy-start(bf16[4,400,256]{2,1,0:T(8,128)(2,1)S(1)} %pad_maximum_fusion.7.refs_0_) | copy-start | bytes 2457604
  95.8 34.7 %collective-permute-start.6 = (bf16[4,400,256]{2,1,0:T(8,128)(2,1)S(1)}, bf16[4,400,256]{2,1,0:T(8,128)(2,1)S(1)}, u32[]{:S(2)}, u32[]{:S(2)}) collective-permute-start(bf16[4,400,256]{2,1,0:T(8,128)(2,1)S(1)} %pad_maximum_fusion.7.refs_0_), channel_id=1, source_target_pairs={{0,8},{8,0},{16,24},{24,16},{1,9},{9,1},{17,25},{25,17},{2,10},{10... | collective-permute-start | bytes 2457608 | tf_op jit(solution)/shard_map/ppermute | solution.py:57
  97.4 34.8 %collective-permute-start.7 = (bf16[4,400,256]{2,1,0:T(8,128)(2,1)S(1)}, bf16[4,400,256]{2,1,0:T(8,128)(2,1)S(1)}, u32[]{:S(2)}, u32[]{:S(2)}) collective-permute-start(bf16[4,400,256]{2,1,0:T(8,128)(2,1)S(1)} %pad_maximum_fusion.7.refs_0_), channel_id=1, source_target_pairs={{0,16},{8,24},{16,0},{24,8},{1,17},{9,25},{17,1},{25,9},{2,18},{10... | collective-permute-start | bytes 2457608 | tf_op jit(solution)/shard_map/ppermute | solution.py:57
  130.6 11.4 %collective-permute-start.8 = (bf16[2,400,256]{2,1,0:T(8,128)(2,1)S(1)}, bf16[2,400,256]{2,1,0:T(8,128)(2,1)S(1)}, u32[]{:S(2)}, u32[]{:S(2)}) collective-permute-start(bf16[2,400,256]{2,1,0:T(8,128)(2,1)S(1)} %slice.207), channel_id=1, source_target_pairs={{0,16},{8,24},{16,0},{24,8},{1,17},{9,25},{17,1},{25,9},{2,18},{10... | collective-permute-start | bytes 1228808 | tf_op jit(solution)/shard_map/ppermute | solution.py:57
  132.2 11.2 %collective-permute-start.9 = (bf16[2,400,256]{2,1,0:T(8,128)(2,1)S(1)}, bf16[2,400,256]{2,1,0:T(8,128)(2,1)}, u32[]{:S(2)}, u32[]{:S(2)}) collective-permute-start(bf16[2,400,256]{2,1,0:T(8,128)(2,1)S(1)} %slice.208), channel_id=1, source_target_pairs={{0,8},{8,0},{16,24},{24,16},{1,9},{9,1},{17,25},{25,17},{2,10},{10... | collective-permute-start | bytes 1228808 | tf_op jit(solution)/shard_map/ppermute | solution.py:57
  144.9 55.4 %all-to-all-start.1 = ((bf16[8,128,1024]{2,1,0:T(8,128)(2,1)}), bf16[8,128,1024]{2,1,0:T(8,128)(2,1)S(1)}, u32[]{:S(2)}, u32[]{:S(2)}) async-start(bf16[8,128,1024]{2,1,0:T(8,128)(2,1)} %get-tuple-element.94), calls=%async_computation.1 | async-start | bytes 4194304 | tf_op jit(solution)/shard_map/all_to_all | solution.py:702
  149.2 218.4 %reduce-scatter.2.cloned.1.call-start = ((), (), s32[]{:S(2)}) async-start(), calls=%async_computation.4 | async-start | bytes 12976128 | tf_op jit(solution)/shard_map/reduce_scatter | solution.py:727
  149.3 6.4 %collective-permute-start.10 = (bf16[4,400,256]{2,1,0:T(8,128)(2,1)S(1)}, bf16[4,400,256]{2,1,0:T(8,128)(2,1)}, u32[]{:S(2)}, u32[]{:S(2)}) collective-permute-start(bf16[4,400,256]{2,1,0:T(8,128)(2,1)S(1)} %pad_maximum_fusion.7.refs_0_), channel_id=1, source_target_pairs={{0,1},{1,0},{2,3},{3,2},{4,5},{5,4},{6,7},{7,6},{8,9},{9,8},{10,11... | collective-permute-start | bytes 2457608 | tf_op jit(solution)/shard_map/ppermute | solution.py:57
  149.8 7.4 %collective-permute-start.13 = (bf16[2,400,256]{2,1,0:T(8,128)(2,1)}, bf16[2,400,256]{2,1,0:T(8,128)(2,1)}, u32[]{:S(2)}, u32[]{:S(2)}) collective-permute-start(bf16[2,400,256]{2,1,0:T(8,128)(2,1)} %copy-done.27), channel_id=1, source_target_pairs={{0,1},{1,0},{2,3},{3,2},{4,5},{5,4},{6,7},{7,6},{8,9},{9,8},{10,11... | collective-permute-start | bytes 1228808 | tf_op jit(solution)/shard_map/ppermute | solution.py:57
  151.2 8.9 %collective-permute-start.11 = (bf16[4,400,256]{2,1,0:T(8,128)(2,1)}, bf16[4,400,256]{2,1,0:T(8,128)(2,1)S(1)}, u32[]{:S(2)}, u32[]{:S(2)}) collective-permute-start(bf16[4,400,256]{2,1,0:T(8,128)(2,1)} %copy-done.18), channel_id=1, source_target_pairs={{0,1},{1,0},{2,3},{3,2},{4,5},{5,4},{6,7},{7,6},{8,9},{9,8},{10,11... | collective-permute-start | bytes 2457608 | tf_op jit(solution)/shard_map/ppermute | solution.py:57
  151.7 8.4 %collective-permute-start.12 = (bf16[4,400,256]{2,1,0:T(8,128)(2,1)}, bf16[4,400,256]{2,1,0:T(8,128)(2,1)S(1)}, u32[]{:S(2)}, u32[]{:S(2)}) collective-permute-start(bf16[4,400,256]{2,1,0:T(8,128)(2,1)} %copy-done.19), channel_id=1, source_target_pairs={{0,1},{1,0},{2,3},{3,2},{4,5},{5,4},{6,7},{7,6},{8,9},{9,8},{10,11... | collective-permute-start | bytes 2457608 | tf_op jit(solution)/shard_map/ppermute | solution.py:57
  154.9 29.7 %collective-permute-start.18 = (bf16[4,480,256]{2,1,0:T(8,128)(2,1)}, bf16[4,480,256]{2,1,0:T(8,128)(2,1)}, u32[]{:S(2)}, u32[]{:S(2)}) collective-permute-start(bf16[4,480,256]{2,1,0:T(8,128)(2,1)} %pad_maximum_fusion.5.refs_0_), channel_id=1, source_target_pairs={{0,8},{8,0},{16,24},{24,16},{1,9},{9,1},{17,25},{25,17},{2,10},{10... | collective-permute-start | bytes 2949128 | tf_op jit(solution)/shard_map/ppermute | solution.py:57
  155.7 28.9 %collective-permute-start.19 = (bf16[4,480,256]{2,1,0:T(8,128)(2,1)}, bf16[4,480,256]{2,1,0:T(8,128)(2,1)S(1)}, u32[]{:S(2)}, u32[]{:S(2)}) collective-permute-start(bf16[4,480,256]{2,1,0:T(8,128)(2,1)} %pad_maximum_fusion.5.refs_0_), channel_id=1, source_target_pairs={{0,16},{8,24},{16,0},{24,8},{1,17},{9,25},{17,1},{25,9},{2,18},{10... | collective-permute-start | bytes 2949128 | tf_op jit(solution)/shard_map/ppermute | solution.py:57
  157.2 2.9 collective-permute-start.14
  186.0 13.8 %collective-permute-start.20 = (bf16[2,480,256]{2,1,0:T(8,128)(2,1)S(1)}, bf16[2,480,256]{2,1,0:T(8,128)(2,1)}, u32[]{:S(2)}, u32[]{:S(2)}) collective-permute-start(bf16[2,480,256]{2,1,0:T(8,128)(2,1)S(1)} %slice.147), channel_id=1, source_target_pairs={{0,16},{8,24},{16,0},{24,8},{1,17},{9,25},{17,1},{25,9},{2,18},{10... | collective-permute-start | bytes 1474568 | tf_op jit(solution)/shard_map/ppermute | solution.py:57
  186.6 13.5 %collective-permute-start.21 = (bf16[2,480,256]{2,1,0:T(8,128)(2,1)S(1)}, bf16[2,480,256]{2,1,0:T(8,128)(2,1)}, u32[]{:S(2)}, u32[]{:S(2)}) collective-permute-start(bf16[2,480,256]{2,1,0:T(8,128)(2,1)S(1)} %slice.148), channel_id=1, source_target_pairs={{0,8},{8,0},{16,24},{24,16},{1,9},{9,1},{17,25},{25,17},{2,10},{10... | collective-permute-start | bytes 1474568 | tf_op jit(solution)/shard_map/ppermute | solution.py:57
  188.0 23.8 %collective-permute-start.22 = (bf16[4,480,256]{2,1,0:T(8,128)(2,1)}, bf16[4,480,256]{2,1,0:T(8,128)(2,1)}, u32[]{:S(2)}, u32[]{:S(2)}) collective-permute-start(bf16[4,480,256]{2,1,0:T(8,128)(2,1)} %pad_maximum_fusion.5.refs_0_), channel_id=1, source_target_pairs={{0,1},{1,0},{2,3},{3,2},{4,5},{5,4},{6,7},{7,6},{8,9},{9,8},{10,11... | collective-permute-start | bytes 2949128 | tf_op jit(solution)/shard_map/ppermute | solution.py:57
  188.0 23.8 %collective-permute-start.23 = (bf16[4,480,256]{2,1,0:T(8,128)(2,1)}, bf16[4,480,256]{2,1,0:T(8,128)(2,1)}, u32[]{:S(2)}, u32[]{:S(2)}) collective-permute-start(bf16[4,480,256]{2,1,0:T(8,128)(2,1)} %collective-permute-done.18.refs_1_), channel_id=1, source_target_pairs={{0,1},{1,0},{2,3},{3,2},{4,5},{5,4},{6,7},{7,6},{8,9},{9,8},{10,11... | collective-permute-start | bytes 2949128 | tf_op jit(solution)/shard_map/ppermute | solution.py:57
  188.5 23.3 %collective-permute-start.24 = (bf16[4,480,256]{2,1,0:T(8,128)(2,1)S(1)}, bf16[4,480,256]{2,1,0:T(8,128)(2,1)}, u32[]{:S(2)}, u32[]{:S(2)}) collective-permute-start(bf16[4,480,256]{2,1,0:T(8,128)(2,1)S(1)} %collective-permute-done.19.refs_2_), channel_id=1, source_target_pairs={{0,1},{1,0},{2,3},{3,2},{4,5},{5,4},{6,7},{7,6},{8,9},{9,8},{10,11... | collective-permute-start | bytes 2949128 | tf_op jit(solution)/shard_map/ppermute | solution.py:57
  199.8 11.9 %collective-permute-start.25 = (bf16[2,480,256]{2,1,0:T(8,128)(2,1)}, bf16[2,480,256]{2,1,0:T(8,128)(2,1)}, u32[]{:S(2)}, u32[]{:S(2)}) collective-permute-start(bf16[2,480,256]{2,1,0:T(8,128)(2,1)} %collective-permute-done.20.refs_3_), channel_id=1, source_target_pairs={{0,1},{1,0},{2,3},{3,2},{4,5},{5,4},{6,7},{7,6},{8,9},{9,8},{10,11... | collective-permute-start | bytes 1474568 | tf_op jit(solution)/shard_map/ppermute | solution.py:57
  200.2 11.6 %collective-permute-start.26 = (bf16[2,480,256]{2,1,0:T(8,128)(2,1)}, bf16[2,480,256]{2,1,0:T(8,128)(2,1)}, u32[]{:S(2)}, u32[]{:S(2)}) collective-permute-start(bf16[2,480,256]{2,1,0:T(8,128)(2,1)} %collective-permute-done.21.refs_4_), channel_id=1, source_target_pairs={{0,1},{1,0},{2,3},{3,2},{4,5},{5,4},{6,7},{7,6},{8,9},{9,8},{10,11... | collective-permute-start | bytes 1474568 | tf_op jit(solution)/shard_map/ppermute | solution.py:57
  257.0 7.1 %collective-permute-start.27 = (bf16[2,4,2,480,256]{4,3,2,1,0:T(8,128)(2,1)}, bf16[2,4,2,480,256]{4,3,2,1,0:T(8,128)(2,1)S(1)}, u32[]{:S(2)}, u32[]{:S(2)}) collective-permute-start(bf16[2,4,2,480,256]{4,3,2,1,0:T(8,128)(2,1)} %get-tuple-element.107), channel_id=1, source_target_pairs={{0,1},{1,0},{2,3},{3,2},{4,5},{5,4},{6,7},{7,6},{8,9},{9,8},{10,11... | collective-permute-start | bytes 11796488 | tf_op jit(solution)/shard_map/ppermute | solution.py:57
  271.2 33.2 %collective-permute-start.28 = (bf16[2,2,480,256]{3,2,1,0:T(8,128)(2,1)}, bf16[2,2,480,256]{3,2,1,0:T(8,128)(2,1)}, u32[]{:S(2)}, u32[]{:S(2)}) collective-permute-start(bf16[2,2,480,256]{3,2,1,0:T(8,128)(2,1)} %get-tuple-element.192), channel_id=1, source_target_pairs={{0,16},{8,24},{16,0},{24,8},{1,17},{9,25},{17,1},{25,9},{2,18},{10... | collective-permute-start | bytes 2949128 | tf_op jit(solution)/shard_map/ppermute | solution.py:57
  272.7 34.3 %collective-permute-start.29 = (bf16[2,2,480,256]{3,2,1,0:T(8,128)(2,1)}, bf16[2,2,480,256]{3,2,1,0:T(8,128)(2,1)}, u32[]{:S(2)}, u32[]{:S(2)}) collective-permute-start(bf16[2,2,480,256]{3,2,1,0:T(8,128)(2,1)} %get-tuple-element.191), channel_id=1, source_target_pairs={{0,8},{8,0},{16,24},{24,16},{1,9},{9,1},{17,25},{25,17},{2,10},{10... | collective-permute-start | bytes 2949128 | tf_op jit(solution)/shard_map/ppermute | solution.py:57
  275.0 81.4 %all-to-all-start.2 = ((bf16[8,2,64,1024]{3,2,1,0:T(8,128)(2,1)}), bf16[8,2,64,1024]{3,2,1,0:T(8,128)(2,1)S(1)}, u32[]{:S(2)}, u32[]{:S(2)}) async-start(bf16[8,2,64,1024]{3,2,1,0:T(8,128)(2,1)} %pad_maximum_fusion.2), calls=%async_computation.2 | async-start | bytes 4194304 | tf_op jit(solution)/shard_map/all_to_all | solution.py:714
  317.8 39.9 %collective-permute-start.32 = (bf16[2,4,2,96,1024]{4,3,2,1,0:T(8,128)(2,1)}, bf16[2,4,2,96,1024]{4,3,2,1,0:T(8,128)(2,1)}, u32[]{:S(2)}, u32[]{:S(2)}) collective-permute-start(bf16[2,4,2,96,1024]{4,3,2,1,0:T(8,128)(2,1)} %get-tuple-element.117), channel_id=1, source_target_pairs={{0,1},{1,0},{2,3},{3,2},{4,5},{5,4},{6,7},{7,6},{8,9},{9,8},{10,11... | collective-permute-start | bytes 9437192 | tf_op jit(solution)/shard_map/ppermute | solution.py:57
  317.8 20.2 %collective-permute-start.30 = (bf16[2,480,256]{2,1,0:T(8,128)(2,1)}, bf16[2,480,256]{2,1,0:T(8,128)(2,1)S(1)}, u32[]{:S(2)}, u32[]{:S(2)}) collective-permute-start(bf16[2,480,256]{2,1,0:T(8,128)(2,1)} %get-tuple-element.190), channel_id=1, source_target_pairs={{0,8},{8,0},{16,24},{24,16},{1,9},{9,1},{17,25},{25,17},{2,10},{10... | collective-permute-start | bytes 1474568 | tf_op jit(solution)/shard_map/ppermute | solution.py:57
  318.9 19.2 %collective-permute-start.31 = (bf16[2,480,256]{2,1,0:T(8,128)(2,1)}, bf16[2,480,256]{2,1,0:T(8,128)(2,1)S(1)}, u32[]{:S(2)}, u32[]{:S(2)}) collective-permute-start(bf16[2,480,256]{2,1,0:T(8,128)(2,1)} %get-tuple-element.189), channel_id=1, source_target_pairs={{0,16},{8,24},{16,0},{24,8},{1,17},{9,25},{17,1},{25,9},{2,18},{10... | collective-permute-start | bytes 1474568 | tf_op jit(solution)/shard_map/ppermute | solution.py:57
  340.5 21.9 %collective-permute-start.38 = (bf16[480,256]{1,0:T(8,128)(2,1)}, bf16[480,256]{1,0:T(8,128)(2,1)}, u32[]{:S(2)}, u32[]{:S(2)}) collective-permute-start(bf16[480,256]{1,0:T(8,128)(2,1)} %get-tuple-element.210), channel_id=1, source_target_pairs={{0,4},{1,5},{2,6},{3,7},{4,0},{5,1},{6,2},{7,3},{8,12},{9,13},{10,... | collective-permute-start | bytes 737288 | tf_op jit(solution)/shard_map/ppermute | solution.py:57
  343.4 19.1 %collective-permute-start.39 = (bf16[480,256]{1,0:T(8,128)(2,1)}, bf16[480,256]{1,0:T(8,128)(2,1)}, u32[]{:S(2)}, u32[]{:S(2)}) collective-permute-start(bf16[480,256]{1,0:T(8,128)(2,1)} %get-tuple-element.209), channel_id=1, source_target_pairs={{0,6},{1,7},{2,4},{3,5},{4,2},{5,3},{6,0},{7,1},{8,14},{9,15},{10,... | collective-permute-start | bytes 737288 | tf_op jit(solution)/shard_map/ppermute | solution.py:57
  345.6 16.9 %collective-permute-start.37 = (bf16[480,256]{1,0:T(8,128)(2,1)}, bf16[480,256]{1,0:T(8,128)(2,1)}, u32[]{:S(2)}, u32[]{:S(2)}) collective-permute-start(bf16[480,256]{1,0:T(8,128)(2,1)} %slice_bitcast_fusion.20), channel_id=1, source_target_pairs={{0,2},{1,3},{2,0},{3,1},{4,6},{5,7},{6,4},{7,5},{8,10},{9,11},{10,... | collective-permute-start | bytes 737288 | tf_op jit(solution)/shard_map/ppermute | solution.py:57
  363.8 19.1 %collective-permute-start.33 = (bf16[2,2,96,1024]{3,2,1,0:T(8,128)(2,1)}, bf16[2,2,96,1024]{3,2,1,0:T(8,128)(2,1)}, u32[]{:S(2)}, u32[]{:S(2)}) collective-permute-start(bf16[2,2,96,1024]{3,2,1,0:T(8,128)(2,1)} %get-tuple-element.198), channel_id=1, source_target_pairs={{0,16},{8,24},{16,0},{24,8},{1,17},{9,25},{17,1},{25,9},{2,18},{10... | collective-permute-start | bytes 2359304 | tf_op jit(solution)/shard_map/ppermute | solution.py:57
  364.3 19.2 %collective-permute-start.34 = (bf16[2,2,96,1024]{3,2,1,0:T(8,128)(2,1)}, bf16[2,2,96,1024]{3,2,1,0:T(8,128)(2,1)}, u32[]{:S(2)}, u32[]{:S(2)}) collective-permute-start(bf16[2,2,96,1024]{3,2,1,0:T(8,128)(2,1)} %get-tuple-element.197), channel_id=1, source_target_pairs={{0,8},{8,0},{16,24},{24,16},{1,9},{9,1},{17,25},{25,17},{2,10},{10... | collective-permute-start | bytes 2359304 | tf_op jit(solution)/shard_map/ppermute | solution.py:57
  369.0 19.2 %collective-permute-start.40 = (bf16[2,32,2816]{2,1,0:T(8,128)(2,1)S(1)}, bf16[2,32,2816]{2,1,0:T(8,128)(2,1)S(1)}, u32[]{:S(2)}, u32[]{:S(2)}) collective-permute-start(bf16[2,32,2816]{2,1,0:T(8,128)(2,1)S(1)} %get-tuple-element.208), channel_id=1, source_target_pairs={{0,2},{1,3},{2,0},{3,1},{4,6},{5,7},{6,4},{7,5},{8,10},{9,11},{10,... | collective-permute-start | bytes 1081352 | tf_op jit(solution)/shard_map/ppermute | solution.py:57
  373.0 27.7 %collective-permute-start.41 = (bf16[2,32,2816]{2,1,0:T(8,128)(2,1)S(1)}, bf16[2,32,2816]{2,1,0:T(8,128)(2,1)S(1)}, u32[]{:S(2)}, u32[]{:S(2)}) collective-permute-start(bf16[2,32,2816]{2,1,0:T(8,128)(2,1)S(1)} %get-tuple-element.207), channel_id=1, source_target_pairs={{0,4},{1,5},{2,6},{3,7},{4,0},{5,1},{6,2},{7,3},{8,12},{9,13},{10,... | collective-permute-start | bytes 1081352 | tf_op jit(solution)/shard_map/ppermute | solution.py:57
  375.0 26.4 %collective-permute-start.42 = (bf16[2,32,2816]{2,1,0:T(8,128)(2,1)S(1)}, bf16[2,32,2816]{2,1,0:T(8,128)(2,1)S(1)}, u32[]{:S(2)}, u32[]{:S(2)}) collective-permute-start(bf16[2,32,2816]{2,1,0:T(8,128)(2,1)S(1)} %get-tuple-element.206), channel_id=1, source_target_pairs={{0,6},{1,7},{2,4},{3,5},{4,2},{5,3},{6,0},{7,1},{8,14},{9,15},{10,... | collective-permute-start | bytes 1081352 | tf_op jit(solution)/shard_map/ppermute | solution.py:57
  382.9 32.1 %collective-permute-start.49 = (bf16[480,256]{1,0:T(8,128)(2,1)}, bf16[480,256]{1,0:T(8,128)(2,1)S(1)}, u32[]{:S(2)}, u32[]{:S(2)}) collective-permute-start(bf16[480,256]{1,0:T(8,128)(2,1)} %add_convert_fusion.2), channel_id=1, source_target_pairs={{0,8},{8,0},{16,24},{24,16},{1,9},{9,1},{17,25},{25,17},{2,10},{10... | collective-permute-start | bytes 737288 | tf_op jit(solution)/shard_map/ppermute | solution.py:57
  383.5 37.3 %collective-permute-start.50 = (bf16[480,256]{1,0:T(8,128)(2,1)}, bf16[480,256]{1,0:T(8,128)(2,1)S(1)}, u32[]{:S(2)}, u32[]{:S(2)}) collective-permute-start(bf16[480,256]{1,0:T(8,128)(2,1)} %add_convert_fusion.2), channel_id=1, source_target_pairs={{0,16},{8,24},{16,0},{24,8},{1,17},{9,25},{17,1},{25,9},{2,18},{10... | collective-permute-start | bytes 737288 | tf_op jit(solution)/shard_map/ppermute | solution.py:57
  388.2 33.0 %collective-permute-start.51 = (bf16[480,256]{1,0:T(8,128)(2,1)}, bf16[480,256]{1,0:T(8,128)(2,1)S(1)}, u32[]{:S(2)}, u32[]{:S(2)}) collective-permute-start(bf16[480,256]{1,0:T(8,128)(2,1)} %add_convert_fusion.2), channel_id=1, source_target_pairs={{0,24},{8,16},{16,8},{24,0},{1,25},{9,17},{17,9},{25,1},{2,26},{10... | collective-permute-start | bytes 737288 | tf_op jit(solution)/shard_map/ppermute | solution.py:57
  400.7 10.7 %collective-permute-start.35 = (bf16[2,96,1024]{2,1,0:T(8,128)(2,1)S(1)}, bf16[2,96,1024]{2,1,0:T(8,128)(2,1)S(1)}, u32[]{:S(2)}, u32[]{:S(2)}) collective-permute-start(bf16[2,96,1024]{2,1,0:T(8,128)(2,1)S(1)} %get-tuple-element.196), channel_id=1, source_target_pairs={{0,8},{8,0},{16,24},{24,16},{1,9},{9,1},{17,25},{25,17},{2,10},{10... | collective-permute-start | bytes 1179656 | tf_op jit(solution)/shard_map/ppermute | solution.py:57
  401.4 11.5 %collective-permute-start.36 = (bf16[2,96,1024]{2,1,0:T(8,128)(2,1)S(1)}, bf16[2,96,1024]{2,1,0:T(8,128)(2,1)S(1)}, u32[]{:S(2)}, u32[]{:S(2)}) collective-permute-start(bf16[2,96,1024]{2,1,0:T(8,128)(2,1)S(1)} %get-tuple-element.195), channel_id=1, source_target_pairs={{0,16},{8,24},{16,0},{24,8},{1,17},{9,25},{17,1},{25,9},{2,18},{10... | collective-permute-start | bytes 1179656 | tf_op jit(solution)/shard_map/ppermute | solution.py:57
  411.4 29.7 %collective-permute-start.52 = (bf16[2,32,2816]{2,1,0:T(8,128)(2,1)}, bf16[2,32,2816]{2,1,0:T(8,128)(2,1)}, u32[]{:S(2)}, u32[]{:S(2)}) collective-permute-start(bf16[2,32,2816]{2,1,0:T(8,128)(2,1)} %fusion.16), channel_id=1, source_target_pairs={{0,8},{8,0},{16,24},{24,16},{1,9},{9,1},{17,25},{25,17},{2,10},{10... | collective-permute-start | bytes 1081352 | tf_op jit(solution)/shard_map/ppermute | solution.py:57
  412.9 29.6 %collective-permute-start.53 = (bf16[2,32,2816]{2,1,0:T(8,128)(2,1)}, bf16[2,32,2816]{2,1,0:T(8,128)(2,1)}, u32[]{:S(2)}, u32[]{:S(2)}) collective-permute-start(bf16[2,32,2816]{2,1,0:T(8,128)(2,1)} %fusion.16), channel_id=1, source_target_pairs={{0,16},{8,24},{16,0},{24,8},{1,17},{9,25},{17,1},{25,9},{2,18},{10... | collective-permute-start | bytes 1081352 | tf_op jit(solution)/shard_map/ppermute | solution.py:57
  415.0 17.8 %collective-permute-start.44 = (bf16[96,1024]{1,0:T(8,128)(2,1)S(1)}, bf16[96,1024]{1,0:T(8,128)(2,1)S(1)}, u32[]{:S(2)}, u32[]{:S(2)}) collective-permute-start(bf16[96,1024]{1,0:T(8,128)(2,1)S(1)} %get-tuple-element.211), channel_id=1, source_target_pairs={{0,4},{1,5},{2,6},{3,7},{4,0},{5,1},{6,2},{7,3},{8,12},{9,13},{10,... | collective-permute-start | bytes 589832 | tf_op jit(solution)/shard_map/ppermute | solution.py:57
  420.8 16.3 %collective-permute-start.45 = (bf16[96,1024]{1,0:T(8,128)(2,1)S(1)}, bf16[96,1024]{1,0:T(8,128)(2,1)S(1)}, u32[]{:S(2)}, u32[]{:S(2)}) collective-permute-start(bf16[96,1024]{1,0:T(8,128)(2,1)S(1)} %get-tuple-element.212), channel_id=1, source_target_pairs={{0,6},{1,7},{2,4},{3,5},{4,2},{5,3},{6,0},{7,1},{8,14},{9,15},{10,... | collective-permute-start | bytes 589832 | tf_op jit(solution)/shard_map/ppermute | solution.py:57
  421.3 16.6 %collective-permute-start.43 = (bf16[96,1024]{1,0:T(8,128)(2,1)S(1)}, bf16[96,1024]{1,0:T(8,128)(2,1)}, u32[]{:S(2)}, u32[]{:S(2)}) collective-permute-start(bf16[96,1024]{1,0:T(8,128)(2,1)S(1)} %slice_bitcast_fusion.24), channel_id=1, source_target_pairs={{0,2},{1,3},{2,0},{3,1},{4,6},{5,7},{6,4},{7,5},{8,10},{9,11},{10,... | collective-permute-start | bytes 589832 | tf_op jit(solution)/shard_map/ppermute | solution.py:57
  432.8 11.5 %collective-permute-start.54 = (bf16[2,32,2816]{2,1,0:T(8,128)(2,1)}, bf16[2,32,2816]{2,1,0:T(8,128)(2,1)S(1)}, u32[]{:S(2)}, u32[]{:S(2)}) collective-permute-start(bf16[2,32,2816]{2,1,0:T(8,128)(2,1)} %fusion.16), channel_id=1, source_target_pairs={{0,24},{8,16},{16,8},{24,0},{1,25},{9,17},{17,9},{25,1},{2,26},{10... | collective-permute-start | bytes 1081352 | tf_op jit(solution)/shard_map/ppermute | solution.py:57
  439.0 11.9 %collective-permute-start.46 = (bf16[96,1024]{1,0:T(8,128)(2,1)S(1)}, bf16[96,1024]{1,0:T(8,128)(2,1)S(1)}, u32[]{:S(2)}, u32[]{:S(2)}) collective-permute-start(bf16[96,1024]{1,0:T(8,128)(2,1)S(1)} %add_convert_fusion.3), channel_id=1, source_target_pairs={{0,8},{8,0},{16,24},{24,16},{1,9},{9,1},{17,25},{25,17},{2,10},{10... | collective-permute-start | bytes 589832 | tf_op jit(solution)/shard_map/ppermute | solution.py:57
  440.4 10.4 %collective-permute-start.47 = (bf16[96,1024]{1,0:T(8,128)(2,1)S(1)}, bf16[96,1024]{1,0:T(8,128)(2,1)S(1)}, u32[]{:S(2)}, u32[]{:S(2)}) collective-permute-start(bf16[96,1024]{1,0:T(8,128)(2,1)S(1)} %add_convert_fusion.3), channel_id=1, source_target_pairs={{0,16},{8,24},{16,0},{24,8},{1,17},{9,25},{17,1},{25,9},{2,18},{10... | collective-permute-start | bytes 589832 | tf_op jit(solution)/shard_map/ppermute | solution.py:57
  441.1 9.7 %collective-permute-start.48 = (bf16[96,1024]{1,0:T(8,128)(2,1)S(1)}, bf16[96,1024]{1,0:T(8,128)(2,1)}, u32[]{:S(2)}, u32[]{:S(2)}) collective-permute-start(bf16[96,1024]{1,0:T(8,128)(2,1)S(1)} %add_convert_fusion.3), channel_id=1, source_target_pairs={{0,24},{8,16},{16,8},{24,0},{1,25},{9,17},{17,9},{25,1},{2,26},{10... | collective-permute-start | bytes 589832 | tf_op jit(solution)/shard_map/ppermute | solution.py:57
  (40 other events, 283.4 us)
Sparse Core Ops, SparseCore 0:
  42.0 86.8 all-gather.2
  257.2 102.8 reduce-scatter.1

commit v4 on v3

--- a/solution.py
+++ b/solution.py
@@ -243,18 +243,18 @@
     p_mem[0] = (e_mem * inverse).astype(BF16)
 
 
-def head_spec(tokens):
-    return pl.BlockSpec((tokens, HD), lambda h: (0, h))
-
-
-def memory_spec(memory):
-    return pl.BlockSpec(memory.shape[:2] + (HD,), lambda h: (0, 0, h))
-
-
-def prob_specs(tokens, keys):
+def head_spec(tokens, heads=1):
+    return pl.BlockSpec((tokens, heads * HD), lambda h: (0, h))
+
+
+def memory_spec(memory, heads=1):
+    return pl.BlockSpec(memory.shape[:2] + (heads * HD,), lambda h: (0, 0, h))
+
+
+def prob_specs(tokens, keys, heads=1):
     return [
-        pl.BlockSpec((1, tokens, tokens), lambda h: (h, 0, 0)),
-        pl.BlockSpec((1, tokens, keys), lambda h: (h, 0, 0)),
+        pl.BlockSpec((heads, tokens, tokens), lambda h: (h, 0, 0)),
+        pl.BlockSpec((heads, tokens, keys), lambda h: (h, 0, 0)),
     ]
 
 
@@ -282,7 +282,10 @@
 
 
 def attend_kernel(p_loc, p_mem, v, mem_v, out):
-    out[...] = (dot(p_loc[0], v[...]) + dot(p_mem[0], flat_rows(mem_v))).astype(BF16)
+    values = flat_rows(mem_v)
+    for i in range(2):
+        cols = slice(i * HD, (i + 1) * HD)
+        out[:, cols] = (dot(p_loc[i], v[:, cols]) + dot(p_mem[i], values[:, cols])).astype(BF16)
 
 
 def attend(p_loc, p_mem, v, mem_v):
@@ -290,9 +293,9 @@
     keys = p_mem.shape[2]
     return pl.pallas_call(
         attend_kernel,
-        grid=(width // HD,),
-        in_specs=prob_specs(tokens, keys) + [head_spec(tokens), memory_spec(mem_v)],
-        out_specs=head_spec(tokens),
+        grid=(width // HD // 2,),
+        in_specs=prob_specs(tokens, keys, 2) + [head_spec(tokens, 2), memory_spec(mem_v, 2)],
+        out_specs=head_spec(tokens, 2),
         out_shape=jax.ShapeDtypeStruct((tokens, width), BF16),
         compiler_params=pltpu.CompilerParams(vmem_limit_bytes=VMEM_LIMIT),
         cost_estimate=cost(2 * tokens * (tokens + keys) * width),
@@ -344,7 +347,7 @@
     gate = dot(normed[...], w_gate)
     up = dot(normed[...], w_up)
     back = dot_nt(ct, down)
-    sigma = 1.0 / (1.0 + jnp.exp(-gate))
+    sigma = 0.5 + 0.5 * jnp.tanh(0.5 * gate)
     swish = gate * sigma
     hidden = (swish * up).astype(BF16)
     d_gate = (back * up * (sigma * (1.0 + gate * (1.0 - sigma)))).astype(BF16)
@@ -462,18 +465,21 @@
 def attend_back_kernel(
     p_loc, p_mem, datt, att, qloc, kloc, v, mem_k, mem_v, cos_ref, sin_ref, dq_ref, dk_ref, dv_ref
 ):
-    grad = datt[...]
-    delta = jnp.sum(grad.astype(F32) * att[...].astype(F32), axis=-1, keepdims=True)
-    low_loc = p_loc[0]
-    ds_loc = (low_loc.astype(F32) * (dot_nt(grad, v[...]) - delta)).astype(BF16)
-    ds_mem = (p_mem[0].astype(F32) * (dot_nt(grad, flat_rows(mem_v)) - delta)).astype(BF16)
+    keys, values = flat_rows(mem_k), flat_rows(mem_v)
     cosine, sine = cos_ref[...], sin_ref[...]
-    dq_loc = dot(ds_loc, kloc[...]) * SCALE
-    dq_mem = dot(ds_mem, flat_rows(mem_k)) * SCALE
-    dk = dot_tn(ds_loc, qloc[...]) * SCALE
-    dq_ref[...] = (dq_mem + turn(dq_loc, cosine, -sine)).astype(BF16)
-    dk_ref[...] = turn(dk, cosine, -sine).astype(BF16)
-    dv_ref[...] = dot_tn(low_loc, grad).astype(BF16)
+    for i in range(2):
+        cols = slice(i * HD, (i + 1) * HD)
+        grad, k_loc = datt[:, cols], kloc[:, cols]
+        delta = jnp.sum(grad.astype(F32) * att[:, cols].astype(F32), axis=-1, keepdims=True)
+        low_loc = p_loc[i]
+        ds_loc = (low_loc.astype(F32) * (dot_nt(grad, v[:, cols]) - delta)).astype(BF16)
+        ds_mem = (p_mem[i].astype(F32) * (dot_nt(grad, values[:, cols]) - delta)).astype(BF16)
+        dq_loc = dot(ds_loc, k_loc) * SCALE
+        dq_mem = dot(ds_mem, keys[:, cols]) * SCALE
+        dk = dot_tn(ds_loc, qloc[:, cols]) * SCALE
+        dq_ref[:, cols] = (dq_mem + turn(dq_loc, cosine, -sine)).astype(BF16)
+        dk_ref[:, cols] = turn(dk, cosine, -sine).astype(BF16)
+        dv_ref[:, cols] = dot_tn(low_loc, grad).astype(BF16)
 
 
 def attend_back(p_loc, p_mem, datt, att, qloc, kloc, v, mem_k, mem_v, cosine, sine):
@@ -482,11 +488,11 @@
     table = pl.BlockSpec((tokens, HD), lambda h: (0, 0))
     return pl.pallas_call(
         attend_back_kernel,
-        grid=(width // HD,),
-        in_specs=prob_specs(tokens, keys)
-        + [head_spec(tokens)] * 5
-        + [memory_spec(mem_k), memory_spec(mem_v), table, table],
-        out_specs=[head_spec(tokens)] * 3,
+        grid=(width // HD // 2,),
+        in_specs=prob_specs(tokens, keys, 2)
+        + [head_spec(tokens, 2)] * 5
+        + [memory_spec(mem_k, 2), memory_spec(mem_v, 2), table, table],
+        out_specs=[head_spec(tokens, 2)] * 3,
         out_shape=[jax.ShapeDtypeStruct((tokens, width), BF16)] * 3,
         compiler_params=pltpu.CompilerParams(vmem_limit_bytes=VMEM_LIMIT),
         cost_estimate=cost(4 * tokens * (2 * tokens + keys) * width),
@@ -705,12 +711,13 @@
     p_loc, p_mem = weigh(qmem, qloc, kloc, mem_k, local_bias, memory_bias)
     if plan.fast:
         project_out = across_second(after(project_out, p_loc))
+        p_mem = after(p_mem, project_out)
         second = project_out + other_core(project_out) + [gate_up]
     attended = attend(p_loc, p_mem, v, mem_v)
 
     run = tokens // group
     fresh = jnp.stack([kraw.reshape(group, run, width), v.reshape(group, run, width)], axis=1)
-    fresh = after(fresh, attended)
+    fresh = after(fresh, (p_loc, project_out) if plan.fast else p_loc)
     arrived = lax.all_to_all(fresh, KEY, split_axis=0, concat_axis=0, tiled=True)
     new_keys = jnp.concatenate([cache_keys[:, run:], arrived[:, 0]], axis=1)
     new_values = jnp.concatenate([cache_values[:, run:], arrived[:, 1]], axis=1)
@@ -723,6 +730,7 @@
         results[1 + n_half :],
     )
     if plan.fast:
+        g_gu, g_do = after((g_gu, g_do), arrived)
         g_gu = g_gu.reshape((8,) + g_gu.shape[2:])
         g_gu = lax.psum_scatter(g_gu, ("dp", "core"), scatter_dimension=0, tiled=True)
         g_gu = lax.optimization_barrier(g_gu)

time: 470 us -> 465 us (0.989)
  the two profiles are of different devices: /device:TPU:0 before, /device:TPU:8 now
where the time goes in v4:
time: 465 us; the launch traced here: 456 us
  waiting for transfers between devices  188 us (40%)
  Pallas kernels  113 us (24%)
  starting transfers between devices  67.6 us (15%)
  other arithmetic  38.9 us (8%)
  local copies, waits for them, and re-layouts  32 us (7%)
  between operations  16 us (3%)
    ppermute x55, waiting for transfers between devices, swap(): return lax.ppermute(values, axis, [(i, i ^ distance) for i in range(size)])  188 us
    ppermute x55, starting transfers between devices, swap(): return lax.ppermute(values, axis, [(i, i ^ distance) for i in range(size)])  53.1 us
    pallas_call x1, Pallas kernels, feed(): pl.pallas_call(functools.partial(feed_kernel, plan, len(pieces)), grid=(s...  44.6 us
    pallas_call x1, Pallas kernels, attend_back(): pl.pallas_call(attend_back_kernel, grid=(width // HD // 2,), in_specs=pro...  16.9 us
    convert_element_type x9, other arithmetic, add(): return total.astype(BF16)  16.5 us
    pallas_call x1, Pallas kernels, weigh(): pl.pallas_call(weigh_kernel, grid=(width // HD,), in_specs=[head_spec(tok...  14.2 us
    unnamed x94, local copies, waits for them, and re-layouts  12.2 us
    pallas_call x1, Pallas kernels, project_back(): pl.pallas_call(functools.partial(project_back_kernel, plan, len(pieces)),...  11.7 us
  transfers between devices with their start and end apart: 60, of which 24 were waited for; matrix products, arithmetic and copies ran while one was open for 12% of the time, Pallas kernels for 25%

profile of v4, /device:TPU:8, one launch (start us, length us, event | category | flops | bytes accessed | tf_op | source)
XLA Modules:
  0.0 455.5 jit_solution(12626913036624557728)
XLA Ops:
  8.5 3.0 collective-permute-start.1
  14.0 1.8 gather_fusion.3
  19.3 2.4 pad_maximum_fusion
  21.7 1.7 collective-permute-done
  23.4 12.4 %collective-permute-done.1 = bf16[32,5632]{1,0:T(8,128)(2,1)} collective-permute-done((bf16[32,5632]{1,0:T(8,128)(2,1)S(1)}, bf16[32,5632]{1,0:T(8,128)(2,1)}, u32[]{:S(2)}, u32[]{:S(2)}) %collective-permute-start.1) | collective-permute-done | bytes 360480 | tf_op jit(solution)/shard_map/ppermute | solution.py:57
  35.9 11.7 %collective-permute-done.2 = bf16[32,5632]{1,0:T(8,128)(2,1)} collective-permute-done((bf16[32,5632]{1,0:T(8,128)(2,1)S(1)}, bf16[32,5632]{1,0:T(8,128)(2,1)}, u32[]{:S(2)}, u32[]{:S(2)}) %collective-permute-start.2) | collective-permute-done | bytes 360480 | tf_op jit(solution)/shard_map/ppermute | solution.py:57
  47.6 2.5 pad_maximum_fusion.3
  50.1 1.6 collective-permute-start.5
  51.7 1.9 collective-permute-start.3
  53.6 6.6 %collective-permute-done.5 = bf16[400,256]{1,0:T(8,128)(2,1)S(1)} collective-permute-done((bf16[400,256]{1,0:T(8,128)(2,1)S(1)}, bf16[400,256]{1,0:T(8,128)(2,1)S(1)}, u32[]{:S(2)}, u32[]{:S(2)}) %collective-permute-start.5) | collective-permute-done | bytes 204832 | tf_op jit(solution)/shard_map/ppermute | solution.py:57
  61.5 2.4 collective-permute-start.15
  65.5 5.9 %collective-permute-done.15 = bf16[480,256]{1,0:T(8,128)(2,1)S(1)} collective-permute-done((bf16[480,256]{1,0:T(8,128)(2,1)S(1)}, bf16[480,256]{1,0:T(8,128)(2,1)S(1)}, u32[]{:S(2)}, u32[]{:S(2)}) %collective-permute-start.15) | collective-permute-done | bytes 245792 | tf_op jit(solution)/shard_map/ppermute | solution.py:57
  71.4 9.0 %collective-permute-done.16 = bf16[480,256]{1,0:T(8,128)(2,1)S(1)} collective-permute-done((bf16[480,256]{1,0:T(8,128)(2,1)S(1)}, bf16[480,256]{1,0:T(8,128)(2,1)S(1)}, u32[]{:S(2)}, u32[]{:S(2)}) %collective-permute-start.16) | collective-permute-done | bytes 245792 | tf_op jit(solution)/shard_map/ppermute | solution.py:57
  81.2 3.6 collective-permute-done.17
  84.8 4.3 all-to-all-start
  90.3 1.6 collective-permute-start.6
  91.9 1.5 collective-permute-start.7
  93.4 35.4 %collective-permute-done.6.refs_1_ = bf16[4,400,256]{2,1,0:T(8,128)(2,1)S(1)} collective-permute-done((bf16[4,400,256]{2,1,0:T(8,128)(2,1)S(1)}, bf16[4,400,256]{2,1,0:T(8,128)(2,1)S(1)}, u32[]{:S(2)}, u32[]{:S(2)}) %collective-permute-start.6) | collective-permute-done | bytes 819232 | tf_op jit(solution)/shard_map/ppermute | solution.py:57
  128.8 1.6 collective-permute-start.8
  130.4 1.6 collective-permute-start.9
  132.0 10.2 %collective-permute-done.8.refs_3_ = bf16[2,400,256]{2,1,0:T(8,128)(2,1)S(1)} collective-permute-done((bf16[2,400,256]{2,1,0:T(8,128)(2,1)S(1)}, bf16[2,400,256]{2,1,0:T(8,128)(2,1)S(1)}, u32[]{:S(2)}, u32[]{:S(2)}) %collective-permute-start.8) | collective-permute-done | bytes 409632 | tf_op jit(solution)/shard_map/ppermute | solution.py:57
  144.3 5.1 %all-to-all-start.1 = ((bf16[8,128,1024]{2,1,0:T(8,128)(2,1)}), bf16[8,128,1024]{2,1,0:T(8,128)(2,1)S(1)}, u32[]{:S(2)}, u32[]{:S(2)}) async-start(bf16[8,128,1024]{2,1,0:T(8,128)(2,1)} %get-tuple-element.106), calls=%async_computation.1 | async-start | bytes 4194304 | tf_op jit(solution)/shard_map/all_to_all | solution.py:708
  153.6 1.5 collective-permute-start.18
  160.3 9.0 %project.1 = (bf16[512,1024]{1,0:T(8,128)(2,1)}, bf16[512,1024]{1,0:T(8,128)(2,1)}, bf16[512,1024]{1,0:T(8,128)(2,1)}, bf16[512,1024]{1,0:T(8,128)(2,1)}, bf16[5...) custom-call(bf16[512,1024]{1,0:T(8,128)(2,1)} %bitcast.175, ...), custom_call_target="tpu_custom_call" | custom-call | flops 3221225472 | bytes 25165824 | tf_op jit(solution)/shard_map/project/pallas_call | solution.py:211
  169.3 14.2 %weigh.1 = (bf16[8,512,512]{2,1,0:T(8,128)(2,1)}, bf16[8,512,1024]{2,1,0:T(8,128)(2,1)}) custom-call(bf16[512,1024]{1,0:T(8,128)(2,1)} %get-tuple-element.89.qmem, bf16[512,1024]{1,0:T(8,128)(2,1)} %get-tuple-element.90.qloc, bf16[512,1024]{1,0:T(8,128)(2,1)} %get-tuple-element.91.kloc, bf16[8,128,1024]{2,1,0:T(8,128)(2,1)} %copy-done.4, ...), custom_call_target="tpu_custom_call" | custom-call | flops 3221225472 | bytes 25165824 | tf_op jit(solution)/shard_map/weigh/pallas_call | solution.py:264
  184.7 1.5 collective-permute-start.20
  187.9 1.5 pad_maximum_fusion.2
  189.4 8.6 %collective-permute-done.20.refs_3_ = bf16[2,480,256]{2,1,0:T(8,128)(2,1)S(1)} collective-permute-done((bf16[2,480,256]{2,1,0:T(8,128)(2,1)S(1)}, bf16[2,480,256]{2,1,0:T(8,128)(2,1)S(1)}, u32[]{:S(2)}, u32[]{:S(2)}) %collective-permute-start.20) | collective-permute-done | bytes 491552 | tf_op jit(solution)/shard_map/ppermute | solution.py:57
  198.7 1.7 collective-permute-done.21.refs_4_
  201.7 5.1 %all-to-all-start.2 = ((bf16[8,2,64,1024]{3,2,1,0:T(8,128)(2,1)}), bf16[8,2,64,1024]{3,2,1,0:T(8,128)(2,1)}, u32[]{:S(2)}, u32[]{:S(2)}) async-start(bf16[8,2,64,1024]{3,2,1,0:T(8,128)(2,1)} %pad_maximum_fusion.2), calls=%async_computation.2 | async-start | bytes 4194304 | tf_op jit(solution)/shard_map/all_to_all | solution.py:721
  208.0 8.6 %attend.1.att_ref.att = bf16[512,1024]{1,0:T(8,128)(2,1)} custom-call(bf16[8,512,512]{2,1,0:T(8,128)(2,1)} %get-tuple-element.94.p_loc, bf16[8,512,1024]{2,1,0:T(8,128)(2,1)} %get-tuple-element.103.p_mem, bf16[512,1024]{1,0:T(8,128)(2,1)} %get-tuple-element.104.v, bf16[8,128,1024]{2,1,0:T(8,128)(2,1)} %copy-done.2), custom_call_target="tpu_custom_call" | custom-call | flops 1610612736 | bytes 25165824 | tf_op jit(solution)/shard_map/attend/pallas_call | solution.py:294
  217.9 44.6 %feed.1 = (bf16[4,2,4,2,32,2816]{5,4,3,2,1,0:T(8,128)(2,1)}, bf16[2,4,2,480,256]{4,3,2,1,0:T(8,128)(2,1)}, bf16[2,4,2,480,256]{4,3,2,1,0:T(8,128)(2,1)}, bf16[51...) custom-call(bf16[512,1024]{1,0:T(8,128)(2,1)} %bitcast.176, ...), custom_call_target="tpu_custom_call" | custom-call | flops 26575110144 | bytes 25165824 | tf_op jit(solution)/shard_map/feed/pallas_call | solution.py:431
  263.0 6.6 %collective-permute-done.27 = bf16[2,4,2,480,256]{4,3,2,1,0:T(8,128)(2,1)S(1)} collective-permute-done((bf16[2,4,2,480,256]{4,3,2,1,0:T(8,128)(2,1)}, bf16[2,4,2,480,256]{4,3,2,1,0:T(8,128)(2,1)S(1)}, u32[]{:S(2)}, u32[]{:S(2)}) %collective-permute-start.27) | collective-permute-done | bytes 3932192 | tf_op jit(solution)/shard_map/ppermute | solution.py:57
  269.6 3.3 add_convert_fusion
  272.9 1.4 slice_bitcast_fusion.3
  275.8 16.9 %attend_back.1 = (bf16[512,1024]{1,0:T(8,128)(2,1)}, bf16[512,1024]{1,0:T(8,128)(2,1)}, bf16[512,1024]{1,0:T(8,128)(2,1)}) custom-call(bf16[8,512,512]{2,1,0:T(8,128)(2,1)} %get-tuple-element.94.p_loc, bf16[8,512,1024]{2,1,0:T(8,128)(2,1)} %get-tuple-element.103.p_mem, bf16[512,1024]{1,0:T(8,128)(2,1)} %get-tuple-element.118.datt, ...), custom_call_target="tpu_custom_call" | custom-call | flops 4294967296 | bytes 25165824 | tf_op jit(solution)/shard_map/attend_back/pallas_call | solution.py:489
  292.7 13.4 %collective-permute-done.28 = bf16[2,2,480,256]{3,2,1,0:T(8,128)(2,1)S(1)} collective-permute-done((bf16[2,2,480,256]{3,2,1,0:T(8,128)(2,1)}, bf16[2,2,480,256]{3,2,1,0:T(8,128)(2,1)S(1)}, u32[]{:S(2)}, u32[]{:S(2)}) %collective-permute-start.28) | collective-permute-done | bytes 983072 | tf_op jit(solution)/shard_map/ppermute | solution.py:57
  308.1 8.4 %project_grads.1 = (bf16[2,4,2,96,1024]{4,3,2,1,0:T(8,128)(2,1)}, bf16[2,4,2,96,1024]{4,3,2,1,0:T(8,128)(2,1)}) custom-call(bf16[512,1024]{1,0:T(8,128)(2,1)} %get-tuple-element.123.normed_ref, bf16[512,1024]{1,0:T(8,128)(2,1)} %get-tuple-element.131.dq, bf16[512,1024]{1,0:T(8,128)(2,1)} %get-tuple-element.124.dk, bf16[512,1024]{1,0:T(8,128)(2,1)} %get-tuple-element.125.dv), custom_call_target="tpu_custom_call" | custom-call | flops 1048576 | bytes 25165824 | tf_op jit(solution)/shard_map/project_grads/pallas_call | solution.py:528
  318.5 21.8 %collective-permute-done.30 = bf16[2,480,256]{2,1,0:T(8,128)(2,1)S(1)} collective-permute-done((bf16[2,480,256]{2,1,0:T(8,128)(2,1)}, bf16[2,480,256]{2,1,0:T(8,128)(2,1)S(1)}, u32[]{:S(2)}, u32[]{:S(2)}) %collective-permute-start.30) | collective-permute-done | bytes 491552 | tf_op jit(solution)/shard_map/ppermute | solution.py:57
  341.8 2.8 collective-permute-start.38
  345.2 11.7 %project_back.1 = f32[512,1024]{1,0:T(8,128)} custom-call(bf16[512,1024]{1,0:T(8,128)(2,1)} %bitcast.177, f32[512,1024]{1,0:T(8,128)} %get-tuple-element.109.dmix_ref, f32[2,1024]{1,0:T(2,128)} %get-tuple-element.107.gains_ref, bf16[512,1024]{1,0:T(8,128)(2,1)} %get-tuple-element.131.dq, bf16[512,1024]{1,0:T(8,128)(2,1)} %get-tuple-element.124.dk, ...), custom_call_target="tpu_custom_call" | custom-call | flops 1048576 | bytes 25165824 | tf_op jit(solution)/shard_map/project_back/pallas_call | solution.py:568
  356.9 4.7 %add_convert_fusion.1 = bf16[2,4,2,96,1024]{4,3,2,1,0:T(8,128)(2,1)S(1)} fusion(bf16[2,4,2,96,1024]{4,3,2,1,0:T(8,128)(2,1)} %collective-permute-done.32, bf16[2,4,2,96,1024]{4,3,2,1,0:T(8,128)(2,1)} %get-tuple-element.132), kind=kLoop, calls=%fused_computation.6 | loop fusion | flops 6291456 | bytes 9437184 | tf_op jit(solution)/shard_map/convert_element_type | solution.py:584
  361.7 1.3 slice_bitcast_fusion.5
  363.0 1.5 collective-permute-start.33
  364.5 2.0 collective-permute-done.39
  368.7 2.9 collective-permute-start.41
  372.2 3.1 slice_bitcast_fusion.1
  375.3 5.9 %collective-permute-done.33 = bf16[2,2,96,1024]{3,2,1,0:T(8,128)(2,1)} collective-permute-done((bf16[2,2,96,1024]{3,2,1,0:T(8,128)(2,1)}, bf16[2,2,96,1024]{3,2,1,0:T(8,128)(2,1)}, u32[]{:S(2)}, u32[]{:S(2)}) %collective-permute-start.33) | collective-permute-done | bytes 786464 | tf_op jit(solution)/shard_map/ppermute | solution.py:57
  381.2 1.4 collective-permute-start.49
  383.9 1.4 fusion.10
  386.6 9.4 %collective-permute-done.41 = bf16[2,32,2816]{2,1,0:T(8,128)(2,1)S(1)} collective-permute-done((bf16[2,32,2816]{2,1,0:T(8,128)(2,1)S(1)}, bf16[2,32,2816]{2,1,0:T(8,128)(2,1)S(1)}, u32[]{:S(2)}, u32[]{:S(2)}) %collective-permute-start.41) | collective-permute-done | bytes 360480 | tf_op jit(solution)/shard_map/ppermute | solution.py:57
  396.9 5.4 %collective-permute-done.42 = bf16[2,32,2816]{2,1,0:T(8,128)(2,1)S(1)} collective-permute-done((bf16[2,32,2816]{2,1,0:T(8,128)(2,1)S(1)}, bf16[2,32,2816]{2,1,0:T(8,128)(2,1)S(1)}, u32[]{:S(2)}, u32[]{:S(2)}) %collective-permute-start.42) | collective-permute-done | bytes 360480 | tf_op jit(solution)/shard_map/ppermute | solution.py:57
  402.3 1.5 collective-permute-start.36
  403.8 1.9 fusion.16
  406.2 5.1 %collective-permute-done.36 = bf16[2,96,1024]{2,1,0:T(8,128)(2,1)S(1)} collective-permute-done((bf16[2,96,1024]{2,1,0:T(8,128)(2,1)S(1)}, bf16[2,96,1024]{2,1,0:T(8,128)(2,1)S(1)}, u32[]{:S(2)}, u32[]{:S(2)}) %collective-permute-start.36) | collective-permute-done | bytes 393248 | tf_op jit(solution)/shard_map/ppermute | solution.py:57
  411.3 1.5 collective-permute-start.53
  412.8 1.5 fusion.13
  415.1 1.4 collective-permute-start.45
  416.5 2.1 collective-permute-start.43
  420.5 5.9 %collective-permute-done.45 = bf16[96,1024]{1,0:T(8,128)(2,1)S(1)} collective-permute-done((bf16[96,1024]{1,0:T(8,128)(2,1)S(1)}, bf16[96,1024]{1,0:T(8,128)(2,1)S(1)}, u32[]{:S(2)}, u32[]{:S(2)}) %collective-permute-start.45) | collective-permute-done | bytes 196640 | tf_op jit(solution)/shard_map/ppermute | solution.py:57
  431.4 2.1 collective-permute-start.48
  434.9 3.0 collective-permute-done.54
  437.9 1.4 pad_maximum_fusion.4
  441.3 1.3 multiply_reduce_fusion.1
  (231 shorter events, 61.2 us)
Async XLA Ops:
  7.2 209.5 %all-gather.3.cloned.1.call-start = ((), (), s32[]{:S(2)}) async-start(), calls=%async_computation.5 | async-start | bytes 12976128 | tf_op jit(solution)/shard_map/all_gather | solution.py:689
  8.4 15.0 %collective-permute-start = (bf16[32,5632]{1,0:T(8,128)(2,1)S(1)}, bf16[32,5632]{1,0:T(8,128)(2,1)}, u32[]{:S(2)}, u32[]{:S(2)}) collective-permute-start(bf16[32,5632]{1,0:T(8,128)(2,1)S(1)} %pad_maximum_fusion.9), channel_id=1, source_target_pairs={{0,2},{1,3},{2,0},{3,1},{4,6},{5,7},{6,4},{7,5},{8,10},{9,11},{10,... | collective-permute-start | bytes 1081352 | tf_op jit(solution)/shard_map/ppermute | solution.py:57
  8.5 27.3 %collective-permute-start.1 = (bf16[32,5632]{1,0:T(8,128)(2,1)S(1)}, bf16[32,5632]{1,0:T(8,128)(2,1)}, u32[]{:S(2)}, u32[]{:S(2)}) collective-permute-start(bf16[32,5632]{1,0:T(8,128)(2,1)S(1)} %pad_maximum_fusion.9), channel_id=1, source_target_pairs={{0,4},{1,5},{2,6},{3,7},{4,0},{5,1},{6,2},{7,3},{8,12},{9,13},{10,... | collective-permute-start | bytes 1081352 | tf_op jit(solution)/shard_map/ppermute | solution.py:57
  11.6 36.0 %collective-permute-start.2 = (bf16[32,5632]{1,0:T(8,128)(2,1)S(1)}, bf16[32,5632]{1,0:T(8,128)(2,1)}, u32[]{:S(2)}, u32[]{:S(2)}) collective-permute-start(bf16[32,5632]{1,0:T(8,128)(2,1)S(1)} %pad_maximum_fusion.9), channel_id=1, source_target_pairs={{0,6},{1,7},{2,4},{3,5},{4,2},{5,3},{6,0},{7,1},{8,14},{9,15},{10,... | collective-permute-start | bytes 1081352 | tf_op jit(solution)/shard_map/ppermute | solution.py:57
  18.0 33.7 %copy-start.21 = (bf16[400,256]{1,0:T(8,128)(2,1)}, bf16[400,256]{1,0:T(8,128)(2,1)S(1)}, u32[]{:S(2)}) copy-start(bf16[400,256]{1,0:T(8,128)(2,1)S(1)} %pad_maximum_fusion.13) | copy-start | bytes 614404
  50.1 10.1 %collective-permute-start.5 = (bf16[400,256]{1,0:T(8,128)(2,1)S(1)}, bf16[400,256]{1,0:T(8,128)(2,1)S(1)}, u32[]{:S(2)}, u32[]{:S(2)}) collective-permute-start(bf16[400,256]{1,0:T(8,128)(2,1)S(1)} %pad_maximum_fusion.13), channel_id=1, source_target_pairs={{0,6},{1,7},{2,4},{3,5},{4,2},{5,3},{6,0},{7,1},{8,14},{9,15},{10,... | collective-permute-start | bytes 614408 | tf_op jit(solution)/shard_map/ppermute | solution.py:57
  51.7 9.8 %collective-permute-start.4 = (bf16[400,256]{1,0:T(8,128)(2,1)S(1)}, bf16[400,256]{1,0:T(8,128)(2,1)S(1)}, u32[]{:S(2)}, u32[]{:S(2)}) collective-permute-start(bf16[400,256]{1,0:T(8,128)(2,1)S(1)} %pad_maximum_fusion.13), channel_id=1, source_target_pairs={{0,4},{1,5},{2,6},{3,7},{4,0},{5,1},{6,2},{7,3},{8,12},{9,13},{10,... | collective-permute-start | bytes 614408 | tf_op jit(solution)/shard_map/ppermute | solution.py:57
  51.7 9.8 %collective-permute-start.3 = (bf16[400,256]{1,0:T(8,128)(2,1)S(1)}, bf16[400,256]{1,0:T(8,128)(2,1)S(1)}, u32[]{:S(2)}, u32[]{:S(2)}) collective-permute-start(bf16[400,256]{1,0:T(8,128)(2,1)S(1)} %pad_maximum_fusion.13), channel_id=1, source_target_pairs={{0,2},{1,3},{2,0},{3,1},{4,6},{5,7},{6,4},{7,5},{8,10},{9,11},{10,... | collective-permute-start | bytes 614408 | tf_op jit(solution)/shard_map/ppermute | solution.py:57
  53.6 35.4 %copy-start.22 = (bf16[400,256]{1,0:T(8,128)(2,1)S(1)}, bf16[400,256]{1,0:T(8,128)(2,1)}, u32[]{:S(2)}) copy-start(bf16[400,256]{1,0:T(8,128)(2,1)} %copy-done.21) | copy-start | bytes 614404
  60.2 28.8 %copy-start.34 = (bf16[400,256]{1,0:T(8,128)(2,1)}, bf16[400,256]{1,0:T(8,128)(2,1)S(1)}, u32[]{:S(2)}) copy-start(bf16[400,256]{1,0:T(8,128)(2,1)S(1)} %collective-permute-done.5) | copy-start | bytes 614404
  61.5 9.9 %collective-permute-start.15 = (bf16[480,256]{1,0:T(8,128)(2,1)S(1)}, bf16[480,256]{1,0:T(8,128)(2,1)S(1)}, u32[]{:S(2)}, u32[]{:S(2)}) collective-permute-start(bf16[480,256]{1,0:T(8,128)(2,1)S(1)} %pad_maximum_fusion.12), channel_id=1, source_target_pairs={{0,2},{1,3},{2,0},{3,1},{4,6},{5,7},{6,4},{7,5},{8,10},{9,11},{10,... | collective-permute-start | bytes 737288 | tf_op jit(solution)/shard_map/ppermute | solution.py:57
  63.9 16.6 %collective-permute-start.16 = (bf16[480,256]{1,0:T(8,128)(2,1)S(1)}, bf16[480,256]{1,0:T(8,128)(2,1)S(1)}, u32[]{:S(2)}, u32[]{:S(2)}) collective-permute-start(bf16[480,256]{1,0:T(8,128)(2,1)S(1)} %pad_maximum_fusion.12), channel_id=1, source_target_pairs={{0,4},{1,5},{2,6},{3,7},{4,0},{5,1},{6,2},{7,3},{8,12},{9,13},{10,... | collective-permute-start | bytes 737288 | tf_op jit(solution)/shard_map/ppermute | solution.py:57
  65.0 19.7 %collective-permute-start.17 = (bf16[480,256]{1,0:T(8,128)(2,1)S(1)}, bf16[480,256]{1,0:T(8,128)(2,1)}, u32[]{:S(2)}, u32[]{:S(2)}) collective-permute-start(bf16[480,256]{1,0:T(8,128)(2,1)S(1)} %pad_maximum_fusion.12), channel_id=1, source_target_pairs={{0,6},{1,7},{2,4},{3,5},{4,2},{5,3},{6,0},{7,1},{8,14},{9,15},{10,... | collective-permute-start | bytes 737288 | tf_op jit(solution)/shard_map/ppermute | solution.py:57
  84.8 58.2 %all-to-all-start = ((bf16[8,128,1024]{2,1,0:T(8,128)(2,1)}), bf16[8,128,1024]{2,1,0:T(8,128)(2,1)S(1)}, u32[]{:S(2)}, u32[]{:S(2)}) async-start(bf16[8,128,1024]{2,1,0:T(8,128)(2,1)} %get-tuple-element.93), calls=%async_computation | async-start | bytes 4194304 | tf_op jit(solution)/shard_map/all_to_all | solution.py:706
  90.3 59.1 %copy-start.8 = (bf16[4,400,256]{2,1,0:T(8,128)(2,1)}, bf16[4,400,256]{2,1,0:T(8,128)(2,1)S(1)}, u32[]{:S(2)}) copy-start(bf16[4,400,256]{2,1,0:T(8,128)(2,1)S(1)} %pad_maximum_fusion.7.refs_0_) | copy-start | bytes 2457604
  90.3 38.4 %collective-permute-start.6 = (bf16[4,400,256]{2,1,0:T(8,128)(2,1)S(1)}, bf16[4,400,256]{2,1,0:T(8,128)(2,1)S(1)}, u32[]{:S(2)}, u32[]{:S(2)}) collective-permute-start(bf16[4,400,256]{2,1,0:T(8,128)(2,1)S(1)} %pad_maximum_fusion.7.refs_0_), channel_id=1, source_target_pairs={{0,8},{8,0},{16,24},{24,16},{1,9},{9,1},{17,25},{25,17},{2,10},{10... | collective-permute-start | bytes 2457608 | tf_op jit(solution)/shard_map/ppermute | solution.py:57
  91.9 38.5 %collective-permute-start.7 = (bf16[4,400,256]{2,1,0:T(8,128)(2,1)S(1)}, bf16[4,400,256]{2,1,0:T(8,128)(2,1)S(1)}, u32[]{:S(2)}, u32[]{:S(2)}) collective-permute-start(bf16[4,400,256]{2,1,0:T(8,128)(2,1)S(1)} %pad_maximum_fusion.7.refs_0_), channel_id=1, source_target_pairs={{0,16},{8,24},{16,0},{24,8},{1,17},{9,25},{17,1},{25,9},{2,18},{10... | collective-permute-start | bytes 2457608 | tf_op jit(solution)/shard_map/ppermute | solution.py:57
  128.8 13.4 %collective-permute-start.8 = (bf16[2,400,256]{2,1,0:T(8,128)(2,1)S(1)}, bf16[2,400,256]{2,1,0:T(8,128)(2,1)S(1)}, u32[]{:S(2)}, u32[]{:S(2)}) collective-permute-start(bf16[2,400,256]{2,1,0:T(8,128)(2,1)S(1)} %slice.207), channel_id=1, source_target_pairs={{0,16},{8,24},{16,0},{24,8},{1,17},{9,25},{17,1},{25,9},{2,18},{10... | collective-permute-start | bytes 1228808 | tf_op jit(solution)/shard_map/ppermute | solution.py:57
  130.4 12.5 %collective-permute-start.9 = (bf16[2,400,256]{2,1,0:T(8,128)(2,1)S(1)}, bf16[2,400,256]{2,1,0:T(8,128)(2,1)}, u32[]{:S(2)}, u32[]{:S(2)}) collective-permute-start(bf16[2,400,256]{2,1,0:T(8,128)(2,1)S(1)} %slice.208), channel_id=1, source_target_pairs={{0,8},{8,0},{16,24},{24,16},{1,9},{9,1},{17,25},{25,17},{2,10},{10... | collective-permute-start | bytes 1228808 | tf_op jit(solution)/shard_map/ppermute | solution.py:57
  144.3 56.1 %all-to-all-start.1 = ((bf16[8,128,1024]{2,1,0:T(8,128)(2,1)}), bf16[8,128,1024]{2,1,0:T(8,128)(2,1)S(1)}, u32[]{:S(2)}, u32[]{:S(2)}) async-start(bf16[8,128,1024]{2,1,0:T(8,128)(2,1)} %get-tuple-element.106), calls=%async_computation.1 | async-start | bytes 4194304 | tf_op jit(solution)/shard_map/all_to_all | solution.py:708
  149.4 6.3 %collective-permute-start.10 = (bf16[4,400,256]{2,1,0:T(8,128)(2,1)S(1)}, bf16[4,400,256]{2,1,0:T(8,128)(2,1)}, u32[]{:S(2)}, u32[]{:S(2)}) collective-permute-start(bf16[4,400,256]{2,1,0:T(8,128)(2,1)S(1)} %pad_maximum_fusion.7.refs_0_), channel_id=1, source_target_pairs={{0,1},{1,0},{2,3},{3,2},{4,5},{5,4},{6,7},{7,6},{8,9},{9,8},{10,11... | collective-permute-start | bytes 2457608 | tf_op jit(solution)/shard_map/ppermute | solution.py:57
  149.5 6.2 %collective-permute-start.11 = (bf16[4,400,256]{2,1,0:T(8,128)(2,1)}, bf16[4,400,256]{2,1,0:T(8,128)(2,1)}, u32[]{:S(2)}, u32[]{:S(2)}) collective-permute-start(bf16[4,400,256]{2,1,0:T(8,128)(2,1)} %copy-done.14), channel_id=1, source_target_pairs={{0,1},{1,0},{2,3},{3,2},{4,5},{5,4},{6,7},{7,6},{8,9},{9,8},{10,11... | collective-permute-start | bytes 2457608 | tf_op jit(solution)/shard_map/ppermute | solution.py:57
  151.2 7.9 %collective-permute-start.12 = (bf16[4,400,256]{2,1,0:T(8,128)(2,1)}, bf16[4,400,256]{2,1,0:T(8,128)(2,1)S(1)}, u32[]{:S(2)}, u32[]{:S(2)}) collective-permute-start(bf16[4,400,256]{2,1,0:T(8,128)(2,1)} %copy-done.15), channel_id=1, source_target_pairs={{0,1},{1,0},{2,3},{3,2},{4,5},{5,4},{6,7},{7,6},{8,9},{9,8},{10,11... | collective-permute-start | bytes 2457608 | tf_op jit(solution)/shard_map/ppermute | solution.py:57
  153.6 29.9 %collective-permute-start.18 = (bf16[4,480,256]{2,1,0:T(8,128)(2,1)S(1)}, bf16[4,480,256]{2,1,0:T(8,128)(2,1)}, u32[]{:S(2)}, u32[]{:S(2)}) collective-permute-start(bf16[4,480,256]{2,1,0:T(8,128)(2,1)S(1)} %pad_maximum_fusion.5.refs_0_), channel_id=1, source_target_pairs={{0,8},{8,0},{16,24},{24,16},{1,9},{9,1},{17,25},{25,17},{2,10},{10... | collective-permute-start | bytes 2949128 | tf_op jit(solution)/shard_map/ppermute | solution.py:57
  155.2 28.3 %collective-permute-start.19 = (bf16[4,480,256]{2,1,0:T(8,128)(2,1)S(1)}, bf16[4,480,256]{2,1,0:T(8,128)(2,1)}, u32[]{:S(2)}, u32[]{:S(2)}) collective-permute-start(bf16[4,480,256]{2,1,0:T(8,128)(2,1)S(1)} %pad_maximum_fusion.5.refs_0_), channel_id=1, source_target_pairs={{0,16},{8,24},{16,0},{24,8},{1,17},{9,25},{17,1},{25,9},{2,18},{10... | collective-permute-start | bytes 2949128 | tf_op jit(solution)/shard_map/ppermute | solution.py:57
  155.7 3.4 collective-permute-start.13
  155.8 3.4 collective-permute-start.14
  184.7 13.3 %collective-permute-start.20 = (bf16[2,480,256]{2,1,0:T(8,128)(2,1)S(1)}, bf16[2,480,256]{2,1,0:T(8,128)(2,1)S(1)}, u32[]{:S(2)}, u32[]{:S(2)}) collective-permute-start(bf16[2,480,256]{2,1,0:T(8,128)(2,1)S(1)} %slice.147), channel_id=1, source_target_pairs={{0,16},{8,24},{16,0},{24,8},{1,17},{9,25},{17,1},{25,9},{2,18},{10... | collective-permute-start | bytes 1474568 | tf_op jit(solution)/shard_map/ppermute | solution.py:57
  187.3 13.1 %collective-permute-start.21 = (bf16[2,480,256]{2,1,0:T(8,128)(2,1)S(1)}, bf16[2,480,256]{2,1,0:T(8,128)(2,1)}, u32[]{:S(2)}, u32[]{:S(2)}) collective-permute-start(bf16[2,480,256]{2,1,0:T(8,128)(2,1)S(1)} %slice.148), channel_id=1, source_target_pairs={{0,8},{8,0},{16,24},{24,16},{1,9},{9,1},{17,25},{25,17},{2,10},{10... | collective-permute-start | bytes 1474568 | tf_op jit(solution)/shard_map/ppermute | solution.py:57
  201.7 60.8 %all-to-all-start.2 = ((bf16[8,2,64,1024]{3,2,1,0:T(8,128)(2,1)}), bf16[8,2,64,1024]{3,2,1,0:T(8,128)(2,1)}, u32[]{:S(2)}, u32[]{:S(2)}) async-start(bf16[8,2,64,1024]{3,2,1,0:T(8,128)(2,1)} %pad_maximum_fusion.2), calls=%async_computation.2 | async-start | bytes 4194304 | tf_op jit(solution)/shard_map/all_to_all | solution.py:721
  206.8 160.6 %reduce-scatter.2.cloned.1.call-start = ((), (), s32[]{:S(2)}) async-start(), calls=%async_computation.4 | async-start | bytes 12976128 | tf_op jit(solution)/shard_map/reduce_scatter | solution.py:735
  206.8 9.8 %collective-permute-start.22 = (bf16[4,480,256]{2,1,0:T(8,128)(2,1)S(1)}, bf16[4,480,256]{2,1,0:T(8,128)(2,1)S(1)}, u32[]{:S(2)}, u32[]{:S(2)}) collective-permute-start(bf16[4,480,256]{2,1,0:T(8,128)(2,1)S(1)} %copy-done.20), channel_id=1, source_target_pairs={{0,1},{1,0},{2,3},{3,2},{4,5},{5,4},{6,7},{7,6},{8,9},{9,8},{10,11... | collective-permute-start | bytes 2949128 | tf_op jit(solution)/shard_map/ppermute | solution.py:57
  207.0 9.6 %collective-permute-start.23 = (bf16[4,480,256]{2,1,0:T(8,128)(2,1)}, bf16[4,480,256]{2,1,0:T(8,128)(2,1)S(1)}, u32[]{:S(2)}, u32[]{:S(2)}) collective-permute-start(bf16[4,480,256]{2,1,0:T(8,128)(2,1)} %collective-permute-done.18.refs_1_), channel_id=1, source_target_pairs={{0,1},{1,0},{2,3},{3,2},{4,5},{5,4},{6,7},{7,6},{8,9},{9,8},{10,11... | collective-permute-start | bytes 2949128 | tf_op jit(solution)/shard_map/ppermute | solution.py:57
  207.4 9.2 %collective-permute-start.24 = (bf16[4,480,256]{2,1,0:T(8,128)(2,1)}, bf16[4,480,256]{2,1,0:T(8,128)(2,1)}, u32[]{:S(2)}, u32[]{:S(2)}) collective-permute-start(bf16[4,480,256]{2,1,0:T(8,128)(2,1)} %collective-permute-done.19.refs_2_), channel_id=1, source_target_pairs={{0,1},{1,0},{2,3},{3,2},{4,5},{5,4},{6,7},{7,6},{8,9},{9,8},{10,11... | collective-permute-start | bytes 2949128 | tf_op jit(solution)/shard_map/ppermute | solution.py:57
  207.5 9.1 %collective-permute-start.25 = (bf16[2,480,256]{2,1,0:T(8,128)(2,1)}, bf16[2,480,256]{2,1,0:T(8,128)(2,1)}, u32[]{:S(2)}, u32[]{:S(2)}) collective-permute-start(bf16[2,480,256]{2,1,0:T(8,128)(2,1)} %copy-done.44), channel_id=1, source_target_pairs={{0,1},{1,0},{2,3},{3,2},{4,5},{5,4},{6,7},{7,6},{8,9},{9,8},{10,11... | collective-permute-start | bytes 1474568 | tf_op jit(solution)/shard_map/ppermute | solution.py:57
  207.9 8.8 %collective-permute-start.26 = (bf16[2,480,256]{2,1,0:T(8,128)(2,1)}, bf16[2,480,256]{2,1,0:T(8,128)(2,1)}, u32[]{:S(2)}, u32[]{:S(2)}) collective-permute-start(bf16[2,480,256]{2,1,0:T(8,128)(2,1)} %collective-permute-done.21.refs_4_), channel_id=1, source_target_pairs={{0,1},{1,0},{2,3},{3,2},{4,5},{5,4},{6,7},{7,6},{8,9},{9,8},{10,11... | collective-permute-start | bytes 1474568 | tf_op jit(solution)/shard_map/ppermute | solution.py:57
  262.5 7.1 %collective-permute-start.27 = (bf16[2,4,2,480,256]{4,3,2,1,0:T(8,128)(2,1)}, bf16[2,4,2,480,256]{4,3,2,1,0:T(8,128)(2,1)S(1)}, u32[]{:S(2)}, u32[]{:S(2)}) collective-permute-start(bf16[2,4,2,480,256]{4,3,2,1,0:T(8,128)(2,1)} %get-tuple-element.117), channel_id=1, source_target_pairs={{0,1},{1,0},{2,3},{3,2},{4,5},{5,4},{6,7},{7,6},{8,9},{9,8},{10,11... | collective-permute-start | bytes 11796488 | tf_op jit(solution)/shard_map/ppermute | solution.py:57
  274.4 31.7 %collective-permute-start.28 = (bf16[2,2,480,256]{3,2,1,0:T(8,128)(2,1)}, bf16[2,2,480,256]{3,2,1,0:T(8,128)(2,1)S(1)}, u32[]{:S(2)}, u32[]{:S(2)}) collective-permute-start(bf16[2,2,480,256]{3,2,1,0:T(8,128)(2,1)} %get-tuple-element.200), channel_id=1, source_target_pairs={{0,16},{8,24},{16,0},{24,8},{1,17},{9,25},{17,1},{25,9},{2,18},{10... | collective-permute-start | bytes 2949128 | tf_op jit(solution)/shard_map/ppermute | solution.py:57
  274.9 32.0 %collective-permute-start.29 = (bf16[2,2,480,256]{3,2,1,0:T(8,128)(2,1)}, bf16[2,2,480,256]{3,2,1,0:T(8,128)(2,1)S(1)}, u32[]{:S(2)}, u32[]{:S(2)}) collective-permute-start(bf16[2,2,480,256]{3,2,1,0:T(8,128)(2,1)} %get-tuple-element.199), channel_id=1, source_target_pairs={{0,8},{8,0},{16,24},{24,16},{1,9},{9,1},{17,25},{25,17},{2,10},{10... | collective-permute-start | bytes 2949128 | tf_op jit(solution)/shard_map/ppermute | solution.py:57
  316.5 40.5 %collective-permute-start.32 = (bf16[2,4,2,96,1024]{4,3,2,1,0:T(8,128)(2,1)}, bf16[2,4,2,96,1024]{4,3,2,1,0:T(8,128)(2,1)}, u32[]{:S(2)}, u32[]{:S(2)}) collective-permute-start(bf16[2,4,2,96,1024]{4,3,2,1,0:T(8,128)(2,1)} %get-tuple-element.127), channel_id=1, source_target_pairs={{0,1},{1,0},{2,3},{3,2},{4,5},{5,4},{6,7},{7,6},{8,9},{9,8},{10,11... | collective-permute-start | bytes 9437192 | tf_op jit(solution)/shard_map/ppermute | solution.py:57
  316.5 23.8 %collective-permute-start.30 = (bf16[2,480,256]{2,1,0:T(8,128)(2,1)}, bf16[2,480,256]{2,1,0:T(8,128)(2,1)S(1)}, u32[]{:S(2)}, u32[]{:S(2)}) collective-permute-start(bf16[2,480,256]{2,1,0:T(8,128)(2,1)} %get-tuple-element.198), channel_id=1, source_target_pairs={{0,8},{8,0},{16,24},{24,16},{1,9},{9,1},{17,25},{25,17},{2,10},{10... | collective-permute-start | bytes 1474568 | tf_op jit(solution)/shard_map/ppermute | solution.py:57
  317.7 22.7 %collective-permute-start.31 = (bf16[2,480,256]{2,1,0:T(8,128)(2,1)}, bf16[2,480,256]{2,1,0:T(8,128)(2,1)S(1)}, u32[]{:S(2)}, u32[]{:S(2)}) collective-permute-start(bf16[2,480,256]{2,1,0:T(8,128)(2,1)} %get-tuple-element.197), channel_id=1, source_target_pairs={{0,16},{8,24},{16,0},{24,8},{1,17},{9,25},{17,1},{25,9},{2,18},{10... | collective-permute-start | bytes 1474568 | tf_op jit(solution)/shard_map/ppermute | solution.py:57
  341.5 23.0 %collective-permute-start.37 = (bf16[480,256]{1,0:T(8,128)(2,1)S(1)}, bf16[480,256]{1,0:T(8,128)(2,1)S(1)}, u32[]{:S(2)}, u32[]{:S(2)}) collective-permute-start(bf16[480,256]{1,0:T(8,128)(2,1)S(1)} %slice_bitcast_fusion.20), channel_id=1, source_target_pairs={{0,2},{1,3},{2,0},{3,1},{4,6},{5,7},{6,4},{7,5},{8,10},{9,11},{10,... | collective-permute-start | bytes 737288 | tf_op jit(solution)/shard_map/ppermute | solution.py:57
  341.8 22.7 %collective-permute-start.38 = (bf16[480,256]{1,0:T(8,128)(2,1)S(1)}, bf16[480,256]{1,0:T(8,128)(2,1)S(1)}, u32[]{:S(2)}, u32[]{:S(2)}) collective-permute-start(bf16[480,256]{1,0:T(8,128)(2,1)S(1)} %get-tuple-element.218), channel_id=1, source_target_pairs={{0,4},{1,5},{2,6},{3,7},{4,0},{5,1},{6,2},{7,3},{8,12},{9,13},{10,... | collective-permute-start | bytes 737288 | tf_op jit(solution)/shard_map/ppermute | solution.py:57
  344.6 21.9 %collective-permute-start.39 = (bf16[480,256]{1,0:T(8,128)(2,1)S(1)}, bf16[480,256]{1,0:T(8,128)(2,1)S(1)}, u32[]{:S(2)}, u32[]{:S(2)}) collective-permute-start(bf16[480,256]{1,0:T(8,128)(2,1)S(1)} %get-tuple-element.217), channel_id=1, source_target_pairs={{0,6},{1,7},{2,4},{3,5},{4,2},{5,3},{6,0},{7,1},{8,14},{9,15},{10,... | collective-permute-start | bytes 737288 | tf_op jit(solution)/shard_map/ppermute | solution.py:57
  363.0 18.1 %collective-permute-start.33 = (bf16[2,2,96,1024]{3,2,1,0:T(8,128)(2,1)}, bf16[2,2,96,1024]{3,2,1,0:T(8,128)(2,1)}, u32[]{:S(2)}, u32[]{:S(2)}) collective-permute-start(bf16[2,2,96,1024]{3,2,1,0:T(8,128)(2,1)} %get-tuple-element.206), channel_id=1, source_target_pairs={{0,16},{8,24},{16,0},{24,8},{1,17},{9,25},{17,1},{25,9},{2,18},{10... | collective-permute-start | bytes 2359304 | tf_op jit(solution)/shard_map/ppermute | solution.py:57
  364.5 18.1 %collective-permute-start.34 = (bf16[2,2,96,1024]{3,2,1,0:T(8,128)(2,1)}, bf16[2,2,96,1024]{3,2,1,0:T(8,128)(2,1)}, u32[]{:S(2)}, u32[]{:S(2)}) collective-permute-start(bf16[2,2,96,1024]{3,2,1,0:T(8,128)(2,1)} %get-tuple-element.205), channel_id=1, source_target_pairs={{0,8},{8,0},{16,24},{24,16},{1,9},{9,1},{17,25},{25,17},{2,10},{10... | collective-permute-start | bytes 2359304 | tf_op jit(solution)/shard_map/ppermute | solution.py:57
  368.6 16.7 %collective-permute-start.40 = (bf16[2,32,2816]{2,1,0:T(8,128)(2,1)S(1)}, bf16[2,32,2816]{2,1,0:T(8,128)(2,1)S(1)}, u32[]{:S(2)}, u32[]{:S(2)}) collective-permute-start(bf16[2,32,2816]{2,1,0:T(8,128)(2,1)S(1)} %get-tuple-element.216), channel_id=1, source_target_pairs={{0,2},{1,3},{2,0},{3,1},{4,6},{5,7},{6,4},{7,5},{8,10},{9,11},{10,... | collective-permute-start | bytes 1081352 | tf_op jit(solution)/shard_map/ppermute | solution.py:57
  368.7 27.2 %collective-permute-start.41 = (bf16[2,32,2816]{2,1,0:T(8,128)(2,1)S(1)}, bf16[2,32,2816]{2,1,0:T(8,128)(2,1)S(1)}, u32[]{:S(2)}, u32[]{:S(2)}) collective-permute-start(bf16[2,32,2816]{2,1,0:T(8,128)(2,1)S(1)} %get-tuple-element.215), channel_id=1, source_target_pairs={{0,4},{1,5},{2,6},{3,7},{4,0},{5,1},{6,2},{7,3},{8,12},{9,13},{10,... | collective-permute-start | bytes 1081352 | tf_op jit(solution)/shard_map/ppermute | solution.py:57
  371.6 30.6 %collective-permute-start.42 = (bf16[2,32,2816]{2,1,0:T(8,128)(2,1)S(1)}, bf16[2,32,2816]{2,1,0:T(8,128)(2,1)S(1)}, u32[]{:S(2)}, u32[]{:S(2)}) collective-permute-start(bf16[2,32,2816]{2,1,0:T(8,128)(2,1)S(1)} %get-tuple-element.214), channel_id=1, source_target_pairs={{0,6},{1,7},{2,4},{3,5},{4,2},{5,3},{6,0},{7,1},{8,14},{9,15},{10,... | collective-permute-start | bytes 1081352 | tf_op jit(solution)/shard_map/ppermute | solution.py:57
  381.2 33.9 %collective-permute-start.49 = (bf16[480,256]{1,0:T(8,128)(2,1)}, bf16[480,256]{1,0:T(8,128)(2,1)S(1)}, u32[]{:S(2)}, u32[]{:S(2)}) collective-permute-start(bf16[480,256]{1,0:T(8,128)(2,1)} %add_convert_fusion.2), channel_id=1, source_target_pairs={{0,8},{8,0},{16,24},{24,16},{1,9},{9,1},{17,25},{25,17},{2,10},{10... | collective-permute-start | bytes 737288 | tf_op jit(solution)/shard_map/ppermute | solution.py:57
  382.6 33.9 %collective-permute-start.50 = (bf16[480,256]{1,0:T(8,128)(2,1)}, bf16[480,256]{1,0:T(8,128)(2,1)S(1)}, u32[]{:S(2)}, u32[]{:S(2)}) collective-permute-start(bf16[480,256]{1,0:T(8,128)(2,1)} %add_convert_fusion.2), channel_id=1, source_target_pairs={{0,16},{8,24},{16,0},{24,8},{1,17},{9,25},{17,1},{25,9},{2,18},{10... | collective-permute-start | bytes 737288 | tf_op jit(solution)/shard_map/ppermute | solution.py:57
  385.3 31.2 %collective-permute-start.51 = (bf16[480,256]{1,0:T(8,128)(2,1)}, bf16[480,256]{1,0:T(8,128)(2,1)S(1)}, u32[]{:S(2)}, u32[]{:S(2)}) collective-permute-start(bf16[480,256]{1,0:T(8,128)(2,1)} %add_convert_fusion.2), channel_id=1, source_target_pairs={{0,24},{8,16},{16,8},{24,0},{1,25},{9,17},{17,9},{25,1},{2,26},{10... | collective-permute-start | bytes 737288 | tf_op jit(solution)/shard_map/ppermute | solution.py:57
  396.0 9.7 %collective-permute-start.35 = (bf16[2,96,1024]{2,1,0:T(8,128)(2,1)S(1)}, bf16[2,96,1024]{2,1,0:T(8,128)(2,1)S(1)}, u32[]{:S(2)}, u32[]{:S(2)}) collective-permute-start(bf16[2,96,1024]{2,1,0:T(8,128)(2,1)S(1)} %get-tuple-element.204), channel_id=1, source_target_pairs={{0,8},{8,0},{16,24},{24,16},{1,9},{9,1},{17,25},{25,17},{2,10},{10... | collective-permute-start | bytes 1179656 | tf_op jit(solution)/shard_map/ppermute | solution.py:57
  402.3 9.1 %collective-permute-start.36 = (bf16[2,96,1024]{2,1,0:T(8,128)(2,1)S(1)}, bf16[2,96,1024]{2,1,0:T(8,128)(2,1)S(1)}, u32[]{:S(2)}, u32[]{:S(2)}) collective-permute-start(bf16[2,96,1024]{2,1,0:T(8,128)(2,1)S(1)} %get-tuple-element.203), channel_id=1, source_target_pairs={{0,16},{8,24},{16,0},{24,8},{1,17},{9,25},{17,1},{25,9},{2,18},{10... | collective-permute-start | bytes 1179656 | tf_op jit(solution)/shard_map/ppermute | solution.py:57
  405.7 28.4 %collective-permute-start.52 = (bf16[2,32,2816]{2,1,0:T(8,128)(2,1)}, bf16[2,32,2816]{2,1,0:T(8,128)(2,1)}, u32[]{:S(2)}, u32[]{:S(2)}) collective-permute-start(bf16[2,32,2816]{2,1,0:T(8,128)(2,1)} %fusion.16), channel_id=1, source_target_pairs={{0,8},{8,0},{16,24},{24,16},{1,9},{9,1},{17,25},{25,17},{2,10},{10... | collective-permute-start | bytes 1081352 | tf_op jit(solution)/shard_map/ppermute | solution.py:57
  411.3 23.6 %collective-permute-start.53 = (bf16[2,32,2816]{2,1,0:T(8,128)(2,1)}, bf16[2,32,2816]{2,1,0:T(8,128)(2,1)}, u32[]{:S(2)}, u32[]{:S(2)}) collective-permute-start(bf16[2,32,2816]{2,1,0:T(8,128)(2,1)} %fusion.16), channel_id=1, source_target_pairs={{0,16},{8,24},{16,0},{24,8},{1,17},{9,25},{17,1},{25,9},{2,18},{10... | collective-permute-start | bytes 1081352 | tf_op jit(solution)/shard_map/ppermute | solution.py:57
  415.1 11.3 %collective-permute-start.45 = (bf16[96,1024]{1,0:T(8,128)(2,1)S(1)}, bf16[96,1024]{1,0:T(8,128)(2,1)S(1)}, u32[]{:S(2)}, u32[]{:S(2)}) collective-permute-start(bf16[96,1024]{1,0:T(8,128)(2,1)S(1)} %get-tuple-element.220), channel_id=1, source_target_pairs={{0,6},{1,7},{2,4},{3,5},{4,2},{5,3},{6,0},{7,1},{8,14},{9,15},{10,... | collective-permute-start | bytes 589832 | tf_op jit(solution)/shard_map/ppermute | solution.py:57
  416.5 13.7 %collective-permute-start.44 = (bf16[96,1024]{1,0:T(8,128)(2,1)}, bf16[96,1024]{1,0:T(8,128)(2,1)}, u32[]{:S(2)}, u32[]{:S(2)}) collective-permute-start(bf16[96,1024]{1,0:T(8,128)(2,1)} %get-tuple-element.219), channel_id=1, source_target_pairs={{0,4},{1,5},{2,6},{3,7},{4,0},{5,1},{6,2},{7,3},{8,12},{9,13},{10,... | collective-permute-start | bytes 589832 | tf_op jit(solution)/shard_map/ppermute | solution.py:57
  416.5 13.7 %collective-permute-start.43 = (bf16[96,1024]{1,0:T(8,128)(2,1)S(1)}, bf16[96,1024]{1,0:T(8,128)(2,1)}, u32[]{:S(2)}, u32[]{:S(2)}) collective-permute-start(bf16[96,1024]{1,0:T(8,128)(2,1)S(1)} %slice_bitcast_fusion.24), channel_id=1, source_target_pairs={{0,2},{1,3},{2,0},{3,1},{4,6},{5,7},{6,4},{7,5},{8,10},{9,11},{10,... | collective-permute-start | bytes 589832 | tf_op jit(solution)/shard_map/ppermute | solution.py:57
  426.4 11.5 %collective-permute-start.54 = (bf16[2,32,2816]{2,1,0:T(8,128)(2,1)}, bf16[2,32,2816]{2,1,0:T(8,128)(2,1)S(1)}, u32[]{:S(2)}, u32[]{:S(2)}) collective-permute-start(bf16[2,32,2816]{2,1,0:T(8,128)(2,1)} %fusion.16), channel_id=1, source_target_pairs={{0,24},{8,16},{16,8},{24,0},{1,25},{9,17},{17,9},{25,1},{2,26},{10... | collective-permute-start | bytes 1081352 | tf_op jit(solution)/shard_map/ppermute | solution.py:57
  431.4 13.1 %collective-permute-start.48 = (bf16[96,1024]{1,0:T(8,128)(2,1)S(1)}, bf16[96,1024]{1,0:T(8,128)(2,1)S(1)}, u32[]{:S(2)}, u32[]{:S(2)}) collective-permute-start(bf16[96,1024]{1,0:T(8,128)(2,1)S(1)} %add_convert_fusion.3), channel_id=1, source_target_pairs={{0,24},{8,16},{16,8},{24,0},{1,25},{9,17},{17,9},{25,1},{2,26},{10... | collective-permute-start | bytes 589832 | tf_op jit(solution)/shard_map/ppermute | solution.py:57
  433.5 11.0 %collective-permute-start.47 = (bf16[96,1024]{1,0:T(8,128)(2,1)S(1)}, bf16[96,1024]{1,0:T(8,128)(2,1)S(1)}, u32[]{:S(2)}, u32[]{:S(2)}) collective-permute-start(bf16[96,1024]{1,0:T(8,128)(2,1)S(1)} %add_convert_fusion.3), channel_id=1, source_target_pairs={{0,16},{8,24},{16,0},{24,8},{1,17},{9,25},{17,1},{25,9},{2,18},{10... | collective-permute-start | bytes 589832 | tf_op jit(solution)/shard_map/ppermute | solution.py:57
  434.0 10.5 %collective-permute-start.46 = (bf16[96,1024]{1,0:T(8,128)(2,1)S(1)}, bf16[96,1024]{1,0:T(8,128)(2,1)}, u32[]{:S(2)}, u32[]{:S(2)}) collective-permute-start(bf16[96,1024]{1,0:T(8,128)(2,1)S(1)} %add_convert_fusion.3), channel_id=1, source_target_pairs={{0,8},{8,0},{16,24},{24,16},{1,9},{9,1},{17,25},{25,17},{2,10},{10... | collective-permute-start | bytes 589832 | tf_op jit(solution)/shard_map/ppermute | solution.py:57
  (42 other events, 273.6 us)
Sparse Core Ops, SparseCore 0:
  50.2 87.6 all-gather.2
  262.7 103.1 reduce-scatter.1
